TPU v7x, 32 devices: a whole 2x2x4 slice. The times are simulated.
32 devices in a mesh: dp: 8 (over y, x, core), tensor: 4 (over z).
Axes of the slice: x: 2, y: 2, z: 4, core: 2. Of those that a mesh axis runs over, the one named last changes fastest.
Arguments:
- tokens_in: bfloat16 [12288, 1024], P(('dp', 'tensor')), may hold values from -6 to 6
- lm_grad: bfloat16 [12288, 1024], P(('dp', 'tensor')), may hold values from -6 to 6
- lm_logprob: float32 [12288], P(('dp', 'tensor')), may hold values from -4 to -0.5
- targets: int32 [12288], P(('dp', 'tensor')), may hold values from 0 to 8191
- neighbor_ids: int32 [12288, 1024], P(('dp', 'tensor')), may hold values from 0 to 8191
- nearby_entry_gaps: float32 [12288, 1024], P(('dp', 'tensor')), may hold values from 0.5 to 6.5
- seq_lengths: int32 [8, 3], P('dp'), may hold values from 0 to 1536, as said below
- attn_weights: float32 [4, 1024, 1024], P(None, 'dp', 'tensor')
- ffn_weights: float32 [2, 1024, 4096], P(None, 'dp', 'tensor')
- attn_left: float32 [4, 1024, 1024], P(None, 'dp', 'tensor'), as said below
- attn_right: float32 [4, 1024, 1024], P(None, 'tensor', 'dp'), as said below
- ffn_left: float32 [2, 1024, 1024], P(None, 'dp', 'tensor'), as said below
- ffn_right: float32 [2, 4096, 4096], P(None, 'tensor', 'dp'), as said below
- attn_left_root: float32 [4, 1024, 1024], P(None, 'dp'), as said below
- attn_right_root: float32 [4, 1024, 1024], P(None, None, 'tensor'), as said below
- ffn_left_root: float32 [2, 1024, 1024], P(None, 'dp'), as said below
- ffn_right_root: float32 [2, 4096, 4096], P(None, None, 'tensor'), as said below
- norm_params: float32 [4, 1024], replicated
- norm_moment1: float32 [4, 1024], replicated
- norm_moment2: float32 [4, 1024], replicated, as said below
- blending_coefficients: float32 [2], replicated, may hold values from -0.5 to 0.5
- knn_moment1: float32 [2], replicated
- knn_moment2: float32 [2], replicated, as said below
Outputs:
- mixed: bfloat16 [12288, 1024], P(('dp', 'tensor'))
- input_grad: float32 [12288, 1024], P(('dp', 'tensor'))
- loss: float32 [], replicated
- attn_grad: float32 [4, 1024, 1024], P(None, 'dp', 'tensor')
- attn_left_new: float32 [4, 1024, 1024], P(None, 'dp', 'tensor')
- attn_right_new: float32 [4, 1024, 1024], P(None, 'tensor', 'dp')
- attn_new: float32 [4, 1024, 1024], P(None, 'dp', 'tensor')
- ffn_grad: float32 [2, 1024, 4096], P(None, 'dp', 'tensor')
- ffn_left_new: float32 [2, 1024, 1024], P(None, 'dp', 'tensor')
- ffn_right_new: float32 [2, 4096, 4096], P(None, 'tensor', 'dp')
- ffn_new: float32 [2, 1024, 4096], P(None, 'dp', 'tensor')
- norm_moment1_new: float32 [4, 1024], replicated
- norm_moment2_new: float32 [4, 1024], replicated
- norm_new: float32 [4, 1024], replicated
- knn_moment1_new: float32 [2], replicated
- knn_moment2_new: float32 [2], replicated
- knn_new: float32 [2], replicated
Inputs may be any that keep to these rules, and one draw needn't show every extreme that they name: `seq_lengths`: each row holds, in order, some sequences of length 1536, then sequences of length 512, then zeros, and sums to 1536; some row holds only sequences of length 1536. `attn_left`: symmetric. `attn_right`: symmetric. `ffn_left`: symmetric. `ffn_right`: symmetric. `attn_left_root`: symmetric. `attn_right_root`: symmetric. `ffn_left_root`: symmetric. `ffn_right_root`: symmetric. `norm_moment2`: positive. `knn_moment2`: positive.
All inputs are finite; a program needn't handle non-finite values.
Results may differ from a plain program's by a relative error of at most 0.014.
Values may be sent and summed in bfloat16 or wider, within the bound.
No kernel may reach another device: no remote copies, remote signals or barrier semaphores. Data moves between devices by JAX's collectives and lax.ppermute only.
A program may use at most 256 MiB of HBM per device.

v0:
```python
import jax
import jax.numpy as jnp
from jax import lax
from jax.sharding import PartitionSpec as P

SHORT = 512
STEP = 10
HEAD_DIM = 64


adam_rate = 0.3
shampoo_rate = 0.5
shampoo_decay = 0.01
norm_eps = 1e-05


def layer_norm(values_in, gain, shift):
    centre = jnp.mean(values_in, axis=-1, keepdims=True)
    centred = values_in - centre
    spread_sq = jnp.mean(centred * centred, axis=-1, keepdims=True)
    return centred * lax.rsqrt(spread_sq + norm_eps) * gain + shift


def gelu_tanh(values_in):
    return jax.nn.gelu(values_in, approximate=True)


def spread_rows(local_low):
    return lax.all_gather(local_low, "tensor", axis=0, tiled=True)


def spread_again(local_low):
    return lax.all_gather(local_low, "tensor", axis=0, tiled=True)


def spread_grads(local_low):
    return lax.all_gather(local_low, "tensor", axis=0, tiled=True)


def branch_total(left_rows, right_mat):
    return lax.psum_scatter(
        jnp.einsum("rc,dc->rd", left_rows, right_mat, preferred_element_type=jnp.float32),
        "tensor",
        scatter_dimension=0,
        tiled=True,
    )


def input_total(left_rows, right_mat):
    return lax.psum_scatter(
        jnp.einsum("rc,dc->rd", left_rows, right_mat, preferred_element_type=jnp.float32),
        "tensor",
        scatter_dimension=0,
        tiled=True,
    )


def first_blocks(seq_lengths, group_rows, block_rows):
    lengths = seq_lengths[0]
    seq_ends = jnp.cumsum(lengths)
    seq_begins = seq_ends - lengths
    block_begins = jnp.arange(group_rows // block_rows, dtype=jnp.int32) * block_rows
    inside = (seq_begins[None, :] <= block_begins[:, None]) & (lengths[None, :] > 0)
    return jnp.max(jnp.where(inside, seq_begins[None, :], 0), axis=1) // block_rows


def block_scores(query_rows, key_rows, query_block, key_block, block_rows, score_scale):
    scores = (
        jnp.einsum("qhd,khd->hqk", query_rows, key_rows, preferred_element_type=jnp.float32)
        * score_scale
    )
    query_pos = query_block * block_rows + jnp.arange(block_rows, dtype=jnp.int32)
    key_pos = key_block * block_rows + jnp.arange(block_rows, dtype=jnp.int32)
    allowed = key_pos[None, :] <= query_pos[:, None]
    return jnp.where(allowed[None], scores, -1e30)


def attend_forward(query_all, key_all, value_all, first_block, block_rows, score_scale):
    group_rows, head_count, head_width = query_all.shape

    def one_block(query_block):
        query_rows = lax.dynamic_slice_in_dim(query_all, query_block * block_rows, block_rows, 0)

        def peak_step(key_block, loop_state):
            running_top, running_mass = loop_state
            key_rows = lax.dynamic_slice_in_dim(key_all, key_block * block_rows, block_rows, 0)
            scores = block_scores(
                query_rows, key_rows, query_block, key_block, block_rows, score_scale
            )
            new_top = jnp.maximum(running_top, jnp.max(scores, axis=2))
            new_mass = running_mass * jnp.exp(running_top - new_top) + jnp.sum(
                jnp.exp(scores - new_top[:, :, None]), axis=2
            )
            return (new_top, new_mass)

        start_state = (
            jnp.full((head_count, block_rows), -1e30, jnp.float32),
            jnp.zeros((head_count, block_rows), jnp.float32),
        )
        final_top, final_mass = lax.fori_loop(
            first_block[query_block], query_block + 1, peak_step, start_state
        )
        log_mass = final_top + jnp.log(final_mass)

        def value_step(key_block, out_acc):
            key_rows = lax.dynamic_slice_in_dim(key_all, key_block * block_rows, block_rows, 0)
            value_rows = lax.dynamic_slice_in_dim(value_all, key_block * block_rows, block_rows, 0)
            scores = block_scores(
                query_rows, key_rows, query_block, key_block, block_rows, score_scale
            )
            attn_probs = jnp.exp(scores - log_mass[:, :, None]).astype(jnp.bfloat16)
            return out_acc + jnp.einsum(
                "hqk,khd->qhd", attn_probs, value_rows, preferred_element_type=jnp.float32
            )

        out_rows = lax.fori_loop(
            first_block[query_block],
            query_block + 1,
            value_step,
            jnp.zeros((block_rows, head_count, head_width), jnp.float32),
        )
        return (out_rows.astype(jnp.bfloat16), log_mass)

    outs, log_masses = lax.map(one_block, jnp.arange(group_rows // block_rows, dtype=jnp.int32))
    return (outs.reshape(group_rows, head_count, head_width), log_masses)


def attend_backward(
    query_all, key_all, value_all, grad_out, log_masses, first_block, block_rows, score_scale
):
    group_rows, head_count, head_width = query_all.shape

    def one_block(query_block, loop_carry):
        grad_keys, grad_values, grad_query = loop_carry
        query_rows = lax.dynamic_slice_in_dim(query_all, query_block * block_rows, block_rows, 0)
        grad_rows = lax.dynamic_slice_in_dim(grad_out, query_block * block_rows, block_rows, 0)
        log_mass = log_masses[query_block]

        def chances(key_block):
            key_rows = lax.dynamic_slice_in_dim(key_all, key_block * block_rows, block_rows, 0)
            value_rows = lax.dynamic_slice_in_dim(value_all, key_block * block_rows, block_rows, 0)
            scores = block_scores(
                query_rows, key_rows, query_block, key_block, block_rows, score_scale
            )
            attn_probs = jnp.exp(scores - log_mass[:, :, None])
            likelihood_cotangent = jnp.einsum(
                "qhd,khd->hqk", grad_rows, value_rows, preferred_element_type=jnp.float32
            )
            return (key_rows, attn_probs, likelihood_cotangent)

        def inner_step(key_block, inner_acc):
            _, attn_probs, likelihood_cotangent = chances(key_block)
            return inner_acc + jnp.sum(attn_probs * likelihood_cotangent, axis=2)

        row_inner = lax.fori_loop(
            first_block[query_block],
            query_block + 1,
            inner_step,
            jnp.zeros((head_count, block_rows), jnp.float32),
        )

        def grad_step(key_block, loop_state):
            query_acc, keys_acc, values_acc = loop_state
            key_rows, attn_probs, likelihood_cotangent = chances(key_block)
            grad_scores = (attn_probs * (likelihood_cotangent - row_inner[:, :, None])).astype(
                jnp.bfloat16
            )
            query_acc = (
                query_acc
                + jnp.einsum(
                    "hqk,khd->qhd", grad_scores, key_rows, preferred_element_type=jnp.float32
                )
                * score_scale
            )
            key_part = (
                jnp.einsum(
                    "hqk,qhd->khd", grad_scores, query_rows, preferred_element_type=jnp.float32
                )
                * score_scale
            )
            value_part = jnp.einsum(
                "hqk,qhd->khd",
                attn_probs.astype(jnp.bfloat16),
                grad_rows,
                preferred_element_type=jnp.float32,
            )
            key_start = key_block * block_rows
            keys_acc = lax.dynamic_update_slice_in_dim(
                keys_acc,
                lax.dynamic_slice_in_dim(keys_acc, key_start, block_rows, 0) + key_part,
                key_start,
                0,
            )
            values_acc = lax.dynamic_update_slice_in_dim(
                values_acc,
                lax.dynamic_slice_in_dim(values_acc, key_start, block_rows, 0) + value_part,
                key_start,
                0,
            )
            return (query_acc, keys_acc, values_acc)

        query_acc, grad_keys, grad_values = lax.fori_loop(
            first_block[query_block],
            query_block + 1,
            grad_step,
            (jnp.zeros((block_rows, head_count, head_width), jnp.float32), grad_keys, grad_values),
        )
        grad_query = lax.dynamic_update_slice_in_dim(
            grad_query, query_acc, query_block * block_rows, 0
        )
        return (grad_keys, grad_values, grad_query)

    zeros_all = jnp.zeros((group_rows, head_count, head_width), jnp.float32)
    return lax.fori_loop(0, group_rows // block_rows, one_block, (zeros_all, zeros_all, zeros_all))


def right_statistics(attn_part_grad, ffn_part_grad, attn_rows, ffn_rows):
    attn_part = jnp.einsum(
        "sri,srj->sij", attn_part_grad, attn_rows, precision=lax.Precision.HIGHEST
    )
    ffn_part = jnp.einsum("sri,srj->sij", ffn_part_grad, ffn_rows, precision=lax.Precision.HIGHEST)
    return (
        lax.psum_scatter(
            attn_part.astype(jnp.bfloat16), "dp", scatter_dimension=2, tiled=True
        ).astype(jnp.float32),
        lax.psum_scatter(
            ffn_part.astype(jnp.bfloat16), "dp", scatter_dimension=2, tiled=True
        ).astype(jnp.float32),
    )


def left_statistics(attn_part_grad, ffn_part_grad, attn_cols, ffn_cols):
    attn_part = jnp.einsum(
        "sri,sqi->srq", attn_part_grad, attn_cols, precision=lax.Precision.HIGHEST
    )
    ffn_part = jnp.einsum("sri,sqi->srq", ffn_part_grad, ffn_cols, precision=lax.Precision.HIGHEST)
    return (
        lax.psum_scatter(
            attn_part.astype(jnp.bfloat16), "tensor", scatter_dimension=2, tiled=True
        ).astype(jnp.float32),
        lax.psum_scatter(
            ffn_part.astype(jnp.bfloat16), "tensor", scatter_dimension=2, tiled=True
        ).astype(jnp.float32),
    )


def adamw_step(params_in, grads_in, first_in, second_in):
    first_new = 0.9 * first_in + 0.1 * grads_in
    second_new = 0.999 * second_in + 0.001 * grads_in * grads_in
    first_hat = first_new / (1.0 - 0.9**STEP)
    second_hat = second_new / (1.0 - 0.999**STEP)
    return (
        first_new,
        second_new,
        params_in - adam_rate * first_hat / (jnp.sqrt(second_hat) + 1e-08),
    )


def local(
    tokens_in,
    lm_grad,
    lm_logprob,
    targets,
    neighbor_ids,
    nearby_entry_gaps,
    seq_lengths,
    attn_weights,
    ffn_weights,
    attn_left,
    attn_right,
    ffn_left,
    ffn_right,
    attn_left_root,
    attn_right_root,
    ffn_left_root,
    ffn_right_root,
    norm_params,
    norm_moment1,
    norm_moment2,
    blending_coefficients,
    knn_moment1,
    knn_moment2,
):
    local_rows = tokens_in.shape[0]
    group_rows = local_rows * lax.axis_size("tensor")
    block_rows = SHORT
    score_scale = HEAD_DIM ** (-0.5)
    attn_full, ffn_full = (
        lax.all_gather(attn_weights.astype(jnp.bfloat16), "dp", axis=1, tiled=True),
        lax.all_gather(ffn_weights.astype(jnp.bfloat16), "dp", axis=1, tiled=True),
    )
    proj_in = jnp.concatenate([attn_full[0], attn_full[1], attn_full[2]], axis=1)
    proj_out = attn_full[3]
    head_cols = proj_out.shape[1]
    head_count = head_cols // HEAD_DIM
    first_block = first_blocks(seq_lengths, group_rows, block_rows)
    resid = tokens_in.astype(jnp.float32)
    normed1, norm1_back = jax.vjp(layer_norm, resid, norm_params[0], norm_params[1])
    normed1_low = normed1.astype(jnp.bfloat16)
    normed1_all = spread_rows(normed1_low)
    qkv_low = jnp.dot(normed1_all, proj_in, preferred_element_type=jnp.float32).astype(jnp.bfloat16)
    query_all = qkv_low[:, :head_cols].reshape(group_rows, head_count, HEAD_DIM)
    key_all = qkv_low[:, head_cols : 2 * head_cols].reshape(group_rows, head_count, HEAD_DIM)
    value_all = qkv_low[:, 2 * head_cols :].reshape(group_rows, head_count, HEAD_DIM)
    heads_out, log_masses = attend_forward(
        query_all, key_all, value_all, first_block, block_rows, score_scale
    )
    heads_flat = heads_out.reshape(group_rows, head_cols)
    attn_out = branch_total(heads_flat, proj_out)
    middle = resid + attn_out
    normed2, norm2_back = jax.vjp(layer_norm, middle, norm_params[2], norm_params[3])
    normed2_low = normed2.astype(jnp.bfloat16)
    w_up = ffn_full[0]
    w_down = ffn_full[1]
    normed2_all = spread_rows(normed2_low)
    hidden_pre = jnp.dot(normed2_all, w_up, preferred_element_type=jnp.float32)
    hidden_act, gelu_back = jax.vjp(gelu_tanh, hidden_pre)
    act_low = hidden_act.astype(jnp.bfloat16)
    ffn_out = branch_total(act_low, w_down)
    mixed = (middle + ffn_out).astype(jnp.bfloat16)
    sharpness_divisor = jnp.exp(blending_coefficients[0])
    interp = jax.nn.sigmoid(blending_coefficients[1])
    nearby_entry_logits = -nearby_entry_gaps / sharpness_divisor
    near_top = jnp.max(nearby_entry_logits, axis=1, keepdims=True)
    near_exp = jnp.exp(nearby_entry_logits - near_top)
    nearby_entry_shares = near_exp / jnp.sum(near_exp, axis=1, keepdims=True)
    target_matches = (neighbor_ids == targets[:, None]).astype(jnp.float32)
    retrieval_probability = jnp.sum(nearby_entry_shares * target_matches, axis=1)
    lm_prob = jnp.exp(lm_logprob)
    mixture = interp * retrieval_probability + (1.0 - interp) * lm_prob
    token_loss = -jnp.log(mixture)
    lm_weight = -(1.0 - interp) * lm_prob / mixture
    temp_terms = (
        jnp.sum(
            nearby_entry_shares
            * (target_matches - retrieval_probability[:, None])
            * nearby_entry_gaps,
            axis=1,
        )
        / sharpness_divisor
    )
    temp_grad = jnp.sum(-(interp / mixture) * temp_terms)
    interp_grad = jnp.sum(-interp * (1.0 - interp) * (retrieval_probability - lm_prob) / mixture)
    knn_grads = jnp.stack([temp_grad, interp_grad])
    cotangent = lm_weight[:, None] * lm_grad.astype(jnp.float32)
    cot_all = spread_grads(cotangent.astype(jnp.bfloat16))
    grad_act = jnp.dot(cot_all, w_down, preferred_element_type=jnp.float32)
    grad_pre_low = gelu_back(grad_act)[0].astype(jnp.bfloat16)
    normed2_used = spread_again(normed2_low)
    grad_up = jnp.einsum(
        "rd,rf->df", normed2_used, grad_pre_low, preferred_element_type=jnp.float32
    )
    grad_down = jnp.einsum("rd,rf->df", cot_all, act_low, preferred_element_type=jnp.float32)
    ffn_local = jnp.stack([grad_up, grad_down])
    grad_normed2 = input_total(grad_pre_low, w_up)
    mid_norm_grad, gain2_grad, shift2_grad = norm2_back(grad_normed2)
    grad_middle = cotangent + mid_norm_grad
    grad_mid_all = spread_grads(grad_middle.astype(jnp.bfloat16))
    grad_heads = jnp.dot(grad_mid_all, proj_out, preferred_element_type=jnp.float32).astype(
        jnp.bfloat16
    )
    grad_out_proj = jnp.einsum(
        "rd,rc->dc", grad_mid_all, heads_flat, preferred_element_type=jnp.float32
    )
    grad_keys, grad_values, grad_query = attend_backward(
        query_all,
        key_all,
        value_all,
        grad_heads.reshape(group_rows, head_count, HEAD_DIM),
        log_masses,
        first_block,
        block_rows,
        score_scale,
    )
    grad_qkv = jnp.concatenate(
        [
            grad_query.reshape(group_rows, head_cols),
            grad_keys.reshape(group_rows, head_cols),
            grad_values.reshape(group_rows, head_cols),
        ],
        axis=1,
    ).astype(jnp.bfloat16)
    normed1_used = spread_again(normed1_low)
    grad_proj_in = jnp.einsum(
        "rd,rc->dc", normed1_used, grad_qkv, preferred_element_type=jnp.float32
    )
    grad_normed1 = input_total(grad_qkv, proj_in)
    res_norm_grad, gain1_grad, bias_first_cotangent = norm1_back(grad_normed1)
    input_grad = grad_middle + res_norm_grad
    norm_grads = jnp.stack([gain1_grad, bias_first_cotangent, gain2_grad, shift2_grad])
    norm_total, knn_total, loss_total = lax.psum(
        (norm_grads, knn_grads, jnp.sum(token_loss)), ("dp", "tensor")
    )
    token_count = group_rows * lax.axis_size("dp")
    attn_local = jnp.stack(
        [
            grad_proj_in[:, :head_cols],
            grad_proj_in[:, head_cols : 2 * head_cols],
            grad_proj_in[:, 2 * head_cols :],
            grad_out_proj,
        ]
    )
    attn_grad, ffn_grad = (
        lax.psum_scatter(attn_local, "dp", scatter_dimension=1, tiled=True),
        lax.psum_scatter(ffn_local, "dp", scatter_dimension=1, tiled=True),
    )
    attn_rows, ffn_rows = (
        lax.all_gather(attn_grad.astype(jnp.bfloat16), "tensor", axis=2, tiled=True).astype(
            attn_grad.dtype
        ),
        lax.all_gather(ffn_grad.astype(jnp.bfloat16), "tensor", axis=2, tiled=True).astype(
            ffn_grad.dtype
        ),
    )
    attn_right_sum, ffn_right_sum = right_statistics(attn_grad, ffn_grad, attn_rows, ffn_rows)
    attn_turned = jnp.einsum(
        "sri,sij->srj", attn_rows, attn_right_root, precision=lax.Precision.HIGHEST
    )
    ffn_turned = jnp.einsum(
        "sri,sij->srj", ffn_rows, ffn_right_root, precision=lax.Precision.HIGHEST
    )
    attn_cols, ffn_cols, attn_turned_cols, ffn_turned_cols = (
        lax.all_gather(attn_grad.astype(jnp.bfloat16), "dp", axis=1, tiled=True).astype(
            attn_grad.dtype
        ),
        lax.all_gather(ffn_grad.astype(jnp.bfloat16), "dp", axis=1, tiled=True).astype(
            ffn_grad.dtype
        ),
        lax.all_gather(attn_turned.astype(jnp.bfloat16), "dp", axis=1, tiled=True).astype(
            attn_turned.dtype
        ),
        lax.all_gather(ffn_turned.astype(jnp.bfloat16), "dp", axis=1, tiled=True).astype(
            ffn_turned.dtype
        ),
    )
    attn_left_sum, ffn_left_sum = left_statistics(attn_grad, ffn_grad, attn_cols, ffn_cols)
    attn_update = jnp.einsum(
        "srq,sqi->sri", attn_left_root, attn_turned_cols, precision=lax.Precision.HIGHEST
    )
    ffn_update = jnp.einsum(
        "srq,sqi->sri", ffn_left_root, ffn_turned_cols, precision=lax.Precision.HIGHEST
    )
    attn_left_new = 0.5 * attn_left + 0.5 * attn_left_sum
    attn_right_new = 0.5 * attn_right + 0.5 * attn_right_sum
    ffn_left_new = 0.5 * ffn_left + 0.5 * ffn_left_sum
    ffn_right_new = 0.5 * ffn_right + 0.5 * ffn_right_sum
    attn_new = attn_weights - shampoo_rate * (attn_update + shampoo_decay * attn_weights)
    ffn_new = ffn_weights - shampoo_rate * (ffn_update + shampoo_decay * ffn_weights)
    norm_m1, norm_m2, norm_new = adamw_step(norm_params, norm_total, norm_moment1, norm_moment2)
    knn_m1, knn_m2, knn_new = adamw_step(blending_coefficients, knn_total, knn_moment1, knn_moment2)
    return (
        mixed,
        input_grad,
        loss_total / token_count,
        attn_grad,
        attn_left_new,
        attn_right_new,
        attn_new,
        ffn_grad,
        ffn_left_new,
        ffn_right_new,
        ffn_new,
        norm_m1,
        norm_m2,
        norm_new,
        knn_m1,
        knn_m2,
        knn_new,
    )


def solution(mesh):
    placed = (
        P(("dp", "tensor"), None),
        P(("dp", "tensor"), None),
        P(("dp", "tensor")),
        P(("dp", "tensor")),
        P(("dp", "tensor"), None),
        P(("dp", "tensor"), None),
        P("dp", None),
        P(None, "dp", "tensor"),
        P(None, "dp", "tensor"),
        P(None, "dp", "tensor"),
        P(None, "tensor", "dp"),
        P(None, "dp", "tensor"),
        P(None, "tensor", "dp"),
        P(None, "dp", None),
        P(None, None, "tensor"),
        P(None, "dp", None),
        P(None, None, "tensor"),
        P(),
        P(),
        P(),
        P(),
        P(),
        P(),
    )
    return jax.shard_map(
        local,
        mesh=mesh,
        in_specs=placed,
        out_specs=(
            P(("dp", "tensor"), None),
            P(("dp", "tensor"), None),
            P(),
            P(None, "dp", "tensor"),
            P(None, "dp", "tensor"),
            P(None, "tensor", "dp"),
            P(None, "dp", "tensor"),
            P(None, "dp", "tensor"),
            P(None, "dp", "tensor"),
            P(None, "tensor", "dp"),
            P(None, "dp", "tensor"),
            P(),
            P(),
            P(),
            P(),
            P(),
            P(),
        ),
        check_vma=False,
    )
```

profile of v0, /device:TPU:0, one launch (start us, length us, event | category | flops | bytes accessed | tf_op | source)
XLA Modules:
  0.0 1511.2 jit_solution(8410613851047264241)
XLA Ops:
  13.9 27.3 %all-gather.15.cloned.1.call-done = bf16[4,1024,256]{2,1,0:T(8,128)(2,1)} async-done(((bf16[4,128,256]{2,1,0:T(8,128)(2,1)}), bf16[4,1024,256]{2,1,0:T(8,128)(2,1)}) %all-gather.15.cloned.1.call-update) | async-done | bytes 2097168 | tf_op jit(solution)/shard_map/all_gather | solution.py:289
  43.4 63.4 %all-gather.13.cloned.1.call-done = bf16[1536,1024]{1,0:T(8,128)(2,1)} async-done(((bf16[384,1024]{1,0:T(8,128)(2,1)}), bf16[1536,1024]{1,0:T(8,128)(2,1)}) %all-gather.13.cloned.1.call-update) | async-done | bytes 3145744 | tf_op jit(solution)/shard_map/all_gather | solution.py:29
  112.8 74.8 %while.113 = (s32[]{:T(128)}, bf16[3,512,4,64]{1,3,2,0:T(8,128)(2,1)}, f32[3,4,512]{2,1,0:T(4,128)S(1)}, s32[3]{0:T(128)S(1)}, s32[3]{0:T(128)S(1)}, /*index=5*/...) while((s32[]{:T(128)}, ...), condition=%wide.region_11.12_spmd, body=%wide.region_4.11_spmd.sunk | while | flops 414982144 | bytes 14075779 | solution.py:124
  141.2 11.9 while.118
  168.3 17.6 %while.118 = (s32[]{:T(128)}, f32[512,4,64]{0,2,1:T(8,128)}, s32[]{:T(128)}, bf16[1536,4,64]{0,2,1:T(8,128)(2,1)}, s32[]{:T(128)}, /*index=5*/bf16[1536,4,64]{0,...) while((s32[]{:T(128)}, f32[512,4,64]{0,2,1:T(8,128)}, ...), condition=%wide.region_10.10_spmd, body=%wide.region_9.9_spmd.sunk | while | flops 273024000 | bytes 2376883 | solution.py:116
  197.6 106.9 %reduce-scatter.13.cloned.1.call-done = f32[384,1024]{1,0:T(8,128)} async-done(((f32[1536,1024]{1,0:T(8,128)}), f32[384,1024]{1,0:T(8,128)}) %reduce-scatter.13.cloned.1.call-update) | async-done | bytes 1572880 | tf_op jit(solution)/shard_map/reduce_scatter | solution.py:41
  316.8 27.4 %all-gather.19.cloned.1.call-done = bf16[2,1024,1024]{2,1,0:T(8,128)(2,1)} async-done(((bf16[2,128,1024]{2,1,0:T(8,128)(2,1)}), bf16[2,1024,1024]{2,1,0:T(8,128)(2,1)}) %all-gather.19.cloned.1.call-update) | async-done | bytes 4194320 | tf_op jit(solution)/shard_map/all_gather | solution.py:290
  344.1 65.5 %all-gather.17.cloned.1.call-done = bf16[1536,1024]{1,0:T(8,128)(2,1)} async-done(((bf16[384,1024]{1,0:T(8,128)(2,1)}), bf16[1536,1024]{1,0:T(8,128)(2,1)}) %all-gather.17.cloned.1.call-update) | async-done | bytes 3145744 | tf_op jit(solution)/shard_map/all_gather | solution.py:29
  418.3 55.5 %all-gather.21.cloned.1.call-done = bf16[1536,1024]{1,0:T(8,128)(2,1)} async-done(((bf16[384,1024]{1,0:T(8,128)(2,1)}), bf16[1536,1024]{1,0:T(8,128)(2,1)}) %all-gather.21.cloned.1.call-update) | async-done | bytes 3145744 | tf_op jit(solution)/shard_map/all_gather | solution.py:37
  473.8 10.5 fusion.61
  491.9 10.0 fusion.69
  502.0 99.2 %reduce-scatter.17.cloned.1.call-done = f32[384,1024]{1,0:T(8,128)} async-done(((f32[1536,1024]{1,0:T(8,128)}), f32[384,1024]{1,0:T(8,128)}) %reduce-scatter.17.cloned.1.call-update) | async-done | bytes 1572880 | tf_op jit(solution)/shard_map/reduce_scatter | solution.py:50
  604.3 110.5 %reduce-scatter.15.cloned.1.call-done = f32[384,1024]{1,0:T(8,128)} async-done(((f32[1536,1024]{1,0:T(8,128)}), f32[384,1024]{1,0:T(8,128)}) %reduce-scatter.15.cloned.1.call-update) | async-done | bytes 1572880 | tf_op jit(solution)/shard_map/reduce_scatter | solution.py:41
  739.4 45.8 %all-gather.23.cloned.1.call-done = bf16[1536,1024]{1,0:T(8,128)(2,1)} async-done(((bf16[384,1024]{1,0:T(8,128)(2,1)}), bf16[1536,1024]{1,0:T(8,128)(2,1)}) %all-gather.23.cloned.1.call-update) | async-done | bytes 3145744 | tf_op jit(solution)/shard_map/all_gather | solution.py:37
  791.9 100.1 %while.116 = (s32[]{:T(128)}, f32[1536,4,64]{0,2,1:T(8,128)}, f32[1536,4,64]{0,2,1:T(8,128)}, bf16[1536,4,64]{0,2,1:T(8,128)(2,1)}, s32[3]{0:T(128)S(1)}, /*inde...) while((s32[]{:T(128)}, f32[1536,4,64]{0,2,1:T(8,128)}, ...), condition=%wide.region_28.29_spmd, body=%wide.region_22.28_spmd.sunk | while | flops 956434432 | bytes 66692192 | solution.py:214
  798.8 11.0 while.120
  822.0 21.4 %while.120 = (s32[]{:T(128)}, f32[512,4,64]{0,2,1:T(8,128)}, f32[1536,4,64]{0,2,1:T(8,128)}, f32[1536,4,64]{0,2,1:T(8,128)}, s32[]{:T(128)}, /*index=5*/bf16[153...) while((s32[]{:T(128)}, f32[512,4,64]{0,2,1:T(8,128)}, ...), condition=%wide.region_27.27_spmd, body=%wide.region_26.26_spmd.sunk | while | flops 682492928 | bytes 54034828 | solution.py:202
  847.6 10.5 while.119
  859.0 31.2 %while.120 = (s32[]{:T(128)}, f32[512,4,64]{0,2,1:T(8,128)}, f32[1536,4,64]{0,2,1:T(8,128)}, f32[1536,4,64]{0,2,1:T(8,128)}, s32[]{:T(128)}, /*index=5*/bf16[153...) while((s32[]{:T(128)}, f32[512,4,64]{0,2,1:T(8,128)}, ...), condition=%wide.region_27.27_spmd, body=%wide.region_26.26_spmd.sunk | while | flops 682492928 | bytes 54034828 | solution.py:202
  907.9 46.7 %reduce-scatter.21.cloned.1.call-done = f32[4,128,256]{2,1,0:T(8,128)} async-done(((f32[4,1024,256]{2,1,0:T(8,128)}), f32[4,128,256]{2,1,0:T(8,128)}) %reduce-scatter.21.cloned.1.call-update) | async-done | bytes 524304 | tf_op jit(solution)/shard_map/reduce_scatter | solution.py:404
  957.3 35.9 %all-gather.31.cloned.1.call-done = bf16[2,1024,1024]{2,1,0:T(8,128)(2,1)} async-done(((bf16[2,128,1024]{2,1,0:T(8,128)(2,1)}), bf16[2,1024,1024]{2,1,0:T(8,128)(2,1)}) %all-gather.31.cloned.1.call-update) | async-done | bytes 4194320 | tf_op jit(solution)/shard_map/all_gather | solution.py:426
  1000.8 39.9 %all-gather.33.cloned.1.call-done = bf16[2,128,4096]{2,1,0:T(8,128)(2,1)} async-done(((bf16[2,128,1024]{2,1,0:T(8,128)(2,1)}), bf16[2,128,4096]{2,1,0:T(8,128)(2,1)}) %all-gather.33.cloned.1.call-update) | async-done | bytes 2097168 | tf_op jit(solution)/shard_map/all_gather | solution.py:411
  1040.7 18.8 %convolution_convert_fusion.6 = bf16[2,128,1024]{2,1,0:T(8,128)(2,1)} fusion(bf16[2,128,4096]{2,1,0:T(8,128)(2,1)} %all-gather.33.cloned.1.call-done, f32[2,4096,1024]{2,1,0:T(8,128)} %param.51), kind=kOutput, calls=%fused_computation.141 | convolution fusion | flops 12885164032 | bytes 36175872 | tf_op jit(solution)/shard_map/sri,sij->srj/dot_general | solution.py:419
  1059.5 12.1 all-gather.27.cloned.1.call-done
  1105.0 18.6 %convolution_convert_fusion = bf16[2,1024,4096]{2,1,0:T(8,128)(2,1)} fusion(f32[2,128,1024]{2,1,0:T(8,128)} %reduce-scatter.25.cloned.1.call-done, bf16[2,128,4096]{2,1,0:T(8,128)(2,1)} %all-gather.33.cloned.1.call-done), kind=kOutput, calls=%fused_computation.76 | convolution fusion | flops 12893290496 | bytes 19922944 | tf_op jit(solution)/shard_map/sri,srj->sij/dot_general | solution.py:221
  1129.9 30.9 %all-gather.35.cloned.1.call-done = bf16[2,1024,1024]{2,1,0:T(8,128)(2,1)} async-done(((bf16[2,128,1024]{2,1,0:T(8,128)(2,1)}), bf16[2,1024,1024]{2,1,0:T(8,128)(2,1)}) %all-gather.35.cloned.1.call-update) | async-done | bytes 4194320 | tf_op jit(solution)/shard_map/all_gather | solution.py:432
  1171.2 34.5 %reduce-scatter.31.cloned.1.call-done = bf16[128,1024]{1,0:T(8,128)(2,1)} async-done(((bf16[1024,1024]{1,0:T(8,128)(2,1)}), bf16[128,1024]{1,0:T(8,128)(2,1)}) %reduce-scatter.31.cloned.1.call-update) | async-done | bytes 262160
  1209.0 26.7 %all-gather.29.cloned.1.call-done = bf16[4,1024,256]{2,1,0:T(8,128)(2,1)} async-done(((bf16[4,128,256]{2,1,0:T(8,128)(2,1)}), bf16[4,1024,256]{2,1,0:T(8,128)(2,1)}) %all-gather.29.cloned.1.call-update) | async-done | bytes 2097168 | tf_op jit(solution)/shard_map/all_gather | solution.py:429
  1239.3 109.4 %reduce-scatter.19.cloned.1.call-done = f32[384,1024]{1,0:T(8,128)} async-done(((f32[1536,1024]{1,0:T(8,128)}), f32[384,1024]{1,0:T(8,128)}) %reduce-scatter.19.cloned.1.call-update) | async-done | bytes 1572880 | tf_op jit(solution)/shard_map/reduce_scatter | solution.py:50
  1351.7 27.1 %reduce-scatter.23.cloned.1.call-done = bf16[4,128,256]{2,1,0:T(8,128)(2,1)} async-done(((bf16[4,128,1024]{2,1,0:T(8,128)(2,1)}), bf16[4,128,256]{2,1,0:T(8,128)(2,1)}) %reduce-scatter.23.cloned.1.call-update) | async-done | bytes 262160 | tf_op jit(solution)/shard_map/reduce_scatter | solution.py:238
  1380.6 39.2 %all-reduce = (f32[]{:T(128)}, f32[4,1024]{1,0:T(4,128)S(1)}, f32[2]{0:T(128)S(1)}) all-reduce(f32[]{:T(128)S(6)} %neg.30, f32[4,1024]{1,0:T(4,128)S(1)} %pad_maximum_fusion.8, f32[2]{0:T(128)S(1)} %pad_maximum_fusion.9), channel_id=1, replica_groups=mesh['dp'=8,'tensor'=4] {'dp','tensor'}, use_global_device_ids=true, to_apply=%region_33.34 | all-reduce | flops 4099 | bytes 32792 | tf_op jit(solution)/shard_map/psum | solution.py:391
  1425.7 71.5 %reduce-scatter.29.cloned.1.call-done = bf16[2,1024,512]{2,1,0:T(8,128)(2,1)} async-done(((bf16[2,1024,4096]{2,1,0:T(8,128)(2,1)}), bf16[2,1024,512]{2,1,0:T(8,128)(2,1)}) %reduce-scatter.29.cloned.1.call-update) | async-done | bytes 2097168 | tf_op jit(solution)/shard_map/reduce_scatter | solution.py:226
  (486 shorter events, 347.1 us)
Async XLA Ops:
  7.2 1228.5 %copy-start = (f32[4,128,1024]{2,1,0:T(8,128)S(1)}, f32[4,128,1024]{2,1,0:T(8,128)}, u32[]{:S(2)}) copy-start(f32[4,128,1024]{2,1,0:T(8,128)} %param.48) | copy-start | bytes 6291460
  7.2 33.9 %all-gather.15.cloned.1.call-start = ((), (), s32[]{:S(2)}) async-start(), calls=%async_computation.11 | async-start | bytes 2359296 | tf_op jit(solution)/shard_map/all_gather | solution.py:289
  9.2 97.6 %all-gather.13.cloned.1.call-start = ((), (), s32[]{:S(2)}) async-start(), calls=%async_computation.10 | async-start | bytes 3932160 | tf_op jit(solution)/shard_map/all_gather | solution.py:29
  13.4 291.1 %reduce-scatter.13.cloned.1.call-start = ((), (), s32[]{:S(2)}) async-start(), calls=%async_computation.12 | async-start | bytes 7864320 | tf_op jit(solution)/shard_map/reduce_scatter | solution.py:41
  195.4 148.7 %all-gather.19.cloned.1.call-start = ((), (), s32[]{:S(2)}) async-start(), calls=%async_computation.14 | async-start | bytes 4718592 | tf_op jit(solution)/shard_map/all_gather | solution.py:290
  197.6 212.1 %all-gather.17.cloned.1.call-start = ((), (), s32[]{:S(2)}) async-start(), calls=%async_computation.13 | async-start | bytes 3932160 | tf_op jit(solution)/shard_map/all_gather | solution.py:29
  308.7 165.1 %all-gather.21.cloned.1.call-start = ((), (), s32[]{:S(2)}) async-start(), calls=%async_computation.16 | async-start | bytes 3932160 | tf_op jit(solution)/shard_map/all_gather | solution.py:37
  315.6 403.1 %copy-start.37 = (f32[384]{0:T(512)}, f32[384]{0:T(512)S(1)}, u32[]{:S(2)}) copy-start(f32[384]{0:T(512)S(1)} %get-tuple-element.933) | copy-start | bytes 4612
  316.7 284.5 %reduce-scatter.17.cloned.1.call-start = ((), (), s32[]{:S(2)}) async-start(), calls=%async_computation.17 | async-start | bytes 7864320 | tf_op jit(solution)/shard_map/reduce_scatter | solution.py:50
  491.6 223.2 %reduce-scatter.15.cloned.1.call-start = ((), (), s32[]{:S(2)}) async-start(), calls=%async_computation.15 | async-start | bytes 7864320 | tf_op jit(solution)/shard_map/reduce_scatter | solution.py:41
  501.9 283.3 %all-gather.23.cloned.1.call-start = ((), (), s32[]{:S(2)}) async-start(), calls=%async_computation.18 | async-start | bytes 3932160 | tf_op jit(solution)/shard_map/all_gather | solution.py:37
  721.0 184.0 %reduce-scatter.25.cloned.1.call-start = ((), (), s32[]{:S(2)}) async-start(), calls=%async_computation.25 | async-start | bytes 9437184 | tf_op jit(solution)/shard_map/reduce_scatter | solution.py:405
  738.9 215.7 %reduce-scatter.21.cloned.1.call-start = ((), (), s32[]{:S(2)}) async-start(), calls=%async_computation.20 | async-start | bytes 4718592 | tf_op jit(solution)/shard_map/reduce_scatter | solution.py:404
  904.9 88.2 %all-gather.31.cloned.1.call-start = ((), (), s32[]{:S(2)}) async-start(), calls=%async_computation.26 | async-start | bytes 4718592 | tf_op jit(solution)/shard_map/all_gather | solution.py:426
  907.1 133.6 %all-gather.33.cloned.1.call-start = ((), (), s32[]{:S(2)}) async-start(), calls=%async_computation.28 | async-start | bytes 2621440 | tf_op jit(solution)/shard_map/all_gather | solution.py:411
  907.9 163.8 %all-gather.27.cloned.1.call-start = ((), (), s32[]{:S(2)}) async-start(), calls=%async_computation.23 | async-start | bytes 1310720 | tf_op jit(solution)/shard_map/all_gather | solution.py:408
  956.4 143.8 %all-gather.25.cloned.1.call-start = ((), (), s32[]{:S(2)}) async-start(), calls=%async_computation.21 | async-start | bytes 2359296 | tf_op jit(solution)/shard_map/all_gather | solution.py:423
  957.0 171.2 %reduce-scatter.27.cloned.1.call-start = ((), (), s32[]{:S(2)}) async-start(), calls=%async_computation.27 | async-start | bytes 655360 | tf_op jit(solution)/shard_map/reduce_scatter | solution.py:241
  1000.7 160.0 %all-gather.35.cloned.1.call-start = ((), (), s32[]{:S(2)}) async-start(), calls=%async_computation.30 | async-start | bytes 4718592 | tf_op jit(solution)/shard_map/all_gather | solution.py:432
  1059.5 146.2 %reduce-scatter.31.cloned.1.call-start = ((), (), s32[]{:S(2)}) async-start(), calls=%async_computation.31 | async-start | bytes 2359296
  1083.7 152.0 %all-gather.29.cloned.1.call-start = ((), (), s32[]{:S(2)}) async-start(), calls=%async_computation.24 | async-start | bytes 2359296 | tf_op jit(solution)/shard_map/all_gather | solution.py:429
  1088.6 260.1 %reduce-scatter.19.cloned.1.call-start = ((), (), s32[]{:S(2)}) async-start(), calls=%async_computation.19 | async-start | bytes 7864320 | tf_op jit(solution)/shard_map/reduce_scatter | solution.py:50
  1096.1 282.7 %reduce-scatter.23.cloned.1.call-start = ((), (), s32[]{:S(2)}) async-start(), calls=%async_computation.22 | async-start | bytes 1310720 | tf_op jit(solution)/shard_map/reduce_scatter | solution.py:238
  1105.0 392.2 %reduce-scatter.29.cloned.1.call-start = ((), (), s32[]{:S(2)}) async-start(), calls=%async_computation.29 | async-start | bytes 18874368 | tf_op jit(solution)/shard_map/reduce_scatter | solution.py:226
  1209.0 139.7 %copy-start.8 = (bf16[384,1024]{1,0:T(8,128)(2,1)S(1)}, bf16[384,1024]{1,0:T(8,128)(2,1)}, u32[]{:S(2)}) copy-start(bf16[384,1024]{1,0:T(8,128)(2,1)} %param.35) | copy-start | bytes 2359300
  1209.0 139.7 %copy-start.30 = (f32[1,1024]{1,0:T(1,128)S(1)}, f32[1,1024]{1,0:T(1,128)}, u32[]{:S(2)}) copy-start(f32[1,1024]{1,0:T(1,128)} %copy-done.29) | copy-start | bytes 12292
  1209.0 139.7 %copy-start.32 = (f32[384]{0:T(512)S(1)}, f32[384]{0:T(512)}, u32[]{:S(2)}) copy-start(f32[384]{0:T(512)} %copy-done.31) | copy-start | bytes 4612
  1239.3 111.4 %copy-start.42 = (f32[384]{0:T(512)S(1)}, f32[384]{0:T(512)}, u32[]{:S(2)}) copy-start(f32[384]{0:T(512)} %copy-done.41) | copy-start | bytes 4612
  1239.3 111.5 %copy-start.36 = (f32[384]{0:T(512)S(1)}, f32[384]{0:T(512)}, u32[]{:S(2)}) copy-start(f32[384]{0:T(512)} %copy-done.35) | copy-start | bytes 4612
  1239.3 112.4 %copy-start.43 = (f32[1024]{0:T(1024)S(1)}, f32[1024]{0:T(1024)}, u32[]{:S(2)}) copy-start(f32[1024]{0:T(1024)} %get-tuple-element.773) | copy-start | bytes 12292
  1239.3 112.4 %copy-start.44 = (f32[1024]{0:T(1024)S(1)}, f32[1024]{0:T(1024)}, u32[]{:S(2)}) copy-start(f32[1024]{0:T(1024)} %get-tuple-element.778) | copy-start | bytes 12292
  1239.3 139.6 %copy-start.25 = (f32[4,128,256]{2,1,0:T(8,128)S(1)}, f32[4,128,256]{2,1,0:T(8,128)}, u32[]{:S(2)}) copy-start(f32[4,128,256]{2,1,0:T(8,128)} %param.44) | copy-start | bytes 1572868
  (78 other events, 988.4 us)
Sparse Core Ops, SparseCore 0:
  10.6 30.5 all-gather.14
  43.3 63.4 all-gather.12
  195.5 108.9 reduce-scatter.12
  306.9 37.2 all-gather.18
  346.1 63.4 all-gather.16
  411.6 62.1 all-gather.20
  491.7 109.4 reduce-scatter.16
  603.5 111.2 reduce-scatter.14
  721.2 64.0 all-gather.22
  789.1 69.9 reduce-scatter.24
  905.0 49.5 reduce-scatter.20
  956.4 36.6 all-gather.30
  994.7 45.9 all-gather.32
  1042.7 28.9 all-gather.26
  1074.0 26.1 all-gather.24
  1102.3 21.6 reduce-scatter.26
  1125.8 34.9 all-gather.34
  1164.5 41.2 reduce-scatter.30
  1207.8 27.8 all-gather.28
  1238.0 110.7 reduce-scatter.18
  1351.1 27.6 reduce-scatter.22
  1382.4 114.7 reduce-scatter.28
where the time goes:
time: 1520 us; the launch traced here: 1510 us
  waiting for transfers between devices  1040 us (68%)
  matrix products  225 us (15%)
  other arithmetic  74 us (5%)
  local copies, waits for them, and re-layouts  68.4 us (5%)
  loops' own time  41.1 us (3%)
  blocking collectives  39.2 us (3%)
  between operations  19.3 us (1%)
    reduce_scatter x2, waiting for transfers between devices, branch_total(): lax.psum_scatter(jnp.einsum('rc,dc->rd', left_rows, right_mat, preferred_...  217 us
    reduce_scatter x2, waiting for transfers between devices, input_total(): lax.psum_scatter(jnp.einsum('rc,dc->rd', left_rows, right_mat, preferred_...  209 us
    all_gather x2, waiting for transfers between devices, spread_rows(): return lax.all_gather(local_low, 'tensor', axis=0, tiled=True)  129 us
    all_gather x2, waiting for transfers between devices, spread_grads(): return lax.all_gather(local_low, 'tensor', axis=0, tiled=True)  101 us
    reduce_scatter x1, waiting for transfers between devices, right_statistics(): lax.psum_scatter(ffn_part.astype(jnp.bfloat16), 'dp', scatter_dimension=2...  71.5 us
    reduce_scatter x1, waiting for transfers between devices, local(): lax.psum_scatter(attn_local, 'dp', scatter_dimension=1, tiled=True)  46.7 us
    all_gather x1, waiting for transfers between devices, local(): lax.all_gather(ffn_grad.astype(jnp.bfloat16), 'tensor', axis=2, tiled=True)  39.9 us
    psum x1, blocking collectives, local(): lax.psum((norm_grads, knn_grads, jnp.sum(token_loss)), ('dp', 'tensor'))  39.2 us
  transfers between devices with their start and end apart: 22, of which 20 were waited for; matrix products, arithmetic and copies ran while one was open for 17% of the time, Pallas kernels for 0%

commit v1 on v0

--- a/solution.py
+++ b/solution.py
@@ -1,6 +1,8 @@
 import jax
 import jax.numpy as jnp
 from jax import lax
+from jax.experimental import pallas as pl
+from jax.experimental.pallas import tpu as pltpu
 from jax.sharding import PartitionSpec as P
 
 SHORT = 512
@@ -469,7 +471,547 @@
     )
 
 
+LINE_BIT, HALF_BIT, CORE_BIT, X_BIT, Y_BIT = 1, 2, 4, 8, 16
+
+
+def flip(values_in, mask):
+    return lax.ppermute(
+        values_in, ("dp", "tensor"), [(index, index ^ mask) for index in range(32)]
+    )
+
+
+def swap_core_half(values_in):
+    pairs = []
+    for index in range(32):
+        core, half = (index >> 2) & 1, (index >> 1) & 1
+        pairs.append((index, (index & 25) | (half << 2) | (core << 1)))
+    return lax.ppermute(values_in, ("dp", "tensor"), pairs)
+
+
+def pick(values_in, index, axis):
+    return lax.dynamic_index_in_dim(values_in, index, axis, keepdims=False)
+
+
+def ordered_pair(own, other, bit, axis):
+    return jnp.where(
+        bit == 0, jnp.stack([own, other], axis=axis), jnp.stack([other, own], axis=axis)
+    )
+
+
+def gather_group(own):
+    near = flip(own, LINE_BIT)
+    far = flip(own, CORE_BIT)
+    both = flip(near, CORE_BIT)
+    return jnp.concatenate([own, near, far, both], axis=0)
+
+
+def reduce_group(partial_of, rows):
+    sent = partial_of(2 * rows, 4 * rows).astype(jnp.bfloat16)
+    received = flip(sent, CORE_BIT)
+    near = partial_of(rows, 2 * rows) + received[rows:].astype(jnp.float32)
+    from_near = flip(near.astype(jnp.bfloat16), LINE_BIT)
+    own = partial_of(0, rows) + received[:rows].astype(jnp.float32)
+    return own + from_near.astype(jnp.float32)
+
+
+def gather_weight(local_low, place, first, second):
+    stack_count, own_rows, width = local_low.shape
+    halves = local_low.reshape(stack_count, own_rows, 2, width // 2)
+    mine = pick(halves, place["core"], 2)
+    theirs = flip(pick(halves, 1 - place["core"], 2), CORE_BIT)
+    both_cores = ordered_pair(mine, theirs, place["core"], 1).reshape(
+        stack_count, 2 * own_rows, width // 2
+    )
+    block = ordered_pair(both_cores, flip(both_cores, HALF_BIT), place["half"], 2).reshape(
+        stack_count, 2 * own_rows, width
+    )
+    first_block = flip(block, first)
+    second_block = flip(block, second)
+    third_block = flip(first_block, second)
+    whole = jnp.zeros((stack_count, 8 * own_rows, width), local_low.dtype)
+    for part, mask in (
+        (block, 0),
+        (first_block, first),
+        (second_block, second),
+        (third_block, first ^ second),
+    ):
+        start = (place["chip"] ^ (mask // X_BIT)) * (2 * own_rows)
+        whole = lax.dynamic_update_slice_in_dim(whole, part, start, 1)
+    return whole
+
+
+def scatter_grad(partial, place, first):
+    stack_count, rows, width = partial.shape
+    parts = partial.reshape(stack_count, 2, 2, rows // 4, width)
+    at = {X_BIT: (2, place["x"]), Y_BIT: (1, place["y"])}
+    second = X_BIT + Y_BIT - first
+    axis, bit = at[first]
+    kept = pick(parts, bit, axis)
+    received = flip(pick(parts, 1 - bit, axis).astype(jnp.bfloat16), first)
+    kept = kept + received.astype(jnp.float32)
+    _, bit = at[second]
+    received = flip(pick(kept, 1 - bit, 1).astype(jnp.bfloat16), second)
+    kept = pick(kept, bit, 1) + received.astype(jnp.float32)
+    halves = kept.reshape(stack_count, 2, rows // 8, width)
+    received = flip(pick(halves, 1 - place["half"], 1).astype(jnp.bfloat16), HALF_BIT)
+    return (pick(halves, place["half"], 1) + received.astype(jnp.float32)).astype(jnp.bfloat16)
+
+
+def gather_grad(own, place, first):
+    stack_count, own_rows, width = own.shape
+    second = X_BIT + Y_BIT - first
+    own = own.reshape(stack_count, 1, own_rows, 2, 1, width // 2)
+    other_half = flip(own, HALF_BIT)
+    near = flip(own, LINE_BIT)
+    near_half = flip(other_half, LINE_BIT)
+    line = jnp.zeros((stack_count, 2, own_rows, 2, 2, width // 2), own.dtype)
+    half, line_bit = place["half"], place["line"]
+    for part, row, col in (
+        (own, half, line_bit),
+        (other_half, 1 - half, line_bit),
+        (near, half, 1 - line_bit),
+        (near_half, 1 - half, 1 - line_bit),
+    ):
+        line = lax.dynamic_update_slice(line, part, (0, row, 0, 0, col, 0))
+    line = line.reshape(stack_count, 1, 1, 2 * own_rows, 4, width // 2)
+    first_block = flip(line, first)
+    second_block = flip(line, second)
+    third_block = flip(first_block, second)
+    whole = jnp.zeros((stack_count, 2, 4, 2 * own_rows, 4, width // 2), own.dtype)
+    for part, mask in (
+        (line, 0),
+        (first_block, first),
+        (second_block, second),
+        (third_block, first ^ second),
+    ):
+        chip = place["chip"] ^ (mask // X_BIT)
+        whole = lax.dynamic_update_slice(whole, part, (0, place["core"], chip, 0, 0, 0))
+        whole = lax.dynamic_update_slice(
+            whole, flip(part, CORE_BIT), (0, 1 - place["core"], chip, 0, 0, 0)
+        )
+    return whole.reshape(stack_count, 2, 8 * own_rows, 4, width // 2)
+
+
+def sum_everywhere(values_in):
+    for mask in (CORE_BIT, LINE_BIT, HALF_BIT, X_BIT, Y_BIT):
+        values_in = values_in + flip(values_in, mask)
+    return values_in
+
+
+def dot32(spec, left_mat, right_mat):
+    return jnp.einsum(spec, left_mat, right_mat, preferred_element_type=jnp.float32)
+
+
+def shampoo_part(
+    whole, weights_in, left_in, right_in, left_root, right_low, place, tensor_index, dp_index
+):
+    stack_count, _, rows, blocks, width = whole.shape
+    own_rows = weights_in.shape[1]
+    left_low = left_root.astype(jnp.bfloat16)
+    flat = whole.reshape(stack_count, 2, rows, blocks * width)
+    turned = dot32("srq,scqk->scrk", left_low, flat).astype(jnp.bfloat16)
+    update = dot32("scrk,sckj->srj", turned, right_low)
+    dp_rows = lax.dynamic_slice_in_dim(flat, dp_index * own_rows, own_rows, 2)
+    line_rows = lax.dynamic_slice_in_dim(flat, tensor_index * 2 * own_rows, 2 * own_rows, 2)
+    left_sum = dot32("scrk,scqk->srq", dp_rows, line_rows)
+    tensor_cols = pick(whole, tensor_index, 3)
+    dp_cols = pick(pick(whole, place["chip"], 3), place["core"], 1)
+    right_sum = dot32("scrk,srj->sckj", tensor_cols, dp_cols).reshape(right_in.shape)
+    grad = lax.dynamic_slice_in_dim(tensor_cols, dp_index * own_rows, own_rows, 2)
+    grad = jnp.swapaxes(grad, 1, 2).reshape(weights_in.shape).astype(jnp.float32)
+    return (
+        grad,
+        0.5 * left_in + 0.5 * left_sum,
+        0.5 * right_in + 0.5 * right_sum,
+        weights_in - shampoo_rate * (update + shampoo_decay * weights_in),
+    )
+
+
+def right_root_low(right_root, blocks):
+    stack_count, rows, width = right_root.shape
+    low = right_root.astype(jnp.bfloat16).reshape(stack_count, blocks, 2, rows // (2 * blocks), width)
+    return jnp.swapaxes(low, 1, 2).reshape(stack_count, 2, rows // 2, width)
+
+
+def masked_heads(values_in, lanes, head, scale):
+    keep = (lanes >= head * HEAD_DIM) & (lanes < (head + 1) * HEAD_DIM)
+    return jnp.where(keep, values_in * scale, jnp.zeros_like(values_in))
+
+
+def forward_kernel(info_ref, qkv_ref, out_ref):
+    pieces = 4
+    rows = qkv_ref.shape[1] // pieces
+    me = info_ref[0]
+    starts = [pl.multiple_of((me ^ piece) * rows, rows) for piece in range(pieces)]
+    lanes = lax.broadcasted_iota(jnp.int32, (rows, 128), 1)
+    row_of = lax.broadcasted_iota(jnp.int32, (rows, rows), 0)
+    col_of = lax.broadcasted_iota(jnp.int32, (rows, rows), 1)
+    row_line = lax.broadcasted_iota(jnp.int32, (rows, 1), 0)
+    for query in range(pieces):
+        query_rows = qkv_ref[0, pl.ds(starts[query], rows), :]
+        place = row_line + query * rows
+        begin = info_ref[1] * jnp.ones_like(place)
+        for block in range(1, qkv_ref.shape[1] // SHORT):
+            begin = jnp.where(place >= block * SHORT, info_ref[1 + block], begin)
+        outs = []
+        for head in range(2):
+            query_head = masked_heads(query_rows, lanes, head, HEAD_DIM**-0.5)
+            scores = []
+            for key in range(query + 1):
+                key_rows = qkv_ref[1, pl.ds(starts[key], rows), :]
+                score = lax.dot_general(
+                    query_head, key_rows, (((1,), (1,)), ((), ())), preferred_element_type=jnp.float32
+                )
+                allowed = col_of + key * rows >= begin
+                if key == query:
+                    allowed = allowed & (col_of <= row_of)
+                scores.append(jnp.where(allowed, score, -1e30))
+            top = scores[0].max(axis=1, keepdims=True)
+            for score in scores[1:]:
+                top = jnp.maximum(top, score.max(axis=1, keepdims=True))
+            mass = jnp.zeros_like(top)
+            total = jnp.zeros((rows, 128), jnp.float32)
+            for key in range(query + 1):
+                value_rows = qkv_ref[2, pl.ds(starts[key], rows), :]
+                chance = jnp.exp(scores[key] - top)
+                mass = mass + chance.sum(axis=1, keepdims=True)
+                total = total + jnp.dot(
+                    chance.astype(jnp.bfloat16), value_rows, preferred_element_type=jnp.float32
+                )
+            outs.append(total / mass)
+        out = jnp.where(lanes < HEAD_DIM, outs[0], outs[1])
+        out_ref[pl.ds(starts[query], rows), :] = out.astype(jnp.bfloat16)
+
+
+def backward_kernel(info_ref, qkv_ref, grad_ref, out_ref, key_acc, value_acc, key_turned):
+    pieces = 4
+    rows = qkv_ref.shape[1] // pieces
+    me = info_ref[0]
+    starts = [pl.multiple_of((me ^ piece) * rows, rows) for piece in range(pieces)]
+    lanes = lax.broadcasted_iota(jnp.int32, (rows, 128), 1)
+    key_of = lax.broadcasted_iota(jnp.int32, (rows, rows), 0)
+    row_of = lax.broadcasted_iota(jnp.int32, (rows, rows), 1)
+    row_line = lax.broadcasted_iota(jnp.int32, (1, rows), 1)
+    key_acc[...] = jnp.zeros_like(key_acc)
+    value_acc[...] = jnp.zeros_like(value_acc)
+    for key in range(pieces):
+        key_rows = qkv_ref[1, pl.ds(starts[key], rows), :]
+        key_turned[key] = key_rows.astype(jnp.float32).T.astype(jnp.bfloat16)
+    for query in range(pieces):
+        query_rows = qkv_ref[0, pl.ds(starts[query], rows), :]
+        grad_rows = grad_ref[pl.ds(starts[query], rows), :]
+        place = row_line + query * rows
+        begin = info_ref[1] * jnp.ones_like(place)
+        for block in range(1, qkv_ref.shape[1] // SHORT):
+            begin = jnp.where(place >= block * SHORT, info_ref[1 + block], begin)
+        query_grad = jnp.zeros((128, rows), jnp.float32)
+        for head in range(2):
+            query_head = masked_heads(query_rows, lanes, head, HEAD_DIM**-0.5)
+            grad_head = masked_heads(grad_rows, lanes, head, 1.0)
+            scores, slopes = [], []
+            for key in range(query + 1):
+                key_rows = qkv_ref[1, pl.ds(starts[key], rows), :]
+                score = lax.dot_general(
+                    key_rows, query_head, (((1,), (1,)), ((), ())), preferred_element_type=jnp.float32
+                )
+                allowed = key_of + key * rows >= begin
+                if key == query:
+                    allowed = allowed & (key_of <= row_of)
+                scores.append(jnp.where(allowed, score, -1e30))
+            top = scores[0].max(axis=0, keepdims=True)
+            for score in scores[1:]:
+                top = jnp.maximum(top, score.max(axis=0, keepdims=True))
+            mass = jnp.zeros_like(top)
+            inner = jnp.zeros_like(top)
+            chances = []
+            for key in range(query + 1):
+                value_rows = qkv_ref[2, pl.ds(starts[key], rows), :]
+                slope = lax.dot_general(
+                    value_rows, grad_head, (((1,), (1,)), ((), ())), preferred_element_type=jnp.float32
+                )
+                chance = jnp.exp(scores[key] - top)
+                mass = mass + chance.sum(axis=0, keepdims=True)
+                inner = inner + (chance * slope).sum(axis=0, keepdims=True)
+                chances.append(chance)
+                slopes.append(slope)
+            share = 1.0 / mass
+            inner = inner * share
+            half = slice(head * HEAD_DIM, (head + 1) * HEAD_DIM)
+            parts = []
+            for key in range(query + 1):
+                probs = chances[key] * share
+                grad_scores = (probs * (slopes[key] - inner)).astype(jnp.bfloat16)
+                value_acc[key] += jnp.dot(
+                    probs.astype(jnp.bfloat16), grad_head, preferred_element_type=jnp.float32
+                )
+                key_acc[key] += jnp.dot(
+                    grad_scores, query_head, preferred_element_type=jnp.float32
+                )
+                parts.append(
+                    jnp.dot(
+                        key_turned[key, half, :], grad_scores, preferred_element_type=jnp.float32
+                    )
+                )
+            total = parts[0]
+            for part in parts[1:]:
+                total = total + part
+            if head == 0:
+                query_grad = total
+            else:
+                query_grad = jnp.concatenate([query_grad, total], axis=0)
+        out_ref[0, pl.ds(starts[query], rows), :] = (
+            query_grad.T * (HEAD_DIM**-0.5)
+        ).astype(jnp.bfloat16)
+    for key in range(pieces):
+        out_ref[1, pl.ds(starts[key], rows), :] = key_acc[key].astype(jnp.bfloat16)
+        out_ref[2, pl.ds(starts[key], rows), :] = value_acc[key].astype(jnp.bfloat16)
+
+
+def attend(info, qkv):
+    _, rows, width = qkv.shape
+    return pl.pallas_call(
+        forward_kernel,
+        grid_spec=pltpu.PrefetchScalarGridSpec(
+            num_scalar_prefetch=1,
+            grid=(width // 128,),
+            in_specs=[pl.BlockSpec((3, rows, 128), lambda pair, info_ref: (0, 0, pair))],
+            out_specs=pl.BlockSpec((rows, 128), lambda pair, info_ref: (0, pair)),
+        ),
+        out_shape=jax.ShapeDtypeStruct((rows, width), jnp.bfloat16),
+        compiler_params=pltpu.CompilerParams(vmem_limit_bytes=48 * 1024 * 1024),
+        cost_estimate=pl.CostEstimate(
+            flops=rows * rows * width * 2, bytes_accessed=8 * rows * width, transcendentals=0
+        ),
+    )(info, qkv)
+
+
+def attend_back(info, qkv, grad_heads):
+    _, rows, width = qkv.shape
+    return pl.pallas_call(
+        backward_kernel,
+        grid_spec=pltpu.PrefetchScalarGridSpec(
+            num_scalar_prefetch=1,
+            grid=(width // 128,),
+            in_specs=[
+                pl.BlockSpec((3, rows, 128), lambda pair, info_ref: (0, 0, pair)),
+                pl.BlockSpec((rows, 128), lambda pair, info_ref: (0, pair)),
+            ],
+            out_specs=pl.BlockSpec((3, rows, 128), lambda pair, info_ref: (0, 0, pair)),
+            scratch_shapes=[
+                pltpu.VMEM((4, rows // 4, 128), jnp.float32),
+                pltpu.VMEM((4, rows // 4, 128), jnp.float32),
+                pltpu.VMEM((4, 128, rows // 4), jnp.bfloat16),
+            ],
+        ),
+        out_shape=jax.ShapeDtypeStruct(qkv.shape, jnp.bfloat16),
+        compiler_params=pltpu.CompilerParams(vmem_limit_bytes=48 * 1024 * 1024),
+        cost_estimate=pl.CostEstimate(
+            flops=rows * rows * width * 5, bytes_accessed=14 * rows * width, transcendentals=0
+        ),
+    )(info, qkv, grad_heads)
+
+
+def regrouped(
+    tokens_in,
+    lm_grad,
+    lm_logprob,
+    targets,
+    neighbor_ids,
+    nearby_entry_gaps,
+    seq_lengths,
+    attn_weights,
+    ffn_weights,
+    attn_left,
+    attn_right,
+    ffn_left,
+    ffn_right,
+    attn_left_root,
+    attn_right_root,
+    ffn_left_root,
+    ffn_right_root,
+    norm_params,
+    norm_moment1,
+    norm_moment2,
+    blending_coefficients,
+    knn_moment1,
+    knn_moment2,
+):
+    low = jnp.bfloat16
+    rows = tokens_in.shape[0]
+    group_rows = 4 * rows
+    dp_index, tensor_index = lax.axis_index("dp"), lax.axis_index("tensor")
+    place = {
+        "line": tensor_index & 1,
+        "half": tensor_index >> 1,
+        "core": dp_index & 1,
+        "x": (dp_index >> 1) & 1,
+        "y": dp_index >> 2,
+        "chip": dp_index >> 1,
+    }
+    me = place["core"] * 2 + place["line"]
+
+    moved = swap_core_half(tokens_in)
+    wa, wf = attn_weights.astype(low), ffn_weights.astype(low)
+    w_first = gather_weight(wa[:2], place, X_BIT, Y_BIT)
+    w_second = gather_weight(wa[2:], place, Y_BIT, X_BIT)
+    w_up = gather_weight(wf[:1], place, X_BIT, Y_BIT)[0]
+    w_down = gather_weight(wf[1:], place, Y_BIT, X_BIT)[0]
+    proj_in = jnp.concatenate([w_first, w_second[:1]], axis=0)
+    proj_out = w_second[1]
+
+    lengths = swap_core_half(seq_lengths.astype(jnp.float32)).astype(jnp.int32)
+    block_begins = first_blocks(lengths, group_rows, SHORT) * SHORT
+    info = jnp.concatenate([me[None].astype(jnp.int32), block_begins.astype(jnp.int32)])
+
+    resid = moved.astype(jnp.float32)
+    normed1, norm1_back = jax.vjp(layer_norm, resid, norm_params[0], norm_params[1])
+    normed1_all = gather_group(normed1.astype(low))
+    qkv = dot32("rd,sdc->src", normed1_all, proj_in).astype(low)
+    heads_flat = attend(info, qkv)
+    attn_out = reduce_group(
+        lambda a, b: dot32("rc,dc->rd", heads_flat[a:b], proj_out), rows
+    )
+    middle = resid + attn_out
+    normed2, norm2_back = jax.vjp(layer_norm, middle, norm_params[2], norm_params[3])
+    normed2_all = gather_group(normed2.astype(low))
+
+    sharpness_divisor = jnp.exp(blending_coefficients[0])
+    interp = jax.nn.sigmoid(blending_coefficients[1])
+    nearby_entry_logits = -nearby_entry_gaps / sharpness_divisor
+    near_top = jnp.max(nearby_entry_logits, axis=1, keepdims=True)
+    near_exp = jnp.exp(nearby_entry_logits - near_top)
+    nearby_entry_shares = near_exp / jnp.sum(near_exp, axis=1, keepdims=True)
+    target_matches = (neighbor_ids == targets[:, None]).astype(jnp.float32)
+    retrieval_probability = jnp.sum(nearby_entry_shares * target_matches, axis=1)
+    lm_prob = jnp.exp(lm_logprob)
+    mixture = interp * retrieval_probability + (1.0 - interp) * lm_prob
+    token_loss = -jnp.log(mixture)
+    lm_weight = -(1.0 - interp) * lm_prob / mixture
+    temp_terms = (
+        jnp.sum(
+            nearby_entry_shares
+            * (target_matches - retrieval_probability[:, None])
+            * nearby_entry_gaps,
+            axis=1,
+        )
+        / sharpness_divisor
+    )
+    temp_grad = jnp.sum(-(interp / mixture) * temp_terms)
+    interp_grad = jnp.sum(-interp * (1.0 - interp) * (retrieval_probability - lm_prob) / mixture)
+    cotangent = swap_core_half(lm_weight)[:, None] * swap_core_half(lm_grad).astype(jnp.float32)
+    cot_all = gather_group(cotangent.astype(low))
+
+    hidden_pre = dot32("rd,df->rf", normed2_all, w_up)
+    hidden_act, gelu_back = jax.vjp(gelu_tanh, hidden_pre)
+    act_low = hidden_act.astype(low)
+    grad_act = dot32("rd,df->rf", cot_all, w_down)
+    grad_pre_low = gelu_back(grad_act)[0].astype(low)
+    grad_normed2 = reduce_group(
+        lambda a, b: dot32("rf,df->rd", grad_pre_low[a:b], w_up), rows
+    )
+    grad_up = dot32("rd,rf->df", normed2_all, grad_pre_low)
+    grad_down = dot32("rd,rf->df", cot_all, act_low)
+    mid_norm_grad, gain2_grad, shift2_grad = norm2_back(grad_normed2)
+    grad_middle = cotangent + mid_norm_grad
+    grad_mid_all = gather_group(grad_middle.astype(low))
+    grad_heads = dot32("rd,dc->rc", grad_mid_all, proj_out).astype(low)
+    grad_qkv = attend_back(info, qkv, grad_heads)
+    grad_out_proj = dot32("rd,rc->dc", grad_mid_all, heads_flat)
+    grad_proj_in = dot32("rd,src->sdc", normed1_all, grad_qkv)
+    grad_normed1 = reduce_group(
+        lambda a, b: dot32("src,sdc->rd", grad_qkv[:, a:b], proj_in), rows
+    )
+    ffn_out = reduce_group(lambda a, b: dot32("rf,df->rd", act_low[a:b], w_down), rows)
+    mixed = swap_core_half((middle + ffn_out).astype(low))
+
+    up_own = scatter_grad(grad_up[None], place, X_BIT)
+    down_own = scatter_grad(grad_down[None], place, Y_BIT)
+    first_own = scatter_grad(grad_proj_in[:2], place, X_BIT)
+    second_own = scatter_grad(
+        jnp.concatenate([grad_proj_in[2:], grad_out_proj[None]], axis=0), place, Y_BIT
+    )
+    up_whole = gather_grad(up_own, place, X_BIT)
+    down_whole = gather_grad(down_own, place, Y_BIT)
+    first_whole = gather_grad(first_own, place, X_BIT)
+    second_whole = gather_grad(second_own, place, Y_BIT)
+
+    res_norm_grad, gain1_grad, shift1_grad = norm1_back(grad_normed1)
+    input_grad = swap_core_half((grad_middle + res_norm_grad).astype(low)).astype(jnp.float32)
+
+    width = norm_params.shape[1]
+    scalars = jnp.zeros((1, width), jnp.float32)
+    scalars = scalars.at[0, 0].set(temp_grad).at[0, 1].set(interp_grad)
+    scalars = scalars.at[0, 2].set(jnp.sum(token_loss))
+    early = sum_everywhere(
+        jnp.concatenate([gain2_grad[None], shift2_grad[None], scalars], axis=0)
+    )
+    late = sum_everywhere(jnp.stack([gain1_grad, shift1_grad]))
+    norm_total = jnp.concatenate([late, early[:2]], axis=0)
+    knn_total = early[2, :2]
+    loss = early[2, 2] / (group_rows * 8)
+
+    blocks = 4
+    attn_right_low = right_root_low(attn_right_root, blocks)
+    ffn_right_low = right_root_low(ffn_right_root, blocks)
+    ffn_parts = [
+        shampoo_part(
+            whole,
+            ffn_weights[at : at + 1],
+            ffn_left[at : at + 1],
+            ffn_right[at : at + 1],
+            ffn_left_root[at : at + 1],
+            ffn_right_low[at : at + 1],
+            place,
+            tensor_index,
+            dp_index,
+        )
+        for at, whole in enumerate((up_whole, down_whole))
+    ]
+    attn_parts = [
+        shampoo_part(
+            whole,
+            attn_weights[at : at + 2],
+            attn_left[at : at + 2],
+            attn_right[at : at + 2],
+            attn_left_root[at : at + 2],
+            attn_right_low[at : at + 2],
+            place,
+            tensor_index,
+            dp_index,
+        )
+        for at, whole in ((0, first_whole), (2, second_whole))
+    ]
+    ffn_grad, ffn_left_new, ffn_right_new, ffn_new = (
+        jnp.concatenate(parts, axis=0) for parts in zip(*ffn_parts)
+    )
+    attn_grad, attn_left_new, attn_right_new, attn_new = (
+        jnp.concatenate(parts, axis=0) for parts in zip(*attn_parts)
+    )
+    norm_m1, norm_m2, norm_new = adamw_step(norm_params, norm_total, norm_moment1, norm_moment2)
+    knn_m1, knn_m2, knn_new = adamw_step(blending_coefficients, knn_total, knn_moment1, knn_moment2)
+    return (
+        mixed,
+        input_grad,
+        loss,
+        attn_grad,
+        attn_left_new,
+        attn_right_new,
+        attn_new,
+        ffn_grad,
+        ffn_left_new,
+        ffn_right_new,
+        ffn_new,
+        norm_m1,
+        norm_m2,
+        norm_new,
+        knn_m1,
+        knn_m2,
+        knn_new,
+    )
+
+
 def solution(mesh):
+    sized = (mesh.shape["dp"], mesh.shape["tensor"]) == (8, 4)
     placed = (
         P(("dp", "tensor"), None),
         P(("dp", "tensor"), None),
@@ -496,7 +1038,7 @@
         P(),
     )
     return jax.shard_map(
-        local,
+        regrouped if sized else local,
         mesh=mesh,
         in_specs=placed,
         out_specs=(

time: 1520 us -> 924 us (0.61)
  waiting for transfers between devices: 1040 us -> 190 us
  local copies, waits for them, and re-layouts: 68.4 us -> 346 us
  starting transfers between devices: 2.08 us -> 125 us
  matrix products: 225 us -> 136 us
  loops' own time: 41.1 us -> 0 us
  blocking collectives: 39.2 us -> 0 us
  Pallas kernels: 0 us -> 35.8 us
    reduce_scatter x9 -> x0, waiting for transfers between devices: 571 us -> none  [the longest x2 217 us: branch_total(): lax.psum_scatter(jnp.einsum('rc,dc->rd', left_rows, right_mat, preferred_...]
    all_gather x12 -> x0, waiting for transfers between devices: 434 us -> none  [the longest x2 129 us: spread_rows(): return lax.all_gather(local_low, 'tensor', axis=0, tiled=True)]
    ppermute x0 -> x108, waiting for transfers between devices: none -> 190 us  [the longest x102 190 us: flip(): lax.ppermute(values_in, ('dp', 'tensor'), [(index, index ^ mask) for inde...]
    dynamic_update_slice x3 -> x66, local copies, waits for them, and re-layouts: 5.56 us -> 142 us  [the longest x16 67.9 us: gather_grad(): line = lax.dynamic_update_slice(line, part, (0, row, 0, 0, col, 0))]
    ppermute x0 -> x108, starting transfers between devices: none -> 125 us  [the longest x102 98.6 us: flip(): lax.ppermute(values_in, ('dp', 'tensor'), [(index, index ^ mask) for inde...]
    dot_general x74 -> x32, matrix products: 225 us -> 136 us  [dot32(): jnp.einsum(spec, left_mat, right_mat, preferred_element_type=jnp.float32)]
    another operation x16 -> x19, local copies, waits for them, and re-layouts: 5.49 us -> 87.3 us  [the longest x4 43.8 us: shampoo_part(): flat = whole.reshape(stack_count, 2, rows, blocks * width)]
    another operation x14 -> x0, loops' own time: 41.1 us -> none  [the longest x3 13.5 us: one_block(): lax.fori_loop(first_block[query_block], query_block + 1, grad_step, (jnp....]
  transfers between devices with their start and end apart: 22 -> 108, of which waited for: 20 -> 40; matrix products, arithmetic and copies ran while one was open for 17% -> 58% of each run, Pallas kernels for 0% -> 4%
where the time goes in v1:
time: 924 us; the launch traced here: 909 us
  local copies, waits for them, and re-layouts  346 us (37%)
  waiting for transfers between devices  190 us (21%)
  matrix products  136 us (15%)
  starting transfers between devices  125 us (14%)
  other arithmetic  67.5 us (7%)
  Pallas kernels  35.8 us (4%)
    ppermute x102, waiting for transfers between devices, flip(): lax.ppermute(values_in, ('dp', 'tensor'), [(index, index ^ mask) for inde...  190 us
    dot_general x32, matrix products, dot32(): jnp.einsum(spec, left_mat, right_mat, preferred_element_type=jnp.float32)  136 us
    ppermute x102, starting transfers between devices, flip(): lax.ppermute(values_in, ('dp', 'tensor'), [(index, index ^ mask) for inde...  98.6 us
    dynamic_update_slice x16, local copies, waits for them, and re-layouts, gather_grad(): line = lax.dynamic_update_slice(line, part, (0, row, 0, 0, col, 0))  67.9 us
    dynamic_update_slice x18, local copies, waits for them, and re-layouts, gather_grad(): lax.dynamic_update_slice(whole, flip(part, CORE_BIT), (0, 1 - place['core...  46.1 us
    another operation x4, local copies, waits for them, and re-layouts, shampoo_part(): flat = whole.reshape(stack_count, 2, rows, blocks * width)  43.8 us
    another operation x15, local copies, waits for them, and re-layouts  43.5 us
    dynamic_update_slice x16, local copies, waits for them, and re-layouts, gather_grad(): lax.dynamic_update_slice(whole, part, (0, place['core'], chip, 0, 0, 0))  27.8 us
  transfers between devices with their start and end apart: 108, of which 40 were waited for; matrix products, arithmetic and copies ran while one was open for 58% of the time, Pallas kernels for 4%

profile of v1, /device:TPU:0, one launch (start us, length us, event | category | flops | bytes accessed | tf_op | source)
XLA Modules:
  0.0 909.0 jit_solution(10501323081479530520)
XLA Ops:
  18.7 14.2 %collective-permute-start.8 = (bf16[2,256,128]{2,1,0:T(8,128)(2,1)S(1)}, bf16[2,256,128]{2,1,0:T(8,128)(2,1)S(1)}, u32[]{:S(2)}, u32[]{:S(2)}) collective-permute-start(bf16[2,256,128]{2,1,0:T(8,128)(2,1)S(1)} %bitcast.538), channel_id=1, source_target_pairs={{0,2},{1,3},{2,0},{3,1},{4,6},{5,7},{6,4},{7,5},{8,10},{9,11},{10,... | collective-permute-start | bytes 393224 | tf_op jit(solution)/shard_map/ppermute | solution.py:478
  64.3 7.7 collective-permute-start.34
  76.6 11.3 %shard_map.350 = bf16[1536,256]{1,0:T(8,128)(2,1)S(1)} custom-call(s32[4]{0:T(128)S(1)} %pad_add_fusion.info_ref, bf16[3,1536,256]{2,1,0:T(8,128)(2,1)S(1)} %fusion.7.qkv_ref), custom_call_target="tpu_custom_call" | custom-call | flops 1207959552 | bytes 3145728 | tf_op jit(solution)/shard_map/pallas_call | solution.py:772
  108.1 12.1 %convert_element_type.479 = bf16[2,4096,1024]{2,1,0:T(8,128)(2,1)S(1)} convert(f32[2,4096,1024]{2,1,0:T(8,128)} %param.45) | non-fusion elementwise | flops 8388608 | bytes 50331648 | tf_op jit(solution)/shard_map/convert_element_type | solution.py:632
  146.1 11.2 %collective-permute-done.28 = bf16[1,256,1024]{1,2,0:T(8,128)(2,1)S(1)} collective-permute-done((bf16[1,256,1024]{1,2,0:T(8,128)(2,1)S(1)}, bf16[1,256,1024]{1,2,0:T(8,128)(2,1)S(1)}, u32[]{:S(2)}, u32[]{:S(2)}) %collective-permute-start.28) | collective-permute-done | bytes 524320 | tf_op jit(solution)/shard_map/ppermute | solution.py:478
  160.4 8.0 collective-permute-done.29
  173.1 10.3 %multiply_convert_fusion = (bf16[1536,1024]{1,0:T(8,128)(2,1)S(1)}, f32[1536,1024]{1,0:T(8,128)}) fusion(bf16[1024,1024]{0,1:T(8,128)(2,1)S(1)} %bitcast_dynamic-update-slice_fusion.10, bf16[384,1024]{1,0:T(8,128)(2,1)S(1)} %collective-permute-done.19, bf16[384,1024]{1,0:T(8,128)(2,1)S(1)} %collective-permute-done.18, ...), kind=kOutput, calls=%fused_computation.10 | convolution fusion | flops 3247964160 | bytes 14680064 | tf_op jit(solution)/shard_map/rd,df->rf/dot_general | solution.py:602
  191.7 12.2 %fusion.6 = bf16[1536,1024]{1,0:T(8,128)(2,1)} fusion(f32[1536,1024]{1,0:T(8,128)} %get-tuple-element.134, bf16[1024,1024]{0,1:T(8,128)(2,1)S(1)} %bitcast_dynamic-update-slice_fusion.7, bf16[384,1024]{1,0:T(8,128)(2,1)S(1)} %collective-permute-done.37, bf16[384,1024]{1,0:T(8,128)(2,1)} %copy-done.93, bf16[384,1024]{1,0:T(8,128)(2,1)} %copy-done.87, ...), kind=kOutput, calls=%fused_computation.9 | convolution fusion | flops 3265265664 | bytes 14680064 | tf_op jit(solution)/shard_map/rd,df->rf/dot_general | solution.py:602
  251.4 8.1 collective-permute-done.91
  268.4 11.5 %collective-permute-done.92 = bf16[1,128,1024]{2,1,0:T(8,128)(2,1)S(1)} collective-permute-done((bf16[1,128,1024]{2,1,0:T(8,128)(2,1)S(1)}, bf16[1,128,1024]{2,1,0:T(8,128)(2,1)S(1)}, u32[]{:S(2)}, u32[]{:S(2)}) %collective-permute-start.92) | collective-permute-done | bytes 262176 | tf_op jit(solution)/shard_map/ppermute | solution.py:478
  312.4 10.1 %collective-permute-done.81 = bf16[1,1,128,2,1,512]{2,5,3,4,1,0:T(8,128)(2,1)} collective-permute-done((bf16[1,1,128,2,1,512]{2,5,3,4,1,0:T(8,128)(2,1)S(1)}, bf16[1,1,128,2,1,512]{2,5,3,4,1,0:T(8,128)(2,1)}, u32[]{:S(2)}, u32[]{:S(2)}) %collective-permute-start.81) | collective-permute-done | bytes 262176 | tf_op jit(solution)/shard_map/ppermute | solution.py:478
  327.0 18.0 %collective-permute-done.95 = bf16[1,1,128,2,1,512]{5,2,1,4,3,0:T(8,128)(2,1)} collective-permute-done((bf16[1,1,128,2,1,512]{5,2,1,4,3,0:T(8,128)(2,1)}, bf16[1,1,128,2,1,512]{5,2,1,4,3,0:T(8,128)(2,1)}, u32[]{:S(2)}, u32[]{:S(2)}) %collective-permute-start.95) | collective-permute-done | bytes 262176 | tf_op jit(solution)/shard_map/ppermute | solution.py:478
  351.6 7.6 collective-permute-start.32
  363.9 10.3 %collective-permute-done.47 = f32[3,1024]{1,0:T(4,128)S(1)} collective-permute-done((f32[3,1024]{1,0:T(4,128)S(1)}, f32[3,1024]{1,0:T(4,128)S(1)}, u32[]{:S(2)}, u32[]{:S(2)}) %collective-permute-start.47) | collective-permute-done | bytes 12320 | tf_op jit(solution)/shard_map/ppermute | solution.py:478
  404.3 11.6 %collective-permute-done.84 = bf16[1,1,1,256,4,512]{5,3,4,2,1,0:T(8,128)(2,1)} collective-permute-done((bf16[1,1,1,256,4,512]{5,3,4,2,1,0:T(8,128)(2,1)}, bf16[1,1,1,256,4,512]{5,3,4,2,1,0:T(8,128)(2,1)}, u32[]{:S(2)}, u32[]{:S(2)}) %collective-permute-start.84) | collective-permute-done | bytes 1048608 | tf_op jit(solution)/shard_map/ppermute | solution.py:478
  427.1 24.5 %shard_map.351 = bf16[3,1536,256]{2,1,0:T(8,128)(2,1)S(1)} custom-call(s32[4]{0:T(128)S(1)} %pad_add_fusion.info_ref, bf16[3,1536,256]{2,1,0:T(8,128)(2,1)S(1)} %fusion.7.qkv_ref, bf16[1536,256]{1,0:T(8,128)(2,1)S(1)} %convolution_convert_fusion.3.grad_ref), custom_call_target="tpu_custom_call" | custom-call | flops 3019898880 | bytes 5505024 | tf_op jit(solution)/shard_map/pallas_call | solution.py:790
  491.4 14.8 %collective-permute-done.101 = bf16[1,1,1,256,4,512]{5,3,2,4,1,0:T(8,128)(2,1)} collective-permute-done((bf16[1,1,1,256,4,512]{5,3,2,4,1,0:T(8,128)(2,1)}, bf16[1,1,1,256,4,512]{5,3,2,4,1,0:T(8,128)(2,1)}, u32[]{:S(2)}, u32[]{:S(2)}) %collective-permute-start.101) | collective-permute-done | bytes 1048608 | tf_op jit(solution)/shard_map/ppermute | solution.py:478
  526.0 8.0 collective-permute-done.66
  552.1 7.4 dynamic_update_slice.228
  582.4 7.0 dynamic_update_slice.217
  598.7 7.0 dynamic_update_slice.231
  628.6 12.3 %copy.449 = bf16[1,2,4,256,4,512]{5,4,3,2,1,0:T(4,128)(2,1)} copy(bf16[1,2,4,256,4,512]{5,3,2,4,1,0:T(8,128)(2,1)} %constant_dynamic-update-slice_fusion) | data formatting | bytes 16777216 | tf_op jit(solution)/shard_map/dynamic_update_slice | solution.py:589
  642.3 8.4 copy.448
  656.5 14.3 %reshape_reshape.15 = bf16[1,2,1024,2048]{3,2,1,0:T(8,128)(2,1)} reshape(bf16[1,2,4,256,4,512]{5,4,3,2,1,0:T(4,128)(2,1)} %copy.449) | data formatting | bytes 16777216 | tf_op jit(solution)/shard_map/reshape;reshape | solution.py:611
  670.8 14.3 %reshape.882 = bf16[2,1024,2048]{2,1,0:T(8,128)(2,1)} reshape(bf16[1,2,4,256,4,512]{5,4,3,2,1,0:T(4,128)(2,1)} %copy.449) | data formatting | bytes 16777216 | tf_op jit(solution)/shard_map/reshape.207
  702.5 14.4 %reshape.880 = bf16[2,1024,2048]{2,1,0:T(8,128)(2,1)} reshape(bf16[1,2,4,256,4,512]{5,4,3,2,1,0:T(4,128)(2,1)} %copy.448) | data formatting | bytes 16777216 | tf_op jit(solution)/shard_map/reshape.200
  724.4 11.5 %fusion.44 = f32[1,128,1024]{2,1,0:T(8,128)} fusion(bf16[2,2048,1024]{2,1,0:T(8,128)(2,1)} %bitcast.486, bf16[2,1024,2048]{2,1,0:T(8,128)(2,1)} %reshape.882, f32[2,128,1024]{2,1,0:T(8,128)} %param.37, bf16[2,128,1024]{2,1,0:T(8,128)(2,1)S(1)} %copy-done.19), kind=kOutput, calls=%fused_computation.103 | convolution fusion | flops 2148532224 | bytes 18087936 | tf_op jit(solution)/shard_map/scrk,sckj->srj/dot_general | solution.py:602
  736.0 11.9 %fusion.45 = f32[1,128,1024]{2,1,0:T(8,128)} fusion(bf16[2,2048,1024]{2,1,0:T(8,128)(2,1)} %bitcast.485, bf16[2,1024,2048]{2,1,0:T(8,128)(2,1)} %reshape.880, f32[2,128,1024]{2,1,0:T(8,128)} %param.37, bf16[2,128,1024]{2,1,0:T(8,128)(2,1)S(1)} %copy-done.19), kind=kOutput, calls=%fused_computation.104 | convolution fusion | flops 2148532224 | bytes 18087936 | tf_op jit(solution)/shard_map/scrk,sckj->srj/dot_general | solution.py:602
  748.9 14.6 %reshape_reshape.14 = bf16[1,2,1024,2048]{3,2,1,0:T(8,128)(2,1)} reshape(bf16[1,2,4,256,4,512]{5,4,3,2,1,0:T(4,128)(2,1)} %copy.448) | data formatting | bytes 16777216 | tf_op jit(solution)/shard_map/reshape;reshape | solution.py:611
  826.1 7.5 collective-permute-start.45
  835.3 7.6 reshape_reshape.12
  854.2 7.3 reshape_reshape.13
  (689 shorter events, 543.5 us)
Async XLA Ops:
  58.8 39.4 %collective-permute-start.25 = (bf16[1,128,512]{2,1,0:T(8,128)(2,1)S(1)}, bf16[1,128,512]{2,1,0:T(8,128)(2,1)S(1)}, u32[]{:S(2)}, u32[]{:S(2)}) collective-permute-start(bf16[1,128,512]{2,1,0:T(8,128)(2,1)S(1)} %bitcast.549), channel_id=1, source_target_pairs={{0,4},{1,5},{2,6},{3,7},{4,0},{5,1},{6,2},{7,3},{8,12},{9,13},{10,... | collective-permute-start | bytes 393224 | tf_op jit(solution)/shard_map/ppermute | solution.py:478
  60.0 39.2 %collective-permute-start.20 = (bf16[1,128,512]{2,1,0:T(8,128)(2,1)}, bf16[1,128,512]{2,1,0:T(8,128)(2,1)}, u32[]{:S(2)}, u32[]{:S(2)}) collective-permute-start(bf16[1,128,512]{2,1,0:T(8,128)(2,1)} %bitcast.28), channel_id=1, source_target_pairs={{0,4},{1,5},{2,6},{3,7},{4,0},{5,1},{6,2},{7,3},{8,12},{9,13},{10,... | collective-permute-start | bytes 393224 | tf_op jit(solution)/shard_map/ppermute | solution.py:478
  64.3 73.7 %collective-permute-start.34 = (bf16[384,1024]{1,0:T(8,128)(2,1)}, bf16[384,1024]{1,0:T(8,128)(2,1)}, u32[]{:S(2)}, u32[]{:S(2)}) collective-permute-start(bf16[384,1024]{1,0:T(8,128)(2,1)} %param.30), channel_id=1, source_target_pairs={{0,0},{1,1},{2,4},{3,5},{4,2},{5,3},{6,6},{7,7},{8,8},{9,9},{10,12... | collective-permute-start | bytes 2359304 | tf_op jit(solution)/shard_map/ppermute | solution.py:488
  93.4 39.2 %collective-permute-start.16 = (bf16[384,1024]{1,0:T(8,128)(2,1)}, bf16[384,1024]{1,0:T(8,128)(2,1)}, u32[]{:S(2)}, u32[]{:S(2)}) collective-permute-start(bf16[384,1024]{1,0:T(8,128)(2,1)} %add_convert_fusion.5), channel_id=1, source_target_pairs={{0,1},{1,0},{2,3},{3,2},{4,5},{5,4},{6,7},{7,6},{8,9},{9,8},{10,11... | collective-permute-start | bytes 2359304 | tf_op jit(solution)/shard_map/ppermute | solution.py:478
  189.4 53.6 %collective-permute-start.90 = (bf16[1,2,256,1024]{3,2,1,0:T(8,128)(2,1)}, bf16[1,2,256,1024]{3,2,1,0:T(8,128)(2,1)}, u32[]{:S(2)}, u32[]{:S(2)}) collective-permute-start(bf16[1,2,256,1024]{3,2,1,0:T(8,128)(2,1)} %fusion.77), channel_id=1, source_target_pairs={{0,16},{1,17},{2,18},{3,19},{4,20},{5,21},{6,22},{7,23},{8,24},{9,... | collective-permute-start | bytes 3145736 | tf_op jit(solution)/shard_map/ppermute | solution.py:478
  212.7 33.0 %collective-permute-start.77 = (bf16[1,2,256,1024]{3,2,1,0:T(8,128)(2,1)}, bf16[1,2,256,1024]{3,2,1,0:T(8,128)(2,1)}, u32[]{:S(2)}, u32[]{:S(2)}) collective-permute-start(bf16[1,2,256,1024]{3,2,1,0:T(8,128)(2,1)} %fusion.78), channel_id=1, source_target_pairs={{0,8},{1,9},{2,10},{3,11},{4,12},{5,13},{6,14},{7,15},{8,0},{9,1},... | collective-permute-start | bytes 3145736 | tf_op jit(solution)/shard_map/ppermute | solution.py:478
  250.9 37.7 %collective-permute-start.38 = (bf16[768,1024]{1,0:T(8,128)(2,1)}, bf16[768,1024]{1,0:T(8,128)(2,1)}, u32[]{:S(2)}, u32[]{:S(2)}) collective-permute-start(bf16[768,1024]{1,0:T(8,128)(2,1)} %convolution_convert_fusion.4), channel_id=1, source_target_pairs={{0,4},{1,5},{2,6},{3,7},{4,0},{5,1},{6,2},{7,3},{8,12},{9,13},{10,... | collective-permute-start | bytes 4718600 | tf_op jit(solution)/shard_map/ppermute | solution.py:478
  268.1 78.7 %collective-permute-start.31 = (bf16[384,1024]{1,0:T(8,128)(2,1)}, bf16[384,1024]{1,0:T(8,128)(2,1)}, u32[]{:S(2)}, u32[]{:S(2)}) collective-permute-start(bf16[384,1024]{1,0:T(8,128)(2,1)} %add_convert_fusion.3), channel_id=1, source_target_pairs={{0,1},{1,0},{2,3},{3,2},{4,5},{5,4},{6,7},{7,6},{8,9},{9,8},{10,11... | collective-permute-start | bytes 2359304 | tf_op jit(solution)/shard_map/ppermute | solution.py:478
  304.2 55.1 %collective-permute-start.39 = (bf16[384,1024]{1,0:T(8,128)(2,1)}, bf16[384,1024]{1,0:T(8,128)(2,1)}, u32[]{:S(2)}, u32[]{:S(2)}) collective-permute-start(bf16[384,1024]{1,0:T(8,128)(2,1)} %add_convert_fusion.1), channel_id=1, source_target_pairs={{0,1},{1,0},{2,3},{3,2},{4,5},{5,4},{6,7},{7,6},{8,9},{9,8},{10,11... | collective-permute-start | bytes 2359304 | tf_op jit(solution)/shard_map/ppermute | solution.py:478
  308.9 36.1 %collective-permute-start.95 = (bf16[1,1,128,2,1,512]{5,2,1,4,3,0:T(8,128)(2,1)}, bf16[1,1,128,2,1,512]{5,2,1,4,3,0:T(8,128)(2,1)}, u32[]{:S(2)}, u32[]{:S(2)}) collective-permute-start(bf16[1,1,128,2,1,512]{5,2,1,4,3,0:T(8,128)(2,1)} %collective-permute-done.93), channel_id=1, source_target_pairs={{0,1},{1,0},{2,3},{3,2},{4,5},{5,4},{6,7},{7,6},{8,9},{9,8},{10,11... | collective-permute-start | bytes 786440 | tf_op jit(solution)/shard_map/ppermute | solution.py:478
  322.5 56.4 %collective-permute-start.82 = (bf16[1,1,128,2,1,512]{2,5,3,4,1,0:T(8,128)(2,1)}, bf16[1,1,128,2,1,512]{2,5,3,4,1,0:T(8,128)(2,1)}, u32[]{:S(2)}, u32[]{:S(2)}) collective-permute-start(bf16[1,1,128,2,1,512]{2,5,3,4,1,0:T(8,128)(2,1)} %collective-permute-done.80), channel_id=1, source_target_pairs={{0,1},{1,0},{2,3},{3,2},{4,5},{5,4},{6,7},{7,6},{8,9},{9,8},{10,11... | collective-permute-start | bytes 786440 | tf_op jit(solution)/shard_map/ppermute | solution.py:478
  346.7 53.3 %collective-permute-start.96 = (bf16[1,1,1,256,4,512]{5,3,2,4,1,0:T(8,128)(2,1)}, bf16[1,1,1,256,4,512]{5,3,2,4,1,0:T(8,128)(2,1)}, u32[]{:S(2)}, u32[]{:S(2)}) collective-permute-start(bf16[1,1,1,256,4,512]{5,3,2,4,1,0:T(8,128)(2,1)} %bitcast.151), channel_id=1, source_target_pairs={{0,4},{1,5},{2,6},{3,7},{4,0},{5,1},{6,2},{7,3},{8,12},{9,13},{10,... | collective-permute-start | bytes 3145736 | tf_op jit(solution)/shard_map/ppermute | solution.py:478
  346.7 53.3 %collective-permute-start.97 = (bf16[1,1,1,256,4,512]{5,3,2,4,1,0:T(8,128)(2,1)}, bf16[1,1,1,256,4,512]{5,3,2,4,1,0:T(8,128)(2,1)}, u32[]{:S(2)}, u32[]{:S(2)}) collective-permute-start(bf16[1,1,1,256,4,512]{5,3,2,4,1,0:T(8,128)(2,1)} %bitcast.151), channel_id=1, source_target_pairs={{0,16},{1,17},{2,18},{3,19},{4,20},{5,21},{6,22},{7,23},{8,24},{9,... | collective-permute-start | bytes 3145736 | tf_op jit(solution)/shard_map/ppermute | solution.py:478
  351.6 38.0 %collective-permute-start.32 = (bf16[384,1024]{1,0:T(8,128)(2,1)}, bf16[384,1024]{1,0:T(8,128)(2,1)}, u32[]{:S(2)}, u32[]{:S(2)}) collective-permute-start(bf16[384,1024]{1,0:T(8,128)(2,1)} %add_convert_fusion.2), channel_id=1, source_target_pairs={{0,0},{1,1},{2,4},{3,5},{4,2},{5,3},{6,6},{7,7},{8,8},{9,9},{10,12... | collective-permute-start | bytes 2359304 | tf_op jit(solution)/shard_map/ppermute | solution.py:488
  403.3 76.4 %collective-permute-start.99 = (bf16[1,1,1,256,4,512]{5,3,2,4,1,0:T(8,128)(2,1)}, bf16[1,1,1,256,4,512]{5,3,2,4,1,0:T(8,128)(2,1)}, u32[]{:S(2)}, u32[]{:S(2)}) collective-permute-start(bf16[1,1,1,256,4,512]{5,3,2,4,1,0:T(8,128)(2,1)} %bitcast.151), channel_id=1, source_target_pairs={{0,8},{1,9},{2,10},{3,11},{4,12},{5,13},{6,14},{7,15},{8,0},{9,1},... | collective-permute-start | bytes 3145736 | tf_op jit(solution)/shard_map/ppermute | solution.py:478
  415.9 75.6 %collective-permute-start.98 = (bf16[1,1,1,256,4,512]{5,3,2,4,1,0:T(8,128)(2,1)}, bf16[1,1,1,256,4,512]{5,3,2,4,1,0:T(8,128)(2,1)}, u32[]{:S(2)}, u32[]{:S(2)}) collective-permute-start(bf16[1,1,1,256,4,512]{5,3,2,4,1,0:T(8,128)(2,1)} %collective-permute-done.97), channel_id=1, source_target_pairs={{0,4},{1,5},{2,6},{3,7},{4,0},{5,1},{6,2},{7,3},{8,12},{9,13},{10,... | collective-permute-start | bytes 3145736 | tf_op jit(solution)/shard_map/ppermute | solution.py:478
  417.2 63.8 %collective-permute-start.85 = (bf16[1,1,1,256,4,512]{5,3,4,2,1,0:T(8,128)(2,1)}, bf16[1,1,1,256,4,512]{5,3,4,2,1,0:T(8,128)(2,1)}, u32[]{:S(2)}, u32[]{:S(2)}) collective-permute-start(bf16[1,1,1,256,4,512]{5,3,4,2,1,0:T(8,128)(2,1)} %collective-permute-done.84), channel_id=1, source_target_pairs={{0,4},{1,5},{2,6},{3,7},{4,0},{5,1},{6,2},{7,3},{8,12},{9,13},{10,... | collective-permute-start | bytes 3145736 | tf_op jit(solution)/shard_map/ppermute | solution.py:478
  422.0 66.2 %collective-permute-start.88 = (bf16[1,1,1,256,4,512]{5,3,4,2,1,0:T(8,128)(2,1)}, bf16[1,1,1,256,4,512]{5,3,4,2,1,0:T(8,128)(2,1)}, u32[]{:S(2)}, u32[]{:S(2)}) collective-permute-start(bf16[1,1,1,256,4,512]{5,3,4,2,1,0:T(8,128)(2,1)} %collective-permute-done.84), channel_id=1, source_target_pairs={{0,16},{1,17},{2,18},{3,19},{4,20},{5,21},{6,22},{7,23},{8,24},{9,... | collective-permute-start | bytes 3145736 | tf_op jit(solution)/shard_map/ppermute | solution.py:478
  423.7 61.8 %collective-permute-start.87 = (bf16[1,1,1,256,4,512]{5,3,4,2,1,0:T(8,128)(2,1)}, bf16[1,1,1,256,4,512]{5,3,4,2,1,0:T(8,128)(2,1)}, u32[]{:S(2)}, u32[]{:S(2)}) collective-permute-start(bf16[1,1,1,256,4,512]{5,3,4,2,1,0:T(8,128)(2,1)} %collective-permute-done.86), channel_id=1, source_target_pairs={{0,4},{1,5},{2,6},{3,7},{4,0},{5,1},{6,2},{7,3},{8,12},{9,13},{10,... | collective-permute-start | bytes 3145736 | tf_op jit(solution)/shard_map/ppermute | solution.py:478
  481.0 58.9 %collective-permute-start.100 = (bf16[1,1,1,256,4,512]{5,3,2,4,1,0:T(8,128)(2,1)}, bf16[1,1,1,256,4,512]{5,3,2,4,1,0:T(8,128)(2,1)}, u32[]{:S(2)}, u32[]{:S(2)}) collective-permute-start(bf16[1,1,1,256,4,512]{5,3,2,4,1,0:T(8,128)(2,1)} %collective-permute-done.99), channel_id=1, source_target_pairs={{0,4},{1,5},{2,6},{3,7},{4,0},{5,1},{6,2},{7,3},{8,12},{9,13},{10,... | collective-permute-start | bytes 3145736 | tf_op jit(solution)/shard_map/ppermute | solution.py:478
  491.4 149.5 %collective-permute-start.89 = (bf16[1,1,1,256,4,512]{5,3,4,2,1,0:T(8,128)(2,1)}, bf16[1,1,1,256,4,512]{5,3,4,2,1,0:T(8,128)(2,1)}, u32[]{:S(2)}, u32[]{:S(2)}) collective-permute-start(bf16[1,1,1,256,4,512]{5,3,4,2,1,0:T(8,128)(2,1)} %collective-permute-done.88), channel_id=1, source_target_pairs={{0,4},{1,5},{2,6},{3,7},{4,0},{5,1},{6,2},{7,3},{8,12},{9,13},{10,... | collective-permute-start | bytes 3145736 | tf_op jit(solution)/shard_map/ppermute | solution.py:478
  506.2 119.0 %collective-permute-start.102 = (bf16[1,1,1,256,4,512]{5,3,2,4,1,0:T(8,128)(2,1)}, bf16[1,1,1,256,4,512]{5,3,2,4,1,0:T(8,128)(2,1)}, u32[]{:S(2)}, u32[]{:S(2)}) collective-permute-start(bf16[1,1,1,256,4,512]{5,3,2,4,1,0:T(8,128)(2,1)} %collective-permute-done.101), channel_id=1, source_target_pairs={{0,4},{1,5},{2,6},{3,7},{4,0},{5,1},{6,2},{7,3},{8,12},{9,13},{10,... | collective-permute-start | bytes 3145736 | tf_op jit(solution)/shard_map/ppermute | solution.py:478
  543.4 46.0 %collective-permute-start.55 = (bf16[2,1,128,2,1,128]{5,3,2,0,4,1:T(2,128)(2,1)S(1)}, bf16[2,1,128,2,1,128]{5,3,2,0,4,1:T(2,128)(2,1)}, u32[]{:S(2)}, u32[]{:S(2)}) collective-permute-start(bf16[2,1,128,2,1,128]{5,3,2,0,4,1:T(2,128)(2,1)S(1)} %reshape.822), channel_id=1, source_target_pairs={{0,1},{1,0},{2,3},{3,2},{4,5},{5,4},{6,7},{7,6},{8,9},{9,8},{10,11... | collective-permute-start | bytes 393224 | tf_op jit(solution)/shard_map/ppermute | solution.py:478
  546.2 51.4 %collective-permute-start.69 = (bf16[2,1,128,2,1,128]{5,3,2,0,4,1:T(2,128)(2,1)S(1)}, bf16[2,1,128,2,1,128]{5,3,2,0,4,1:T(2,128)(2,1)}, u32[]{:S(2)}, u32[]{:S(2)}) collective-permute-start(bf16[2,1,128,2,1,128]{5,3,2,0,4,1:T(2,128)(2,1)S(1)} %collective-permute-done.67), channel_id=1, source_target_pairs={{0,1},{1,0},{2,3},{3,2},{4,5},{5,4},{6,7},{7,6},{8,9},{9,8},{10,11... | collective-permute-start | bytes 393224 | tf_op jit(solution)/shard_map/ppermute | solution.py:478
  546.8 59.4 %collective-permute-start.56 = (bf16[2,1,128,2,1,128]{5,3,2,0,4,1:T(2,128)(2,1)S(1)}, bf16[2,1,128,2,1,128]{5,3,2,0,4,1:T(2,128)(2,1)S(1)}, u32[]{:S(2)}, u32[]{:S(2)}) collective-permute-start(bf16[2,1,128,2,1,128]{5,3,2,0,4,1:T(2,128)(2,1)S(1)} %collective-permute-done.54), channel_id=1, source_target_pairs={{0,1},{1,0},{2,3},{3,2},{4,5},{5,4},{6,7},{7,6},{8,9},{9,8},{10,11... | collective-permute-start | bytes 393224 | tf_op jit(solution)/shard_map/ppermute | solution.py:478
  589.4 181.5 %collective-permute-start.43 = (bf16[768,1024]{1,0:T(8,128)(2,1)}, bf16[768,1024]{1,0:T(8,128)(2,1)}, u32[]{:S(2)}, u32[]{:S(2)}) collective-permute-start(bf16[768,1024]{1,0:T(8,128)(2,1)} %bitcast_convert_fusion), channel_id=1, source_target_pairs={{0,4},{1,5},{2,6},{3,7},{4,0},{5,1},{6,2},{7,3},{8,12},{9,13},{10,... | collective-permute-start | bytes 4718600 | tf_op jit(solution)/shard_map/ppermute | solution.py:478
  605.7 168.3 %collective-permute-start.70 = (bf16[2,1,1,256,4,128]{5,4,3,2,1,0:T(4,128)(2,1)}, bf16[2,1,1,256,4,128]{5,4,3,2,1,0:T(4,128)(2,1)}, u32[]{:S(2)}, u32[]{:S(2)}) collective-permute-start(bf16[2,1,1,256,4,128]{5,4,3,2,1,0:T(4,128)(2,1)} %bitcast.87), channel_id=1, source_target_pairs={{0,4},{1,5},{2,6},{3,7},{4,0},{5,1},{6,2},{7,3},{8,12},{9,13},{10,... | collective-permute-start | bytes 1572872 | tf_op jit(solution)/shard_map/ppermute | solution.py:478
  606.3 165.7 %collective-permute-start.71 = (bf16[2,1,1,256,4,128]{5,4,3,2,1,0:T(4,128)(2,1)}, bf16[2,1,1,256,4,128]{5,4,3,2,1,0:T(4,128)(2,1)}, u32[]{:S(2)}, u32[]{:S(2)}) collective-permute-start(bf16[2,1,1,256,4,128]{5,4,3,2,1,0:T(4,128)(2,1)} %bitcast.87), channel_id=1, source_target_pairs={{0,16},{1,17},{2,18},{3,19},{4,20},{5,21},{6,22},{7,23},{8,24},{9,... | collective-permute-start | bytes 1572872 | tf_op jit(solution)/shard_map/ppermute | solution.py:478
  625.2 152.7 %collective-permute-start.73 = (bf16[2,1,1,256,4,128]{5,4,3,2,1,0:T(4,128)(2,1)}, bf16[2,1,1,256,4,128]{5,4,3,2,1,0:T(4,128)(2,1)}, u32[]{:S(2)}, u32[]{:S(2)}) collective-permute-start(bf16[2,1,1,256,4,128]{5,4,3,2,1,0:T(4,128)(2,1)} %bitcast.87), channel_id=1, source_target_pairs={{0,8},{1,9},{2,10},{3,11},{4,12},{5,13},{6,14},{7,15},{8,0},{9,1},... | collective-permute-start | bytes 1572872 | tf_op jit(solution)/shard_map/ppermute | solution.py:478
  640.9 138.3 %collective-permute-start.57 = (bf16[2,1,1,256,4,128]{5,4,3,2,1,0:T(4,128)(2,1)}, bf16[2,1,1,256,4,128]{5,4,3,2,1,0:T(4,128)(2,1)}, u32[]{:S(2)}, u32[]{:S(2)}) collective-permute-start(bf16[2,1,1,256,4,128]{5,4,3,2,1,0:T(4,128)(2,1)} %bitcast.73), channel_id=1, source_target_pairs={{0,4},{1,5},{2,6},{3,7},{4,0},{5,1},{6,2},{7,3},{8,12},{9,13},{10,... | collective-permute-start | bytes 1572872 | tf_op jit(solution)/shard_map/ppermute | solution.py:478
  796.7 55.5 %collective-permute-start.76 = (bf16[2,1,1,256,4,128]{5,4,3,2,1,0:T(4,128)(2,1)}, bf16[2,1,1,256,4,128]{5,4,3,2,1,0:T(4,128)(2,1)}, u32[]{:S(2)}, u32[]{:S(2)}) collective-permute-start(bf16[2,1,1,256,4,128]{5,4,3,2,1,0:T(4,128)(2,1)} %collective-permute-done.75), channel_id=1, source_target_pairs={{0,4},{1,5},{2,6},{3,7},{4,0},{5,1},{6,2},{7,3},{8,12},{9,13},{10,... | collective-permute-start | bytes 1572872 | tf_op jit(solution)/shard_map/ppermute | solution.py:478
  826.1 77.0 %collective-permute-start.45 = (bf16[384,1024]{1,0:T(8,128)(2,1)}, bf16[384,1024]{1,0:T(8,128)(2,1)}, u32[]{:S(2)}, u32[]{:S(2)}) collective-permute-start(bf16[384,1024]{1,0:T(8,128)(2,1)} %add_convert_fusion), channel_id=1, source_target_pairs={{0,0},{1,1},{2,4},{3,5},{4,2},{5,3},{6,6},{7,7},{8,8},{9,9},{10,12... | collective-permute-start | bytes 2359304 | tf_op jit(solution)/shard_map/ppermute | solution.py:488
  (179 other events, 2380.2 us)

commit v2 on v1

--- a/solution.py
+++ b/solution.py
@@ -474,18 +474,43 @@
 LINE_BIT, HALF_BIT, CORE_BIT, X_BIT, Y_BIT = 1, 2, 4, 8, 16
 
 
+def send_by(values_in, target):
+    return lax.ppermute(values_in, ("dp", "tensor"), [(index, target(index)) for index in range(32)])
+
+
 def flip(values_in, mask):
-    return lax.ppermute(
-        values_in, ("dp", "tensor"), [(index, index ^ mask) for index in range(32)]
-    )
+    return send_by(values_in, lambda index: index ^ mask)
+
+
+def moves(index):
+    return ((index >> 2) ^ (index >> 1)) & 1 == 1
+
+
+def swapped(index):
+    return index ^ (CORE_BIT | HALF_BIT) if moves(index) else index
 
 
 def swap_core_half(values_in):
-    pairs = []
-    for index in range(32):
-        core, half = (index >> 2) & 1, (index >> 1) & 1
-        pairs.append((index, (index & 25) | (half << 2) | (core << 1)))
+    return send_by(values_in, swapped)
+
+
+def swap_or_near(values_in):
+    return send_by(
+        values_in, lambda index: swapped(index) if moves(index) else index ^ LINE_BIT
+    )
+
+
+def near_of_moved(values_in):
+    pairs = [(index, index ^ LINE_BIT) for index in range(32) if moves(index)]
     return lax.ppermute(values_in, ("dp", "tensor"), pairs)
+
+
+def cross_one(values_in):
+    return send_by(values_in, lambda index: index ^ (Y_BIT if index & CORE_BIT else X_BIT))
+
+
+def cross_two(values_in):
+    return send_by(values_in, lambda index: index ^ (X_BIT if index & CORE_BIT else Y_BIT))
 
 
 def pick(values_in, index, axis):
@@ -498,139 +523,382 @@
     )
 
 
-def gather_group(own):
-    near = flip(own, LINE_BIT)
-    far = flip(own, CORE_BIT)
-    both = flip(near, CORE_BIT)
-    return jnp.concatenate([own, near, far, both], axis=0)
-
-
-def reduce_group(partial_of, rows):
-    sent = partial_of(2 * rows, 4 * rows).astype(jnp.bfloat16)
-    received = flip(sent, CORE_BIT)
-    near = partial_of(rows, 2 * rows) + received[rows:].astype(jnp.float32)
-    from_near = flip(near.astype(jnp.bfloat16), LINE_BIT)
-    own = partial_of(0, rows) + received[:rows].astype(jnp.float32)
-    return own + from_near.astype(jnp.float32)
-
-
-def gather_weight(local_low, place, first, second):
-    stack_count, own_rows, width = local_low.shape
-    halves = local_low.reshape(stack_count, own_rows, 2, width // 2)
-    mine = pick(halves, place["core"], 2)
-    theirs = flip(pick(halves, 1 - place["core"], 2), CORE_BIT)
-    both_cores = ordered_pair(mine, theirs, place["core"], 1).reshape(
-        stack_count, 2 * own_rows, width // 2
-    )
-    block = ordered_pair(both_cores, flip(both_cores, HALF_BIT), place["half"], 2).reshape(
-        stack_count, 2 * own_rows, width
-    )
-    first_block = flip(block, first)
-    second_block = flip(block, second)
-    third_block = flip(first_block, second)
-    whole = jnp.zeros((stack_count, 8 * own_rows, width), local_low.dtype)
-    for part, mask in (
-        (block, 0),
-        (first_block, first),
-        (second_block, second),
-        (third_block, first ^ second),
-    ):
-        start = (place["chip"] ^ (mask // X_BIT)) * (2 * own_rows)
-        whole = lax.dynamic_update_slice_in_dim(whole, part, start, 1)
-    return whole
-
-
-def scatter_grad(partial, place, first):
-    stack_count, rows, width = partial.shape
-    parts = partial.reshape(stack_count, 2, 2, rows // 4, width)
-    at = {X_BIT: (2, place["x"]), Y_BIT: (1, place["y"])}
-    second = X_BIT + Y_BIT - first
-    axis, bit = at[first]
-    kept = pick(parts, bit, axis)
-    received = flip(pick(parts, 1 - bit, axis).astype(jnp.bfloat16), first)
-    kept = kept + received.astype(jnp.float32)
-    _, bit = at[second]
-    received = flip(pick(kept, 1 - bit, 1).astype(jnp.bfloat16), second)
-    kept = pick(kept, bit, 1) + received.astype(jnp.float32)
-    halves = kept.reshape(stack_count, 2, rows // 8, width)
-    received = flip(pick(halves, 1 - place["half"], 1).astype(jnp.bfloat16), HALF_BIT)
-    return (pick(halves, place["half"], 1) + received.astype(jnp.float32)).astype(jnp.bfloat16)
-
-
-def gather_grad(own, place, first):
-    stack_count, own_rows, width = own.shape
-    second = X_BIT + Y_BIT - first
-    own = own.reshape(stack_count, 1, own_rows, 2, 1, width // 2)
-    other_half = flip(own, HALF_BIT)
-    near = flip(own, LINE_BIT)
-    near_half = flip(other_half, LINE_BIT)
-    line = jnp.zeros((stack_count, 2, own_rows, 2, 2, width // 2), own.dtype)
-    half, line_bit = place["half"], place["line"]
-    for part, row, col in (
-        (own, half, line_bit),
-        (other_half, 1 - half, line_bit),
-        (near, half, 1 - line_bit),
-        (near_half, 1 - half, 1 - line_bit),
-    ):
-        line = lax.dynamic_update_slice(line, part, (0, row, 0, 0, col, 0))
-    line = line.reshape(stack_count, 1, 1, 2 * own_rows, 4, width // 2)
-    first_block = flip(line, first)
-    second_block = flip(line, second)
-    third_block = flip(first_block, second)
-    whole = jnp.zeros((stack_count, 2, 4, 2 * own_rows, 4, width // 2), own.dtype)
-    for part, mask in (
-        (line, 0),
-        (first_block, first),
-        (second_block, second),
-        (third_block, first ^ second),
-    ):
-        chip = place["chip"] ^ (mask // X_BIT)
-        whole = lax.dynamic_update_slice(whole, part, (0, place["core"], chip, 0, 0, 0))
-        whole = lax.dynamic_update_slice(
-            whole, flip(part, CORE_BIT), (0, 1 - place["core"], chip, 0, 0, 0)
-        )
-    return whole.reshape(stack_count, 2, 8 * own_rows, 4, width // 2)
-
-
-def sum_everywhere(values_in):
-    for mask in (CORE_BIT, LINE_BIT, HALF_BIT, X_BIT, Y_BIT):
-        values_in = values_in + flip(values_in, mask)
-    return values_in
+def together(*values_in):
+    return lax.optimization_barrier(values_in)
+
+
+def by_chip(values_in, chip):
+    width = values_in.shape[-1] // 4
+    return jnp.concatenate(
+        [
+            lax.dynamic_slice_in_dim(values_in, (chip ^ block) * width, width, values_in.ndim - 1)
+            for block in range(4)
+        ],
+        axis=-1,
+    )
+
+
+def add_far(pair):
+    return jnp.concatenate([pair, flip(pair, CORE_BIT)], axis=0)
+
+
+def weight_core(local_low, place):
+    width = local_low.shape[2] // 2
+    mine = lax.dynamic_slice_in_dim(local_low, place["core"] * width, width, 2)
+    theirs = lax.dynamic_slice_in_dim(local_low, (1 - place["core"]) * width, width, 2)
+    both = ordered_pair(mine, flip(theirs, CORE_BIT), place["core"], 1)
+    return both.reshape(local_low.shape[0], 2 * local_low.shape[1], width)
+
+
+def weight_halves(own, other, place):
+    return jnp.where(
+        place["half"] == 0,
+        jnp.concatenate([own, other], axis=2),
+        jnp.concatenate([other, own], axis=2),
+    )
+
+
+def by_rel(core, own, first, pair, axis):
+    middle = jnp.where(
+        core == 0,
+        jnp.concatenate([first, pair[0]], axis=axis),
+        jnp.concatenate([pair[0], first], axis=axis),
+    )
+    return jnp.concatenate([own, middle, pair[1]], axis=axis)
+
+
+def scatter_parts(core, partials):
+    parts = [partial.reshape(2, 2, -1, partial.shape[1]) for partial in partials]
+    kept = [jnp.where(core == 0, part[:, 0], part[0]) for part in parts]
+    sent = [jnp.where(core == 0, part[:, 1], part[1]) for part in parts]
+    return jnp.stack(kept), jnp.stack(sent)
+
+
+def add_low(left_part, right_part):
+    return (left_part.astype(jnp.float32) + right_part.astype(jnp.float32)).astype(jnp.bfloat16)
 
 
 def dot32(spec, left_mat, right_mat):
     return jnp.einsum(spec, left_mat, right_mat, preferred_element_type=jnp.float32)
 
 
-def shampoo_part(
-    whole, weights_in, left_in, right_in, left_root, right_low, place, tensor_index, dp_index
+def update_kernel(
+    info_ref, left_ref, line_ref, first_ref, pair_ref, root_ref, own_ref, sent_ref, update_acc, gram_acc
 ):
-    stack_count, _, rows, blocks, width = whole.shape
-    own_rows = weights_in.shape[1]
-    left_low = left_root.astype(jnp.bfloat16)
-    flat = whole.reshape(stack_count, 2, rows, blocks * width)
-    turned = dot32("srq,scqk->scrk", left_low, flat).astype(jnp.bfloat16)
-    update = dot32("scrk,sckj->srj", turned, right_low)
-    dp_rows = lax.dynamic_slice_in_dim(flat, dp_index * own_rows, own_rows, 2)
-    line_rows = lax.dynamic_slice_in_dim(flat, tensor_index * 2 * own_rows, 2 * own_rows, 2)
-    left_sum = dot32("scrk,scqk->srq", dp_rows, line_rows)
-    tensor_cols = pick(whole, tensor_index, 3)
-    dp_cols = pick(pick(whole, place["chip"], 3), place["core"], 1)
-    right_sum = dot32("scrk,srj->sckj", tensor_cols, dp_cols).reshape(right_in.shape)
-    grad = lax.dynamic_slice_in_dim(tensor_cols, dp_index * own_rows, own_rows, 2)
-    grad = jnp.swapaxes(grad, 1, 2).reshape(weights_in.shape).astype(jnp.float32)
+    step = pl.program_id(1)
+    steps = pl.num_programs(1)
+    chip, core, tensor = info_ref[0], info_ref[1], info_ref[2]
+    block = left_ref.shape[2] // 4
+    own_rows = block // 2
+    cols = update_acc.shape[1]
+
+    @pl.when(step == 0)
+    def _():
+        update_acc[...] = jnp.zeros_like(update_acc)
+        gram_acc[...] = jnp.zeros_like(gram_acc)
+
+    pieces = (
+        lambda: line_ref[0, 0],
+        lambda: first_ref[0, 0],
+        lambda: pair_ref[0, 0, 0],
+        lambda: pair_ref[1, 0, 0],
+    )
+    rels = (0, 1 + core, 2 - core, 3)
+    turned = None
+    for rel, piece in zip(rels, pieces):
+        start = pl.multiple_of((chip ^ rel) * block, block)
+        part = jnp.dot(
+            left_ref[0, :, pl.ds(start, block)], piece(), preferred_element_type=jnp.float32
+        )
+        turned = part if turned is None else turned + part
+
+        @pl.when((chip ^ tensor) == rel)
+        def _(piece=piece):
+            gram_acc[...] += lax.dot_general(
+                pieces[0](), piece(), (((1,), (1,)), ((), ())), preferred_element_type=jnp.float32
+            )
+
+    root = root_ref[...].reshape(-1, cols).astype(jnp.bfloat16)
+    update_acc[...] += jnp.dot(
+        turned.astype(jnp.bfloat16), root, preferred_element_type=jnp.float32
+    )
+
+    @pl.when(step == steps - 1)
+    def _():
+        own_ref[0, :, :cols] = update_acc[:own_rows]
+        sent_ref[0, :, :cols] = update_acc[own_rows:].astype(jnp.bfloat16)
+        gram_own = gram_acc[pl.ds(pl.multiple_of(core * own_rows, own_rows), own_rows), :]
+        gram_sent = gram_acc[pl.ds(pl.multiple_of((1 - core) * own_rows, own_rows), own_rows), :]
+        own_ref[0, :, cols:] = gram_own
+        sent_ref[0, :, cols:] = gram_sent.astype(jnp.bfloat16)
+
+
+def updates(info, left_low, pieces, root, split, at):
+    line, first, pair = pieces
+    _, lead, rows, width = line.shape
+    count = 1 if split else lead
+    cols = root.shape[2]
+    root_rows = root.shape[1] // 8
+    root = root.reshape(root.shape[0], 2, 2, 2, root_rows, cols)
+    if split:
+        steps = 4
+        root_spec = pl.BlockSpec(
+            (1, 1, 1, 1, root_rows, cols),
+            lambda m, k, info_ref: (at, k & 1, info_ref[3] ^ (k >> 1), info_ref[1], 0, 0),
+        )
+    else:
+        steps = 2
+        root_spec = pl.BlockSpec(
+            (1, 2, 1, 1, root_rows, cols),
+            lambda m, k, info_ref: (m, 0, info_ref[3] ^ k, info_ref[1], 0, 0),
+        )
+
+    def place_of(m, k):
+        return (k >> 1, k & 1) if split else (k, m)
+
+    out_shape = (count, rows // 2, cols + rows)
+    out_spec = pl.BlockSpec((1, rows // 2, cols + rows), lambda m, k, info_ref: (m, 0, 0))
+    piece_spec = pl.BlockSpec(
+        (1, 1, rows, width), lambda m, k, info_ref: place_of(m, k) + (0, 0)
+    )
+    return pl.pallas_call(
+        update_kernel,
+        grid_spec=pltpu.PrefetchScalarGridSpec(
+            num_scalar_prefetch=1,
+            grid=(count, steps),
+            in_specs=[
+                pl.BlockSpec((1, rows, 4 * rows), lambda m, k, info_ref: (m, 0, 0)),
+                piece_spec,
+                piece_spec,
+                pl.BlockSpec(
+                    (2, 1, 1, rows, width), lambda m, k, info_ref: (0,) + place_of(m, k) + (0, 0)
+                ),
+                root_spec,
+            ],
+            out_specs=[out_spec, out_spec],
+            scratch_shapes=[
+                pltpu.VMEM((rows, cols), jnp.float32),
+                pltpu.VMEM((rows, rows), jnp.float32),
+            ],
+        ),
+        out_shape=(
+            jax.ShapeDtypeStruct(out_shape, jnp.float32),
+            jax.ShapeDtypeStruct(out_shape, jnp.bfloat16),
+        ),
+        compiler_params=pltpu.CompilerParams(vmem_limit_bytes=48 * 1024 * 1024),
+        cost_estimate=pl.CostEstimate(flops=1_000_000, bytes_accessed=100_000, transcendentals=0),
+    )(info, left_low, line, first, pair, root)
+
+
+def column_block(pieces, line_rel, half, split, core):
+    line, first, pair = pieces
+
+    def cut(piece):
+        piece = piece[0] if line_rel is None else pick(piece, line_rel, 0)
+        if split:
+            return pick(piece, half, 0)[None]
+        width = piece.shape[2] // 2
+        return lax.dynamic_slice_in_dim(piece, half * width, width, 2)
+
+    return by_rel(core, cut(line), cut(first), (cut(pair[0]), cut(pair[1])), 1)
+
+
+def shampoo_part(info, pieces, left_low, weights_in, left_in, right_in, root, place, split, at):
+    core = place["core"]
+    own, sent = updates(info, left_low, pieces, root, split, at)
+    received = flip(sent, CORE_BIT)
+    total = own + received.astype(jnp.float32)
+    rows, cols = weights_in.shape[1:]
+    tensor_cols = column_block(pieces, None, place["half"], split, core)
+    other_cols = flip(tensor_cols, CORE_BIT)
+    chip_cols = column_block(pieces, place["line"] ^ place["x"], place["y"], split, core)
+    both = jnp.where(
+        core == 0,
+        jnp.concatenate([tensor_cols, other_cols], axis=2),
+        jnp.concatenate([other_cols, tensor_cols], axis=2),
+    )
+    right_sum = dot32("srk,srj->skj", both, chip_cols)
+    grad = lax.dynamic_slice_in_dim(both, core * rows, rows, 1).astype(jnp.float32)
     return (
         grad,
-        0.5 * left_in + 0.5 * left_sum,
+        0.5 * left_in + 0.5 * total[:, :, cols:],
         0.5 * right_in + 0.5 * right_sum,
-        weights_in - shampoo_rate * (update + shampoo_decay * weights_in),
-    )
-
-
-def right_root_low(right_root, blocks):
-    stack_count, rows, width = right_root.shape
-    low = right_root.astype(jnp.bfloat16).reshape(stack_count, blocks, 2, rows // (2 * blocks), width)
-    return jnp.swapaxes(low, 1, 2).reshape(stack_count, 2, rows // 2, width)
+        weights_in - shampoo_rate * (total[:, :, :cols] + shampoo_decay * weights_in),
+    )
+
+
+def knn_kernel(
+    info_ref, blend_ref, gaps_ref, ids_ref, targets_ref, logprob_ref, lm_ref, cot_ref, sums_ref
+):
+    step = pl.program_id(0)
+    chip = info_ref[0]
+    log_temperature = blend_ref[0:1, 0:1]
+    sharpness_divisor = jnp.exp(log_temperature)
+    interp = 1.0 / (1.0 + jnp.exp(-blend_ref[0:1, 1:2]))
+    gaps = gaps_ref[...]
+    logits = -gaps / sharpness_divisor
+    near_exp = jnp.exp(logits - jnp.max(logits, axis=1, keepdims=True))
+    mass = jnp.sum(near_exp, axis=1, keepdims=True)
+    hits = ids_ref[...] == targets_ref[...]
+    hit_exp = jnp.where(hits, near_exp, 0.0)
+    retrieval = jnp.sum(hit_exp, axis=1, keepdims=True) / mass
+    hit_gaps = jnp.sum(hit_exp * gaps, axis=1, keepdims=True) / mass
+    all_gaps = jnp.sum(near_exp * gaps, axis=1, keepdims=True) / mass
+    temp_terms = (hit_gaps - retrieval * all_gaps) / sharpness_divisor
+    lm_prob = jnp.exp(logprob_ref[...])
+    mixture = interp * retrieval + (1.0 - interp) * lm_prob
+    lm_weight = -(1.0 - interp) * lm_prob / mixture
+    temp_grad = jnp.sum(-(interp / mixture) * temp_terms, axis=0, keepdims=True)
+    interp_grad = jnp.sum(
+        -interp * (1.0 - interp) * (retrieval - lm_prob) / mixture, axis=0, keepdims=True
+    )
+    loss = jnp.sum(-jnp.log(mixture), axis=0, keepdims=True)
+    lane = lax.broadcasted_iota(jnp.int32, sums_ref.shape, 1)
+    sums = jnp.where(lane == 0, temp_grad, jnp.where(lane == 1, interp_grad, 0.0))
+    sums = jnp.where(lane == 2, loss, sums)
+
+    @pl.when(step == 0)
+    def _():
+        sums_ref[...] = jnp.zeros_like(sums_ref)
+
+    sums_ref[...] += sums
+    block = lm_ref.shape[1] // 4
+    for rel in range(4):
+        start = pl.multiple_of((chip ^ rel) * block, block)
+        part = lm_weight * lm_ref[:, pl.ds(start, block)].astype(jnp.float32)
+        cot_ref[:, rel * block : (rel + 1) * block] = part.astype(cot_ref.dtype)
+
+
+def neighbours(where, blend, gaps, ids, targets, logprob, lm_grad):
+    rows, width = gaps.shape
+    step_rows = rows // 3
+    wide = pl.BlockSpec((step_rows, width), lambda r, info_ref: (r, 0))
+    thin = pl.BlockSpec((step_rows, 1), lambda r, info_ref: (r, 0))
+    cot, sums = pl.pallas_call(
+        knn_kernel,
+        grid_spec=pltpu.PrefetchScalarGridSpec(
+            num_scalar_prefetch=1,
+            grid=(3,),
+            in_specs=[
+                pl.BlockSpec((1, 2), lambda r, info_ref: (0, 0)),
+                wide,
+                wide,
+                thin,
+                thin,
+                wide,
+            ],
+            out_specs=[wide, pl.BlockSpec((8, width), lambda r, info_ref: (0, 0))],
+        ),
+        out_shape=(
+            jax.ShapeDtypeStruct((rows, width), jnp.bfloat16),
+            jax.ShapeDtypeStruct((8, width), jnp.float32),
+        ),
+        compiler_params=pltpu.CompilerParams(vmem_limit_bytes=32 * 1024 * 1024),
+        cost_estimate=pl.CostEstimate(flops=1_000_000, bytes_accessed=100_000, transcendentals=0),
+    )(where, blend[None], gaps, ids, targets[:, None], logprob[:, None], lm_grad)
+    return cot, sums[:1]
+
+
+def normalize_kernel(info_ref, pair_ref, far_ref, params_ref, out_ref, own_ref):
+    step = pl.program_id(0)
+    chip = info_ref[0]
+    block = out_ref.shape[1] // 4
+
+    def work(rows_ref):
+        values_in = rows_ref[...].astype(jnp.float32)
+        centre = jnp.mean(values_in, axis=-1, keepdims=True)
+        spread_sq = jnp.mean((values_in - centre) ** 2, axis=-1, keepdims=True)
+        scale = lax.rsqrt(spread_sq + norm_eps)
+        for rel in range(4):
+            start = pl.multiple_of((chip ^ rel) * block, block)
+            own = slice(rel * block, (rel + 1) * block)
+            part = rows_ref[:, pl.ds(start, block)].astype(jnp.float32)
+            normed = (part - centre) * scale * params_ref[0:1, own] + params_ref[1:2, own]
+            out_ref[:, own] = normed.astype(out_ref.dtype)
+
+    @pl.when(step < 2)
+    def _():
+        work(pair_ref)
+
+    @pl.when(step >= 2)
+    def _():
+        work(far_ref)
+
+    @pl.when(step == 0)
+    def _():
+        for rel in range(4):
+            start = pl.multiple_of((chip ^ rel) * block, block)
+            own_ref[:, rel * block : (rel + 1) * block] = pair_ref[:, pl.ds(start, block)]
+
+
+def normalize(where, pair, far, params):
+    rows, width = pair.shape
+    step_rows = rows // 2
+    pair_spec = pl.BlockSpec((step_rows, width), lambda r, info_ref: (jnp.minimum(r, 1), 0))
+    far_spec = pl.BlockSpec((step_rows, width), lambda r, info_ref: (jnp.maximum(r - 2, 0), 0))
+    return pl.pallas_call(
+        normalize_kernel,
+        grid_spec=pltpu.PrefetchScalarGridSpec(
+            num_scalar_prefetch=1,
+            grid=(4,),
+            in_specs=[
+                pair_spec,
+                far_spec,
+                pl.BlockSpec(params.shape, lambda r, info_ref: (0, 0)),
+            ],
+            out_specs=[
+                pl.BlockSpec((step_rows, width), lambda r, info_ref: (r, 0)),
+                pl.BlockSpec((step_rows, width), lambda r, info_ref: (0, 0)),
+            ],
+        ),
+        out_shape=(
+            jax.ShapeDtypeStruct((2 * rows, width), pair.dtype),
+            jax.ShapeDtypeStruct((step_rows, width), pair.dtype),
+        ),
+        compiler_params=pltpu.CompilerParams(vmem_limit_bytes=32 * 1024 * 1024),
+        cost_estimate=pl.CostEstimate(flops=1_000_000, bytes_accessed=100_000, transcendentals=0),
+    )(where, pair, far, params)
+
+
+def ffn_kernel(normed_a, normed_b, cot_a, cot_b, up_ref, down_ref, act_ref, grad_ref):
+    def work(normed_ref, cot_ref):
+        pre = jnp.dot(normed_ref[...], up_ref[...], preferred_element_type=jnp.float32)
+        grad_act = jnp.dot(cot_ref[...], down_ref[...], preferred_element_type=jnp.float32)
+        scale = 0.7978845608028654
+        square = pre * pre
+        turn = jnp.tanh(pre * (scale + (scale * 0.044715) * square))
+        gate = 0.5 + 0.5 * turn
+        act_ref[...] = (pre * gate).astype(jnp.bfloat16)
+        slope = gate + 0.5 * pre * (1.0 - turn * turn) * (scale + (3.0 * scale * 0.044715) * square)
+        grad_ref[...] = (grad_act * slope).astype(jnp.bfloat16)
+
+    @pl.when(pl.program_id(1) < 2)
+    def _():
+        work(normed_a, cot_a)
+
+    @pl.when(pl.program_id(1) >= 2)
+    def _():
+        work(normed_b, cot_b)
+
+
+def ffn_middle(normed, cot, w_up, w_down):
+    rows, width = normed[0].shape
+    hidden = w_up.shape[1]
+    step_rows, step_cols = rows // 2, hidden // 2
+    pair_spec = pl.BlockSpec((step_rows, width), lambda f, r: (jnp.minimum(r, 1), 0))
+    far_spec = pl.BlockSpec((step_rows, width), lambda f, r: (jnp.maximum(r - 2, 0), 0))
+    col_spec = pl.BlockSpec((width, step_cols), lambda f, r: (0, f))
+    out_spec = pl.BlockSpec((step_rows, step_cols), lambda f, r: (r, f))
+    shape = jax.ShapeDtypeStruct((2 * rows, hidden), jnp.bfloat16)
+    return pl.pallas_call(
+        ffn_kernel,
+        grid=(2, 4),
+        in_specs=[pair_spec, far_spec, pair_spec, far_spec, col_spec, col_spec],
+        out_specs=[out_spec, out_spec],
+        out_shape=(shape, shape),
+        compiler_params=pltpu.CompilerParams(vmem_limit_bytes=48 * 1024 * 1024),
+        cost_estimate=pl.CostEstimate(flops=1_000_000, bytes_accessed=100_000, transcendentals=0),
+    )(*normed, *cot, w_up, w_down)
 
 
 def masked_heads(values_in, lanes, head, scale):
@@ -780,23 +1048,29 @@
         out_shape=jax.ShapeDtypeStruct((rows, width), jnp.bfloat16),
         compiler_params=pltpu.CompilerParams(vmem_limit_bytes=48 * 1024 * 1024),
         cost_estimate=pl.CostEstimate(
-            flops=rows * rows * width * 2, bytes_accessed=8 * rows * width, transcendentals=0
+            flops=1_000_000, bytes_accessed=100_000, transcendentals=0
         ),
     )(info, qkv)
 
 
-def attend_back(info, qkv, grad_heads):
+def attend_back(info, qkv, grad_heads, pair, earlier):
     _, rows, width = qkv.shape
+    extra = [] if earlier is None else [pl.BlockSpec(memory_space=pl.ANY)]
+
+    def kernel(info_ref, qkv_ref, grad_ref, *others):
+        backward_kernel(info_ref, qkv_ref, grad_ref, *others[len(extra) :])
+
     return pl.pallas_call(
-        backward_kernel,
+        kernel,
         grid_spec=pltpu.PrefetchScalarGridSpec(
             num_scalar_prefetch=1,
-            grid=(width // 128,),
+            grid=(1,),
             in_specs=[
-                pl.BlockSpec((3, rows, 128), lambda pair, info_ref: (0, 0, pair)),
-                pl.BlockSpec((rows, 128), lambda pair, info_ref: (0, pair)),
-            ],
-            out_specs=pl.BlockSpec((3, rows, 128), lambda pair, info_ref: (0, 0, pair)),
+                pl.BlockSpec((3, rows, 128), lambda step, info_ref: (0, 0, pair)),
+                pl.BlockSpec((rows, 128), lambda step, info_ref: (0, pair)),
+            ]
+            + extra,
+            out_specs=pl.BlockSpec((3, rows, 128), lambda step, info_ref: (0, 0, pair)),
             scratch_shapes=[
                 pltpu.VMEM((4, rows // 4, 128), jnp.float32),
                 pltpu.VMEM((4, rows // 4, 128), jnp.float32),
@@ -804,11 +1078,12 @@
             ],
         ),
         out_shape=jax.ShapeDtypeStruct(qkv.shape, jnp.bfloat16),
+        input_output_aliases={} if earlier is None else {3: 0},
         compiler_params=pltpu.CompilerParams(vmem_limit_bytes=48 * 1024 * 1024),
         cost_estimate=pl.CostEstimate(
-            flops=rows * rows * width * 5, bytes_accessed=14 * rows * width, transcendentals=0
-        ),
-    )(info, qkv, grad_heads)
+            flops=1_000_000, bytes_accessed=100_000, transcendentals=0
+        ),
+    )(info, qkv, grad_heads, *([] if earlier is None else [earlier]))
 
 
 def regrouped(
@@ -849,144 +1124,286 @@
         "chip": dp_index >> 1,
     }
     me = place["core"] * 2 + place["line"]
-
-    moved = swap_core_half(tokens_in)
-    wa, wf = attn_weights.astype(low), ffn_weights.astype(low)
-    w_first = gather_weight(wa[:2], place, X_BIT, Y_BIT)
-    w_second = gather_weight(wa[2:], place, Y_BIT, X_BIT)
-    w_up = gather_weight(wf[:1], place, X_BIT, Y_BIT)[0]
-    w_down = gather_weight(wf[1:], place, Y_BIT, X_BIT)[0]
-    proj_in = jnp.concatenate([w_first, w_second[:1]], axis=0)
-    proj_out = w_second[1]
-
-    lengths = swap_core_half(seq_lengths.astype(jnp.float32)).astype(jnp.int32)
+    chip, core = place["chip"], place["core"]
+    staying = core == place["half"]
+
+    where = jnp.stack([chip, core, tensor_index, place["line"]]).astype(jnp.int32)
+    tokens_one = swap_or_near(tokens_in)
+    wa = weight_core(attn_weights.astype(low), place)
+    wa, ffn_weights_in, nearby_entry_gaps, lengths_in = together(
+        wa, ffn_weights, nearby_entry_gaps, seq_lengths
+    )
+    wa_other = flip(wa, HALF_BIT)
+    wf = weight_core(ffn_weights_in.astype(low), place)
+    other_lengths = flip(lengths_in.astype(jnp.float32), CORE_BIT).astype(jnp.int32)
+    lengths = jnp.where(staying, seq_lengths, other_lengths)
+    params = by_chip(norm_params, chip)
     block_begins = first_blocks(lengths, group_rows, SHORT) * SHORT
     info = jnp.concatenate([me[None].astype(jnp.int32), block_begins.astype(jnp.int32)])
-
-    resid = moved.astype(jnp.float32)
-    normed1, norm1_back = jax.vjp(layer_norm, resid, norm_params[0], norm_params[1])
-    normed1_all = gather_group(normed1.astype(low))
+    cot_low, knn_sums = neighbours(
+        where,
+        blending_coefficients,
+        nearby_entry_gaps,
+        neighbor_ids,
+        targets,
+        lm_logprob,
+        lm_grad,
+    )
+    tokens_one, wf, params, info, wa_other, cot_low = together(
+        tokens_one, wf, params, info, wa_other, cot_low
+    )
+    tokens_two = near_of_moved(tokens_one)
+    wa = weight_halves(wa, wa_other, place)
+    wa_first = cross_one(wa)
+    wf_other = flip(wf, HALF_BIT)
+    tokens_one, tokens_two, wa_first, cot_low = together(tokens_one, tokens_two, wa_first, cot_low)
+    pair1 = jnp.concatenate(
+        [
+            jnp.where(staying, tokens_in, tokens_one),
+            jnp.where(staying, tokens_one, tokens_two),
+        ],
+        axis=0,
+    )
+    far1 = flip(pair1, CORE_BIT)
+    wa_pair = cross_two(jnp.stack([wa, wa_first]))
+    cot_one = swap_or_near(cot_low)
+    far1, pair1 = together(far1, pair1)
+    normed1_all, own_low = normalize(where, pair1, far1, params)
+    resid = own_low.astype(jnp.float32)
+    _, norm1_back = jax.vjp(layer_norm, resid, params[0], params[1])
+    normed1_all, wa_pair = together(normed1_all, wa_pair)
+    wa_all = by_rel(core, wa, wa_first, wa_pair, 1)
+    proj_in, proj_out = wa_all[:3], wa_all[3]
+
     qkv = dot32("rd,sdc->src", normed1_all, proj_in).astype(low)
     heads_flat = attend(info, qkv)
-    attn_out = reduce_group(
-        lambda a, b: dot32("rc,dc->rd", heads_flat[a:b], proj_out), rows
-    )
-    middle = resid + attn_out
-    normed2, norm2_back = jax.vjp(layer_norm, middle, norm_params[2], norm_params[3])
-    normed2_all = gather_group(normed2.astype(low))
-
-    sharpness_divisor = jnp.exp(blending_coefficients[0])
-    interp = jax.nn.sigmoid(blending_coefficients[1])
-    nearby_entry_logits = -nearby_entry_gaps / sharpness_divisor
-    near_top = jnp.max(nearby_entry_logits, axis=1, keepdims=True)
-    near_exp = jnp.exp(nearby_entry_logits - near_top)
-    nearby_entry_shares = near_exp / jnp.sum(near_exp, axis=1, keepdims=True)
-    target_matches = (neighbor_ids == targets[:, None]).astype(jnp.float32)
-    retrieval_probability = jnp.sum(nearby_entry_shares * target_matches, axis=1)
-    lm_prob = jnp.exp(lm_logprob)
-    mixture = interp * retrieval_probability + (1.0 - interp) * lm_prob
-    token_loss = -jnp.log(mixture)
-    lm_weight = -(1.0 - interp) * lm_prob / mixture
-    temp_terms = (
-        jnp.sum(
-            nearby_entry_shares
-            * (target_matches - retrieval_probability[:, None])
-            * nearby_entry_gaps,
-            axis=1,
-        )
-        / sharpness_divisor
-    )
-    temp_grad = jnp.sum(-(interp / mixture) * temp_terms)
-    interp_grad = jnp.sum(-interp * (1.0 - interp) * (retrieval_probability - lm_prob) / mixture)
-    cotangent = swap_core_half(lm_weight)[:, None] * swap_core_half(lm_grad).astype(jnp.float32)
-    cot_all = gather_group(cotangent.astype(low))
-
-    hidden_pre = dot32("rd,df->rf", normed2_all, w_up)
-    hidden_act, gelu_back = jax.vjp(gelu_tanh, hidden_pre)
-    act_low = hidden_act.astype(low)
-    grad_act = dot32("rd,df->rf", cot_all, w_down)
-    grad_pre_low = gelu_back(grad_act)[0].astype(low)
-    grad_normed2 = reduce_group(
-        lambda a, b: dot32("rf,df->rd", grad_pre_low[a:b], w_up), rows
-    )
-    grad_up = dot32("rd,rf->df", normed2_all, grad_pre_low)
-    grad_down = dot32("rd,rf->df", cot_all, act_low)
+    heads_flat, wf_other, wf, cot_one = together(heads_flat, wf_other, wf, cot_one)
+
+    def out_rows(a, b):
+        return dot32("rc,dc->rd", heads_flat[a:b], proj_out)
+
+    sent4 = out_rows(2 * rows, 4 * rows).astype(low)
+    sent4, wf, heads_flat = together(sent4, weight_halves(wf, wf_other, place), heads_flat)
+    received4 = flip(sent4, CORE_BIT)
+    wf_first = cross_one(wf)
+    near4 = (out_rows(rows, 2 * rows) + received4[rows:].astype(jnp.float32)).astype(low)
+    near4, cot_one, heads_flat = together(near4, cot_one, heads_flat)
+    from_near4 = flip(near4, LINE_BIT)
+    cot_two = near_of_moved(cot_one)
+    attn_out = out_rows(0, rows) + received4[:rows].astype(jnp.float32)
+    attn_out, from_near4, wf_first, cot_two = together(attn_out, from_near4, wf_first, cot_two)
+    middle = resid + attn_out + from_near4.astype(jnp.float32)
+    normed2, norm2_back = jax.vjp(layer_norm, middle, params[2], params[3])
+    normed2_low = normed2.astype(low)
+    normed2_low, cot_two = together(normed2_low, cot_two)
+    near2 = flip(normed2_low, LINE_BIT)
+    wf_pair = cross_two(jnp.stack([wf, wf_first]))
+    cot_moved = jnp.where(staying, cot_low, cot_one)
+    pair_cot = jnp.concatenate([cot_moved, jnp.where(staying, cot_one, cot_two)], axis=0)
+    far_cot = flip(pair_cot, CORE_BIT)
+    cotangent = cot_moved.astype(jnp.float32)
+    near2, far_cot, cotangent, normed2_low, wf_pair = together(
+        near2, far_cot, cotangent, normed2_low, wf_pair
+    )
+    pair2 = jnp.concatenate([normed2_low, near2], axis=0)
+    far2 = flip(pair2, CORE_BIT)
+    wf_all = by_rel(core, wf, wf_first, wf_pair, 1)
+    w_up, w_down = wf_all[0], wf_all[1]
+
+    far2, w_up, w_down = together(far2, w_up, w_down)
+    act_low, grad_pre_low = ffn_middle((pair2, far2), (pair_cot, far_cot), w_up, w_down)
+
+    def back_rows(a, b):
+        return dot32("rf,df->rd", grad_pre_low[a:b], w_up)
+
+    sent2 = back_rows(2 * rows, 4 * rows).astype(low)
+    sent2, pair2, far2, pair_cot, far_cot, act_low = together(
+        sent2, pair2, far2, pair_cot, far_cot, act_low
+    )
+    normed2_all = jnp.concatenate([pair2, far2], axis=0)
+    cot_all = jnp.concatenate([pair_cot, far_cot], axis=0)
+    received2 = flip(sent2, CORE_BIT)
+    cut = ffn_weights.shape[2] // 2
+    up_halves = [
+        dot32("rd,rf->df", normed2_all, grad_pre_low[:, :cut]),
+        dot32("rd,rf->df", normed2_all, grad_pre_low[:, cut:]),
+    ]
+    up_kept, up_sent = scatter_parts(core, [part.astype(low) for part in up_halves])
+    near2 = back_rows(rows, 2 * rows) + received2[rows:].astype(jnp.float32)
+    near2, up_kept, up_sent, act_low = together(near2.astype(low), up_kept, up_sent, act_low)
+    from_near2 = flip(near2, LINE_BIT)
+    up_got = cross_one(up_sent)
+    own2 = back_rows(0, rows) + received2[:rows].astype(jnp.float32)
+    down_halves = [
+        dot32("rd,rf->df", cot_all, act_low[:, :cut]),
+        dot32("rd,rf->df", cot_all, act_low[:, cut:]),
+    ]
+    down_kept, down_sent = scatter_parts(core, [part.astype(low) for part in down_halves])
+    down_got = cross_one(down_sent)
+    own2, from_near2, up_kept, up_got, down_kept = together(
+        own2, from_near2, up_kept, up_got, down_kept
+    )
+    grad_normed2 = own2 + from_near2.astype(jnp.float32)
     mid_norm_grad, gain2_grad, shift2_grad = norm2_back(grad_normed2)
     grad_middle = cotangent + mid_norm_grad
-    grad_mid_all = gather_group(grad_middle.astype(low))
-    grad_heads = dot32("rd,dc->rc", grad_mid_all, proj_out).astype(low)
-    grad_qkv = attend_back(info, qkv, grad_heads)
-    grad_out_proj = dot32("rd,rc->dc", grad_mid_all, heads_flat)
-    grad_proj_in = dot32("rd,src->sdc", normed1_all, grad_qkv)
-    grad_normed1 = reduce_group(
-        lambda a, b: dot32("src,sdc->rd", grad_qkv[:, a:b], proj_in), rows
-    )
-    ffn_out = reduce_group(lambda a, b: dot32("rf,df->rd", act_low[a:b], w_down), rows)
-    mixed = swap_core_half((middle + ffn_out).astype(low))
-
-    up_own = scatter_grad(grad_up[None], place, X_BIT)
-    down_own = scatter_grad(grad_down[None], place, Y_BIT)
-    first_own = scatter_grad(grad_proj_in[:2], place, X_BIT)
-    second_own = scatter_grad(
-        jnp.concatenate([grad_proj_in[2:], grad_out_proj[None]], axis=0), place, Y_BIT
-    )
-    up_whole = gather_grad(up_own, place, X_BIT)
-    down_whole = gather_grad(down_own, place, Y_BIT)
-    first_whole = gather_grad(first_own, place, X_BIT)
-    second_whole = gather_grad(second_own, place, Y_BIT)
-
+    up_kept = add_low(up_kept, up_got)
+    mid_low, up_kept, act_low = together(grad_middle.astype(low), up_kept, act_low)
+    near_mid = flip(mid_low, LINE_BIT)
+    up_got = cross_two(up_kept[:, 1])
+    ffn_sent = dot32("rf,df->rd", act_low[2 * rows :], w_down).astype(low)
+    down_got, ffn_sent, act_low = together(down_got, ffn_sent, act_low)
+    down_kept = add_low(down_kept, down_got)
+    down_got = cross_two(down_kept[:, 1])
+    ffn_received = flip(ffn_sent, CORE_BIT)
+    ffn_near = dot32("rf,df->rd", act_low[rows : 2 * rows], w_down) + ffn_received[rows:].astype(
+        jnp.float32
+    )
+    ffn_out = dot32("rf,df->rd", act_low[:rows], w_down) + ffn_received[:rows].astype(jnp.float32)
+    near_mid, up_got, ffn_near, ffn_out, mid_low = together(
+        near_mid, up_got, ffn_near.astype(low), ffn_out, mid_low
+    )
+    pair_mid = jnp.concatenate([mid_low, near_mid], axis=0)
+    far_mid = flip(pair_mid, CORE_BIT)
+    up_part = add_low(up_kept[:, 0], up_got)
+    up_other = flip(up_part, HALF_BIT)
+
+    grad_heads = jnp.concatenate(
+        [dot32("rd,dc->rc", part, proj_out).astype(low) for part in (pair_mid, far_mid)], axis=0
+    )
+    grad_heads, down_got, ffn_near = together(grad_heads, down_got, ffn_near)
+    grad_heads, down_part = together(grad_heads, add_low(down_kept[:, 0], down_got))
+    down_other = flip(down_part, HALF_BIT)
+    ffn_from_near = flip(ffn_near, LINE_BIT)
+    grad_half = attend_back(info, qkv, grad_heads, 0, None)
+    grad_half, pair_mid, far_mid = together(grad_half, pair_mid, far_mid)
+    grad_out_proj = dot32("rd,rc->dc", pair_mid, heads_flat[: 2 * rows]) + dot32(
+        "rd,rc->dc", far_mid, heads_flat[2 * rows :]
+    )
+    grad_out_proj = grad_out_proj.astype(low)
+    grad_qkv = attend_back(info, qkv, grad_heads, 1, grad_half)
+    grad_qkv, up_other, grad_out_proj = together(grad_qkv, up_other, grad_out_proj)
+    grad_qkv, up_own = together(grad_qkv, add_low(up_part, up_other))
+    up_near = flip(up_own, LINE_BIT)
+    grad_parts = [
+        dot32("rd,rc->dc", normed1_all, grad_qkv[part]).astype(low) for part in range(3)
+    ] + [grad_out_proj]
+    attn_kept, attn_sent = scatter_parts(core, grad_parts)
+    attn_kept, attn_sent, grad_qkv, up_near = together(attn_kept, attn_sent, grad_qkv, up_near)
+    attn_got = cross_one(attn_sent)
+
+    def back_in(a, b):
+        return dot32("src,sdc->rd", grad_qkv[:, a:b], proj_in)
+
+    sent1 = back_in(2 * rows, 4 * rows).astype(low)
+    attn_got, attn_kept, sent1, up_own, up_near, down_other = together(
+        attn_got, attn_kept, sent1, up_own, up_near, down_other
+    )
+
+    attn_kept = add_low(attn_kept, attn_got)
+    down_own = add_low(down_part, down_other)
+    up_line = jnp.stack([up_own, up_near])
+    attn_kept, down_own, up_line, sent1, grad_qkv = together(
+        attn_kept, down_own, up_line, sent1, grad_qkv
+    )
+    attn_got = cross_two(attn_kept[:, 1])
+    down_first = cross_one(down_own)
+    up_first = cross_one(up_line)
+    received1 = flip(sent1, CORE_BIT)
+    near3 = back_in(rows, 2 * rows)
+    attn_got, attn_kept, received1, near3, grad_qkv = together(
+        attn_got, attn_kept, received1, near3, grad_qkv
+    )
+
+    attn_part = add_low(attn_kept[:, 0], attn_got)
+    near3 = near3 + received1[rows:].astype(jnp.float32)
+    attn_part, near3, grad_qkv = together(attn_part, near3.astype(low), grad_qkv)
+    attn_other = flip(attn_part, HALF_BIT)
+    from_near3 = flip(near3, LINE_BIT)
+    own3 = back_in(0, rows) + received1[:rows].astype(jnp.float32)
+    up_first, up_line, down_first, down_own, own3, ffn_out = together(
+        up_first, up_line, down_first, down_own, own3, ffn_out
+    )
+    down_two = jnp.stack([down_own, down_first])
+    down_pair = cross_two(down_two)
+    up_pair = cross_two(jnp.stack([up_line, up_first]))
+    ffn_out = ffn_out + ffn_from_near.astype(jnp.float32)
+    mixed = by_chip((middle + ffn_out).astype(low), chip)
+    attn_other, attn_part, from_near3, mixed, own3 = together(
+        attn_other, attn_part, from_near3, mixed, own3
+    )
+
+    attn_own = add_low(attn_part, attn_other)
+    attn_own, own3, from_near3 = together(attn_own, own3, from_near3)
+    attn_near = flip(attn_own, LINE_BIT)
+    grad_normed1 = own3 + from_near3.astype(jnp.float32)
     res_norm_grad, gain1_grad, shift1_grad = norm1_back(grad_normed1)
-    input_grad = swap_core_half((grad_middle + res_norm_grad).astype(low)).astype(jnp.float32)
-
-    width = norm_params.shape[1]
-    scalars = jnp.zeros((1, width), jnp.float32)
-    scalars = scalars.at[0, 0].set(temp_grad).at[0, 1].set(interp_grad)
-    scalars = scalars.at[0, 2].set(jnp.sum(token_loss))
-    early = sum_everywhere(
-        jnp.concatenate([gain2_grad[None], shift2_grad[None], scalars], axis=0)
-    )
-    late = sum_everywhere(jnp.stack([gain1_grad, shift1_grad]))
-    norm_total = jnp.concatenate([late, early[:2]], axis=0)
-    knn_total = early[2, :2]
-    loss = early[2, 2] / (group_rows * 8)
-
-    blocks = 4
-    attn_right_low = right_root_low(attn_right_root, blocks)
-    ffn_right_low = right_root_low(ffn_right_root, blocks)
-    ffn_parts = [
-        shampoo_part(
-            whole,
+    input_grad = by_chip((grad_middle + res_norm_grad).astype(low), chip)
+    norm_grads = by_chip(jnp.stack([gain1_grad, shift1_grad, gain2_grad, shift2_grad]), chip)
+    small = jnp.concatenate([norm_grads, knn_sums], axis=0)
+
+    attn_left_low = attn_left_root.astype(low)
+    ffn_left_low = ffn_left_root.astype(low)
+    attn_left_low = jnp.concatenate([attn_left_low, flip(attn_left_low, CORE_BIT)], axis=1)
+    ffn_left_low = jnp.concatenate([ffn_left_low, flip(ffn_left_low, CORE_BIT)], axis=1)
+
+    def ffn_part(at, pieces):
+        return shampoo_part(
+            where,
+            pieces,
+            ffn_left_low[at : at + 1],
             ffn_weights[at : at + 1],
             ffn_left[at : at + 1],
             ffn_right[at : at + 1],
-            ffn_left_root[at : at + 1],
-            ffn_right_low[at : at + 1],
+            ffn_right_root,
             place,
-            tensor_index,
-            dp_index,
+            True,
+            at,
         )
-        for at, whole in enumerate((up_whole, down_whole))
-    ]
-    attn_parts = [
-        shampoo_part(
-            whole,
-            attn_weights[at : at + 2],
-            attn_left[at : at + 2],
-            attn_right[at : at + 2],
-            attn_left_root[at : at + 2],
-            attn_right_low[at : at + 2],
-            place,
-            tensor_index,
-            dp_index,
-        )
-        for at, whole in ((0, first_whole), (2, second_whole))
-    ]
-    ffn_grad, ffn_left_new, ffn_right_new, ffn_new = (
-        jnp.concatenate(parts, axis=0) for parts in zip(*ffn_parts)
-    )
-    attn_grad, attn_left_new, attn_right_new, attn_new = (
-        jnp.concatenate(parts, axis=0) for parts in zip(*attn_parts)
-    )
+
+    attn_near, attn_own, small, mixed, input_grad, up_pair, down_pair = together(
+        attn_near, attn_own, small, mixed, input_grad, up_pair, down_pair
+    )
+
+    attn_line = jnp.stack([attn_own, attn_near])
+    down_four = jnp.concatenate([down_two, down_pair], axis=0)
+    attn_line, up_pair, small, mixed, down_four = together(
+        attn_line, up_pair, small, mixed, down_four
+    )
+    attn_first = cross_one(attn_line)
+    down_far = flip(down_four, LINE_BIT)
+    mixed = swap_core_half(mixed)
+    small = small + flip(small, CORE_BIT)
+    up_new = ffn_part(0, (up_line, up_first, up_pair))
+    attn_first, attn_line, small, input_grad = together(attn_first, attn_line, small, input_grad)
+
+    attn_two = jnp.stack([attn_line, attn_first])
+    attn_two, input_grad, small, down_far = together(attn_two, input_grad, small, down_far)
+    attn_pair = cross_two(attn_two)
+    input_grad = swap_core_half(input_grad)
+    down_all = jnp.stack([down_four, down_far], axis=1)
+    down_new = ffn_part(1, (down_all[0], down_all[1], down_all[2:]))
+    ffn_new_all = tuple(jnp.concatenate(parts, axis=0) for parts in zip(up_new, down_new))
+    attn_pair, ffn_new_all, mixed, small = together(attn_pair, ffn_new_all, mixed, small)
+    ffn_grad, ffn_left_new, ffn_right_new, ffn_new = ffn_new_all
+    for mask in (X_BIT, Y_BIT, LINE_BIT, HALF_BIT):
+        small = small + flip(small, mask)
+    summed = small
+    attn_grad, attn_left_new, attn_right_new, attn_new = shampoo_part(
+        where,
+        (attn_line, attn_first, attn_pair),
+        attn_left_low,
+        attn_weights,
+        attn_left,
+        attn_right,
+        attn_right_root,
+        place,
+        False,
+        0,
+    )
+    input_grad = input_grad.astype(jnp.float32)
+    norm_total = summed[:4]
+    knn_total = summed[4, :2]
+    loss = summed[4, 2] / (group_rows * 8)
     norm_m1, norm_m2, norm_new = adamw_step(norm_params, norm_total, norm_moment1, norm_moment2)
     knn_m1, knn_m2, knn_new = adamw_step(blending_coefficients, knn_total, knn_moment1, knn_moment2)
     return (

time: 924 us -> 525 us (0.57); the launches traced: 909 us -> 520 us
  local copies, waits for them, and re-layouts: 346 us -> 36.7 us
  matrix products: 136 us -> 45.2 us
  Pallas kernels: 35.8 us -> 83.2 us
  starting transfers between devices: 125 us -> 94.5 us
    dynamic_update_slice x66 -> x0, local copies, waits for them, and re-layouts: 142 us -> none  [the longest x16 67.9 us: gather_grad(): line = lax.dynamic_update_slice(line, part, (0, row, 0, 0, col, 0))]
    dot_general x32 -> x27, matrix products: 136 us -> 45.2 us  [dot32(): jnp.einsum(spec, left_mat, right_mat, preferred_element_type=jnp.float32)]
    another operation x19 -> x2, local copies, waits for them, and re-layouts: 87.3 us -> 1.54 us  [ordered_pair(): jnp.stack([own, other], axis=axis)]
    pallas_call x1 -> x8, Pallas kernels: 24.5 us -> 71.8 us  [the longest x3 27.7 us: updates(): pl.pallas_call(update_kernel, grid_spec=pltpu.PrefetchScalarGridSpec(num_...]
    ppermute x108 -> x60, starting transfers between devices: 125 us -> 94.5 us  [the longest x58 92.6 us: send_by(): lax.ppermute(values_in, ('dp', 'tensor'), [(index, target(index)) for ind...]
    dynamic_slice x17 -> x7, local copies, waits for them, and re-layouts: 27.3 us -> 2.27 us  [pick(): return lax.dynamic_index_in_dim(values_in, index, axis, keepdims=False)]
    convert_element_type x15 -> x22, other arithmetic: 29.7 us -> 13.2 us  [the longest x9 3.53 us: add_low(): (left_part.astype(jnp.float32) + right_part.astype(jnp.float32)).astype(j...]
    select_n x0 -> x22, other arithmetic: none -> 14.5 us  [the longest x3 4.6 us: shampoo_part(): jnp.where(core == 0, jnp.concatenate([tensor_cols, other_cols], axis=2),...]
  transfers between devices with their start and end apart: 108 -> 60, of which waited for: 40 -> 28; matrix products, arithmetic and copies ran while one was open for 58% -> 20% of each run, Pallas kernels for 4% -> 13%
where the time goes in v2:
time: 525 us; the launch traced here: 520 us
  waiting for transfers between devices  195 us (37%)
  starting transfers between devices  94.5 us (18%)
  Pallas kernels  83.2 us (16%)
  other arithmetic  60.9 us (12%)
  matrix products  45.2 us (9%)
  local copies, waits for them, and re-layouts  36.7 us (7%)
    ppermute x58, waiting for transfers between devices, send_by(): lax.ppermute(values_in, ('dp', 'tensor'), [(index, target(index)) for ind...  195 us
    ppermute x58, starting transfers between devices, send_by(): lax.ppermute(values_in, ('dp', 'tensor'), [(index, target(index)) for ind...  92.6 us
    dot_general x27, matrix products, dot32(): jnp.einsum(spec, left_mat, right_mat, preferred_element_type=jnp.float32)  45.2 us
    pallas_call x3, Pallas kernels, updates(): pl.pallas_call(update_kernel, grid_spec=pltpu.PrefetchScalarGridSpec(num_...  27.7 us
    pallas_call x2, Pallas kernels, attend_back(): pl.pallas_call(kernel, grid_spec=pltpu.PrefetchScalarGridSpec(num_scalar_...  24.8 us
    unnamed x131, local copies, waits for them, and re-layouts  15.3 us
    pallas_call x1, Pallas kernels, ffn_middle(): pl.pallas_call(ffn_kernel, grid=(2, 4), in_specs=[pair_spec, far_spec, pa...  13 us
    pallas_call x1, Pallas kernels, attend(): pl.pallas_call(forward_kernel, grid_spec=pltpu.PrefetchScalarGridSpec(num...  11.3 us
  transfers between devices with their start and end apart: 60, of which 28 were waited for; matrix products, arithmetic and copies ran while one was open for 20% of the time, Pallas kernels for 13%

profile of v2, /device:TPU:0, one launch (start us, length us, event | category | flops | bytes accessed | tf_op | source)
XLA Modules:
  0.0 520.4 jit_solution(8549185544977534074)
XLA Ops:
  27.0 8.0 %collective-permute-done.4 = bf16[4,256,128]{1,2,0:T(8,128)(2,1)} collective-permute-done((bf16[4,256,128]{1,2,0:T(8,128)(2,1)}, bf16[4,256,128]{1,2,0:T(8,128)(2,1)}, u32[]{:S(2)}, u32[]{:S(2)}) %collective-permute-start.4) | collective-permute-done | bytes 262176 | tf_op jit(solution)/shard_map/ppermute | solution.py:478
  38.8 7.7 %collective-permute-done.6 = bf16[4,256,256]{1,2,0:T(8,128)(2,1)S(1)} collective-permute-done((bf16[4,256,256]{1,2,0:T(8,128)(2,1)S(1)}, bf16[4,256,256]{1,2,0:T(8,128)(2,1)S(1)}, u32[]{:S(2)}, u32[]{:S(2)}) %collective-permute-start.6) | collective-permute-done | bytes 524320 | tf_op jit(solution)/shard_map/ppermute | solution.py:478
  59.9 5.8 %collective-permute-done.8 = bf16[2,4,256,256]{2,3,1,0:T(8,128)(2,1)S(1)} collective-permute-done((bf16[2,4,256,256]{2,3,1,0:T(8,128)(2,1)S(1)}, bf16[2,4,256,256]{2,3,1,0:T(8,128)(2,1)S(1)}, u32[]{:S(2)}, u32[]{:S(2)}) %collective-permute-start.8) | collective-permute-done | bytes 1048608 | tf_op jit(solution)/shard_map/ppermute | solution.py:478
  69.0 11.3 %shard_map.352 = bf16[1536,256]{1,0:T(8,128)(2,1)S(1)} custom-call(s32[4]{0:T(128)S(1)} %pad_add_fusion.1.info_ref, bf16[3,1536,256]{2,1,0:T(8,128)(2,1)S(1)} %fusion.1.qkv_ref), custom_call_target="tpu_custom_call" | custom-call | flops 1000000 | bytes 100000 | tf_op jit(solution)/shard_map/pallas_call | solution.py:1040
  80.4 6.5 %collective-permute-done.9 = bf16[2,256,512]{2,1,0:T(8,128)(2,1)S(1)} collective-permute-done((bf16[2,256,512]{2,1,0:T(8,128)(2,1)S(1)}, bf16[2,256,512]{2,1,0:T(8,128)(2,1)S(1)}, u32[]{:S(2)}, u32[]{:S(2)}) %collective-permute-start.9) | collective-permute-done | bytes 524320 | tf_op jit(solution)/shard_map/ppermute | solution.py:478
  87.8 8.3 %collective-permute-start.11 = (bf16[768,1024]{1,0:T(8,128)(2,1)S(1)}, bf16[768,1024]{1,0:T(8,128)(2,1)S(1)}, u32[]{:S(2)}, u32[]{:S(2)}) collective-permute-start(bf16[768,1024]{1,0:T(8,128)(2,1)S(1)} %convolution_convert_fusion.3), channel_id=1, source_target_pairs={{0,4},{1,5},{2,6},{3,7},{4,0},{5,1},{6,2},{7,3},{8,12},{9,13},{10,... | collective-permute-start | bytes 4718600 | tf_op jit(solution)/shard_map/ppermute | solution.py:478
  102.3 8.7 %collective-permute-done.13 = bf16[2,256,1024]{2,1,0:T(8,128)(2,1)S(1)} collective-permute-done((bf16[2,256,1024]{2,1,0:T(8,128)(2,1)S(1)}, bf16[2,256,1024]{2,1,0:T(8,128)(2,1)S(1)}, u32[]{:S(2)}, u32[]{:S(2)}) %collective-permute-start.13) | collective-permute-done | bytes 1048608 | tf_op jit(solution)/shard_map/ppermute | solution.py:478
  110.9 9.1 %collective-permute-done.12 = bf16[384,1024]{1,0:T(8,128)(2,1)S(1)} collective-permute-done((bf16[384,1024]{1,0:T(8,128)(2,1)S(1)}, bf16[384,1024]{1,0:T(8,128)(2,1)S(1)}, u32[]{:S(2)}, u32[]{:S(2)}) %collective-permute-start.12) | collective-permute-done | bytes 786464 | tf_op jit(solution)/shard_map/ppermute | solution.py:478
  123.4 7.4 %collective-permute-start.16 = (bf16[768,1024]{1,0:T(8,128)(2,1)S(1)}, bf16[768,1024]{1,0:T(8,128)(2,1)S(1)}, u32[]{:S(2)}, u32[]{:S(2)}) collective-permute-start(bf16[768,1024]{1,0:T(8,128)(2,1)S(1)} %pad_maximum_fusion.9.cot_a), channel_id=1, source_target_pairs={{0,4},{1,5},{2,6},{3,7},{4,0},{5,1},{6,2},{7,3},{8,12},{9,13},{10,... | collective-permute-start | bytes 4718600 | tf_op jit(solution)/shard_map/ppermute | solution.py:478
  131.7 18.6 %collective-permute-done.15 = bf16[384,1024]{1,0:T(8,128)(2,1)S(1)} collective-permute-done((bf16[384,1024]{1,0:T(8,128)(2,1)S(1)}, bf16[384,1024]{1,0:T(8,128)(2,1)S(1)}, u32[]{:S(2)}, u32[]{:S(2)}) %collective-permute-start.15) | collective-permute-done | bytes 786464 | tf_op jit(solution)/shard_map/ppermute | solution.py:478
  158.3 13.0 %shard_map.353 = (bf16[1536,1024]{1,0:T(8,128)(2,1)}, bf16[1536,1024]{1,0:T(8,128)(2,1)}) custom-call(bf16[768,1024]{1,0:T(8,128)(2,1)S(1)} %constant_dynamic-update-slice_fusion.normed_a, bf16[768,1024]{1,0:T(8,128)(2,1)S(1)} %collective-permute-done.18.normed_b, bf16[768,1024]{1,0:T(8,128)(2,1)S(1)} %pad_maximum_fusion.9.cot_a, ...), custom_call_target="tpu_custom_call" | custom-call | flops 1000000 | bytes 100000 | tf_op jit(solution)/shard_map/pallas_call | solution.py:893
  171.4 3.9 convolution_convert_fusion.2
  194.4 15.2 %collective-permute-done.20 = bf16[384,1024]{1,0:T(8,128)(2,1)S(1)} collective-permute-done((bf16[384,1024]{1,0:T(8,128)(2,1)S(1)}, bf16[384,1024]{1,0:T(8,128)(2,1)S(1)}, u32[]{:S(2)}, u32[]{:S(2)}) %collective-permute-start.20) | collective-permute-done | bytes 786464 | tf_op jit(solution)/shard_map/ppermute | solution.py:478
  227.0 9.6 %collective-permute-done.22 = bf16[384,1024]{1,0:T(8,128)(2,1)S(1)} collective-permute-done((bf16[384,1024]{1,0:T(8,128)(2,1)S(1)}, bf16[384,1024]{1,0:T(8,128)(2,1)S(1)}, u32[]{:S(2)}, u32[]{:S(2)}) %collective-permute-start.22) | collective-permute-done | bytes 786464 | tf_op jit(solution)/shard_map/ppermute | solution.py:478
  238.6 5.0 collective-permute-start.28
  246.5 12.3 %shard_map.354.others_0_ = bf16[3,1536,256]{2,1,0:T(8,128)(2,1)S(1)} custom-call(s32[4]{0:T(128)S(1)} %pad_add_fusion.1.info_ref, bf16[3,1536,256]{2,1,0:T(8,128)(2,1)S(1)} %fusion.1.qkv_ref, bf16[1536,256]{1,0:T(8,128)(2,1)S(1)} %pad_maximum_fusion.24.grad_ref), custom_call_target="tpu_custom_call" | custom-call | flops 1000000 | bytes 100000 | tf_op jit(solution)/shard_map/pallas_call | solution.py:1063
  258.8 12.5 %shard_map.355 = bf16[3,1536,256]{2,1,0:T(8,128)(2,1)S(1)} custom-call(s32[4]{0:T(128)S(1)} %pad_add_fusion.1.info_ref, bf16[3,1536,256]{2,1,0:T(8,128)(2,1)S(1)} %fusion.1.qkv_ref, bf16[1536,256]{1,0:T(8,128)(2,1)S(1)} %pad_maximum_fusion.24.grad_ref, bf16[3,1536,256]{2,1,0:T(8,128)(2,1)S(1)} %shard_map.354.others_0_), custom_call_target="tpu_custom_call", output_to_operand_aliasing={{}: (3, {})} | custom-call | flops 1000000 | bytes 100000 | tf_op jit(solution)/shard_map/pallas_call | solution.py:1063
  280.2 11.7 %collective-permute-done.29 = bf16[2,256,512]{2,1,0:T(8,128)(2,1)S(1)} collective-permute-done((bf16[2,256,512]{2,1,0:T(8,128)(2,1)S(1)}, bf16[2,256,512]{2,1,0:T(8,128)(2,1)S(1)}, u32[]{:S(2)}, u32[]{:S(2)}) %collective-permute-start.29) | collective-permute-done | bytes 524320 | tf_op jit(solution)/shard_map/ppermute | solution.py:478
  292.5 4.9 collective-permute-start.31
  302.5 17.2 %collective-permute-done.31 = bf16[2,256,512]{2,1,0:T(8,128)(2,1)S(1)} collective-permute-done((bf16[2,256,512]{2,1,0:T(8,128)(2,1)S(1)}, bf16[2,256,512]{2,1,0:T(8,128)(2,1)S(1)}, u32[]{:S(2)}, u32[]{:S(2)}) %collective-permute-start.31) | collective-permute-done | bytes 524320 | tf_op jit(solution)/shard_map/ppermute | solution.py:478
  330.3 6.7 %collective-permute-done.32 = bf16[4,256,256]{2,1,0:T(8,128)(2,1)S(1)} collective-permute-done((bf16[4,256,256]{2,1,0:T(8,128)(2,1)S(1)}, bf16[4,256,256]{2,1,0:T(8,128)(2,1)S(1)}, u32[]{:S(2)}, u32[]{:S(2)}) %collective-permute-start.32) | collective-permute-done | bytes 524320 | tf_op jit(solution)/shard_map/ppermute | solution.py:478
  343.8 6.2 %collective-permute-done.37 = bf16[2,256,512]{2,1,0:T(8,128)(2,1)S(1)} collective-permute-done((bf16[2,256,512]{2,1,0:T(8,128)(2,1)S(1)}, bf16[2,256,512]{2,1,0:T(8,128)(2,1)S(1)}, u32[]{:S(2)}, u32[]{:S(2)}) %collective-permute-start.37) | collective-permute-done | bytes 524320 | tf_op jit(solution)/shard_map/ppermute | solution.py:478
  357.0 6.0 %collective-permute-done.34 = bf16[4,256,256]{2,1,0:T(8,128)(2,1)S(1)} collective-permute-done((bf16[4,256,256]{2,1,0:T(8,128)(2,1)S(1)}, bf16[4,256,256]{2,1,0:T(8,128)(2,1)S(1)}, u32[]{:S(2)}, u32[]{:S(2)}) %collective-permute-start.34) | collective-permute-done | bytes 524320 | tf_op jit(solution)/shard_map/ppermute | solution.py:478
  363.0 12.1 %collective-permute-done.35 = bf16[384,1024]{1,0:T(8,128)(2,1)S(1)} collective-permute-done((bf16[384,1024]{1,0:T(8,128)(2,1)S(1)}, bf16[384,1024]{1,0:T(8,128)(2,1)S(1)}, u32[]{:S(2)}, u32[]{:S(2)}) %collective-permute-start.35) | collective-permute-done | bytes 786464 | tf_op jit(solution)/shard_map/ppermute | solution.py:478
  379.8 7.8 %collective-permute-done.41 = bf16[2,2,256,512]{3,2,1,0:T(8,128)(2,1)S(1)} collective-permute-done((bf16[2,2,256,512]{3,2,1,0:T(8,128)(2,1)S(1)}, bf16[2,2,256,512]{3,2,1,0:T(8,128)(2,1)S(1)}, u32[]{:S(2)}, u32[]{:S(2)}) %collective-permute-start.41) | collective-permute-done | bytes 1048608 | tf_op jit(solution)/shard_map/ppermute | solution.py:478
  395.5 8.6 %shard_map.356 = (f32[1,128,1280]{2,1,0:T(8,128)S(1)}, bf16[1,128,1280]{2,1,0:T(8,128)(2,1)S(1)}) custom-call(s32[4]{0:T(128)S(1)} %copy-done.8, bf16[1,256,1024]{2,1,0:T(8,128)(2,1)S(1)} %get-tuple-element.381.left_ref, bf16[2,2,256,512]{3,2,1,0:T(8,128)(2,1)S(1)} %pad_maximum_fusion.17.line_ref, ...), custom_call_target="tpu_custom_call" | custom-call | flops 1000000 | bytes 100000 | tf_op jit(solution)/shard_map/pallas_call | solution.py:664
  408.4 7.6 %collective-permute-start.51 = (bf16[384,1024]{1,0:T(8,128)(2,1)}, bf16[384,1024]{1,0:T(8,128)(2,1)}, u32[]{:S(2)}, u32[]{:S(2)}) collective-permute-start(bf16[384,1024]{1,0:T(8,128)(2,1)} %pad_maximum_fusion.25), channel_id=1, source_target_pairs={{0,0},{1,1},{2,4},{3,5},{4,2},{5,3},{6,6},{7,7},{8,8},{9,9},{10,12... | collective-permute-start | bytes 2359304 | tf_op jit(solution)/shard_map/ppermute | solution.py:478
  427.3 16.6 %collective-permute-done.44 = bf16[4,2,256,512]{3,2,1,0:T(8,128)(2,1)} collective-permute-done((bf16[4,2,256,512]{3,2,1,0:T(8,128)(2,1)S(1)}, bf16[4,2,256,512]{3,2,1,0:T(8,128)(2,1)}, u32[]{:S(2)}, u32[]{:S(2)}) %collective-permute-start.44) | collective-permute-done | bytes 2097184 | tf_op jit(solution)/shard_map/ppermute | solution.py:478
  449.9 8.6 %shard_map.357 = (f32[1,128,1280]{2,1,0:T(8,128)S(1)}, bf16[1,128,1280]{2,1,0:T(8,128)(2,1)S(1)}) custom-call(s32[4]{0:T(128)S(1)} %copy-done.8, bf16[1,256,1024]{2,1,0:T(8,128)(2,1)S(1)} %get-tuple-element.382.left_ref, bf16[2,2,256,512]{3,2,1,0:T(8,128)(2,1)S(1)} %bitcast.327, bf16[2,2,256,512]{3,2,1,0:T(8,128)(2,1)S(1)} %bitcast.326, ...), custom_call_target="tpu_custom_call" | custom-call | flops 1000000 | bytes 100000 | tf_op jit(solution)/shard_map/pallas_call | solution.py:664
  461.4 4.5 fusion.26
  479.6 6.3 %collective-permute-start.57 = (bf16[4,1024,128]{2,1,0:T(8,128)(2,1)S(1)}, bf16[4,1024,128]{2,1,0:T(8,128)(2,1)S(1)}, u32[]{:S(2)}, u32[]{:S(2)}) collective-permute-start(bf16[4,1024,128]{2,1,0:T(8,128)(2,1)S(1)} %pad_maximum_fusion.23), channel_id=1, source_target_pairs={{0,4},{1,5},{2,6},{3,7},{4,0},{5,1},{6,2},{7,3},{8,12},{9,13},{10,... | collective-permute-start | bytes 3145736 | tf_op jit(solution)/shard_map/ppermute | solution.py:478
  485.9 10.6 %shard_map.358 = (f32[4,128,512]{2,1,0:T(8,128)S(1)}, bf16[4,128,512]{2,1,0:T(8,128)(2,1)S(1)}) custom-call(s32[4]{0:T(128)S(1)} %copy-done.8, bf16[4,256,1024]{2,1,0:T(8,128)(2,1)S(1)} %pad_maximum_fusion.6.left_ref, bf16[2,4,256,256]{3,2,1,0:T(8,128)(2,1)S(1)} %pad_maximum_fusion.19.line_ref, ...), custom_call_target="tpu_custom_call" | custom-call | flops 1000000 | bytes 100000 | tf_op jit(solution)/shard_map/pallas_call | solution.py:664
  (437 shorter events, 217.8 us)
Async XLA Ops:
  0.7 34.3 %collective-permute-start = (bf16[384,1024]{1,0:T(8,128)(2,1)}, bf16[384,1024]{1,0:T(8,128)(2,1)}, u32[]{:S(2)}, u32[]{:S(2)}) collective-permute-start(bf16[384,1024]{1,0:T(8,128)(2,1)} %param.23), channel_id=1, source_target_pairs={{0,1},{1,0},{2,4},{3,5},{4,2},{5,3},{6,7},{7,6},{8,9},{9,8},{10,12... | collective-permute-start | bytes 2359304 | tf_op jit(solution)/shard_map/ppermute | solution.py:478
  52.4 34.5 %collective-permute-start.9 = (bf16[2,256,512]{2,1,0:T(8,128)(2,1)S(1)}, bf16[2,256,512]{2,1,0:T(8,128)(2,1)S(1)}, u32[]{:S(2)}, u32[]{:S(2)}) collective-permute-start(bf16[2,256,512]{2,1,0:T(8,128)(2,1)S(1)} %bitcast.343), channel_id=1, source_target_pairs={{0,2},{1,3},{2,0},{3,1},{4,6},{5,7},{6,4},{7,5},{8,10},{9,11},{10,... | collective-permute-start | bytes 1572872 | tf_op jit(solution)/shard_map/ppermute | solution.py:478
  55.0 31.9 %collective-permute-start.10 = (bf16[384,1024]{1,0:T(8,128)(2,1)S(1)}, bf16[384,1024]{1,0:T(8,128)(2,1)S(1)}, u32[]{:S(2)}, u32[]{:S(2)}) collective-permute-start(bf16[384,1024]{1,0:T(8,128)(2,1)S(1)} %copy-done.6), channel_id=1, source_target_pairs={{0,1},{1,0},{2,4},{3,5},{4,2},{5,3},{6,7},{7,6},{8,9},{9,8},{10,12... | collective-permute-start | bytes 2359304 | tf_op jit(solution)/shard_map/ppermute | solution.py:478
  99.5 20.4 %collective-permute-start.12 = (bf16[384,1024]{1,0:T(8,128)(2,1)S(1)}, bf16[384,1024]{1,0:T(8,128)(2,1)S(1)}, u32[]{:S(2)}, u32[]{:S(2)}) collective-permute-start(bf16[384,1024]{1,0:T(8,128)(2,1)S(1)} %add_convert_fusion.9), channel_id=1, source_target_pairs={{0,1},{1,0},{2,3},{3,2},{4,5},{5,4},{6,7},{7,6},{8,9},{9,8},{10,11... | collective-permute-start | bytes 2359304 | tf_op jit(solution)/shard_map/ppermute | solution.py:478
  100.6 19.4 %collective-permute-start.14 = (bf16[384,1024]{1,0:T(8,128)(2,1)S(1)}, bf16[384,1024]{1,0:T(8,128)(2,1)S(1)}, u32[]{:S(2)}, u32[]{:S(2)}) collective-permute-start(bf16[384,1024]{1,0:T(8,128)(2,1)S(1)} %collective-permute-done.10), channel_id=1, source_target_pairs={{2,3},{3,2},{4,5},{5,4},{10,11},{11,10},{12,13},{13,12},{18,19},{1... | collective-permute-start | bytes 2359304 | tf_op jit(solution)/shard_map/ppermute | solution.py:505
  121.2 29.1 %collective-permute-start.17 = (bf16[2,2,256,1024]{3,2,1,0:T(8,128)(2,1)S(1)}, bf16[2,2,256,1024]{3,2,1,0:T(8,128)(2,1)S(1)}, u32[]{:S(2)}, u32[]{:S(2)}) collective-permute-start(bf16[2,2,256,1024]{3,2,1,0:T(8,128)(2,1)S(1)} %pad_maximum_fusion.2), channel_id=1, source_target_pairs={{0,16},{1,17},{2,18},{3,19},{4,12},{5,13},{6,14},{7,15},{8,24},{9,... | collective-permute-start | bytes 6291464 | tf_op jit(solution)/shard_map/ppermute | solution.py:478
  123.4 26.9 %collective-permute-start.16 = (bf16[768,1024]{1,0:T(8,128)(2,1)S(1)}, bf16[768,1024]{1,0:T(8,128)(2,1)S(1)}, u32[]{:S(2)}, u32[]{:S(2)}) collective-permute-start(bf16[768,1024]{1,0:T(8,128)(2,1)S(1)} %pad_maximum_fusion.9.cot_a), channel_id=1, source_target_pairs={{0,4},{1,5},{2,6},{3,7},{4,0},{5,1},{6,2},{7,3},{8,12},{9,13},{10,... | collective-permute-start | bytes 4718600 | tf_op jit(solution)/shard_map/ppermute | solution.py:478
  130.8 19.5 %collective-permute-start.15 = (bf16[384,1024]{1,0:T(8,128)(2,1)S(1)}, bf16[384,1024]{1,0:T(8,128)(2,1)S(1)}, u32[]{:S(2)}, u32[]{:S(2)}) collective-permute-start(bf16[384,1024]{1,0:T(8,128)(2,1)S(1)} %add_convert_fusion.8), channel_id=1, source_target_pairs={{0,1},{1,0},{2,3},{3,2},{4,5},{5,4},{6,7},{7,6},{8,9},{9,8},{10,11... | collective-permute-start | bytes 2359304 | tf_op jit(solution)/shard_map/ppermute | solution.py:478
  189.6 20.0 %collective-permute-start.20 = (bf16[384,1024]{1,0:T(8,128)(2,1)S(1)}, bf16[384,1024]{1,0:T(8,128)(2,1)S(1)}, u32[]{:S(2)}, u32[]{:S(2)}) collective-permute-start(bf16[384,1024]{1,0:T(8,128)(2,1)S(1)} %add_convert_fusion.7), channel_id=1, source_target_pairs={{0,1},{1,0},{2,3},{3,2},{4,5},{5,4},{6,7},{7,6},{8,9},{9,8},{10,11... | collective-permute-start | bytes 2359304 | tf_op jit(solution)/shard_map/ppermute | solution.py:478
  190.5 19.0 %collective-permute-start.21 = (bf16[2,2,256,512]{3,2,0,1:T(8,128)(2,1)S(1)}, bf16[2,2,256,512]{3,2,0,1:T(8,128)(2,1)S(1)}, u32[]{:S(2)}, u32[]{:S(2)}) collective-permute-start(bf16[2,2,256,512]{3,2,0,1:T(8,128)(2,1)S(1)} %pad_maximum_fusion.12), channel_id=1, source_target_pairs={{0,8},{1,9},{2,10},{3,11},{4,20},{5,21},{6,22},{7,23},{8,0},{9,1},... | collective-permute-start | bytes 3145736 | tf_op jit(solution)/shard_map/ppermute | solution.py:478
  191.7 24.9 %collective-permute-start.24 = (bf16[2,2,256,512]{3,2,0,1:T(8,128)(2,1)S(1)}, bf16[2,2,256,512]{3,2,0,1:T(8,128)(2,1)S(1)}, u32[]{:S(2)}, u32[]{:S(2)}) collective-permute-start(bf16[2,2,256,512]{3,2,0,1:T(8,128)(2,1)S(1)} %pad_maximum_fusion.14), channel_id=1, source_target_pairs={{0,8},{1,9},{2,10},{3,11},{4,20},{5,21},{6,22},{7,23},{8,0},{9,1},... | collective-permute-start | bytes 3145736 | tf_op jit(solution)/shard_map/ppermute | solution.py:478
  216.6 20.0 %collective-permute-start.22 = (bf16[384,1024]{1,0:T(8,128)(2,1)S(1)}, bf16[384,1024]{1,0:T(8,128)(2,1)S(1)}, u32[]{:S(2)}, u32[]{:S(2)}) collective-permute-start(bf16[384,1024]{1,0:T(8,128)(2,1)S(1)} %fusion.138), channel_id=1, source_target_pairs={{0,1},{1,0},{2,3},{3,2},{4,5},{5,4},{6,7},{7,6},{8,9},{9,8},{10,11... | collective-permute-start | bytes 2359304 | tf_op jit(solution)/shard_map/ppermute | solution.py:478
  238.6 36.3 %collective-permute-start.28 = (bf16[2,256,512]{2,1,0:T(8,128)(2,1)S(1)}, bf16[2,256,512]{2,1,0:T(8,128)(2,1)S(1)}, u32[]{:S(2)}, u32[]{:S(2)}) collective-permute-start(bf16[2,256,512]{2,1,0:T(8,128)(2,1)S(1)} %fusion.76), channel_id=1, source_target_pairs={{0,2},{1,3},{2,0},{3,1},{4,6},{5,7},{6,4},{7,5},{8,10},{9,11},{10,... | collective-permute-start | bytes 1572872 | tf_op jit(solution)/shard_map/ppermute | solution.py:478
  291.9 27.8 %collective-permute-start.30 = (bf16[4,2,256,256]{3,2,0,1:T(8,128)(2,1)S(1)}, bf16[4,2,256,256]{3,2,0,1:T(8,128)(2,1)S(1)}, u32[]{:S(2)}, u32[]{:S(2)}) collective-permute-start(bf16[4,2,256,256]{3,2,0,1:T(8,128)(2,1)S(1)} %pad_maximum_fusion.16), channel_id=1, source_target_pairs={{0,8},{1,9},{2,10},{3,11},{4,20},{5,21},{6,22},{7,23},{8,0},{9,1},... | collective-permute-start | bytes 3145736 | tf_op jit(solution)/shard_map/ppermute | solution.py:478
  292.5 27.2 %collective-permute-start.31 = (bf16[2,256,512]{2,1,0:T(8,128)(2,1)S(1)}, bf16[2,256,512]{2,1,0:T(8,128)(2,1)S(1)}, u32[]{:S(2)}, u32[]{:S(2)}) collective-permute-start(bf16[2,256,512]{2,1,0:T(8,128)(2,1)S(1)} %fusion.77), channel_id=1, source_target_pairs={{0,2},{1,3},{2,0},{3,1},{4,6},{5,7},{6,4},{7,5},{8,10},{9,11},{10,... | collective-permute-start | bytes 1572872 | tf_op jit(solution)/shard_map/ppermute | solution.py:478
  298.3 24.7 %collective-permute-start.48 = (bf16[2,128,1024]{2,1,0:T(8,128)(2,1)}, bf16[2,128,1024]{2,1,0:T(8,128)(2,1)}, u32[]{:S(2)}, u32[]{:S(2)}) collective-permute-start(bf16[2,128,1024]{2,1,0:T(8,128)(2,1)} %convert_element_type.310), channel_id=1, source_target_pairs={{0,4},{1,5},{2,6},{3,7},{4,0},{5,1},{6,2},{7,3},{8,12},{9,13},{10,... | collective-permute-start | bytes 1572872 | tf_op jit(solution)/shard_map/ppermute | solution.py:478
  299.4 25.7 %collective-permute-start.58 = (bf16[4,128,1024]{2,1,0:T(8,128)(2,1)}, bf16[4,128,1024]{2,1,0:T(8,128)(2,1)}, u32[]{:S(2)}, u32[]{:S(2)}) collective-permute-start(bf16[4,128,1024]{2,1,0:T(8,128)(2,1)} %convert_element_type.315), channel_id=1, source_target_pairs={{0,4},{1,5},{2,6},{3,7},{4,0},{5,1},{6,2},{7,3},{8,12},{9,13},{10,... | collective-permute-start | bytes 3145736 | tf_op jit(solution)/shard_map/ppermute | solution.py:478
  327.4 28.1 %collective-permute-start.38 = (bf16[384,1024]{1,0:T(8,128)(2,1)S(1)}, bf16[384,1024]{1,0:T(8,128)(2,1)S(1)}, u32[]{:S(2)}, u32[]{:S(2)}) collective-permute-start(bf16[384,1024]{1,0:T(8,128)(2,1)S(1)} %copy-done.61), channel_id=1, source_target_pairs={{0,1},{1,0},{2,3},{3,2},{4,5},{5,4},{6,7},{7,6},{8,9},{9,8},{10,11... | collective-permute-start | bytes 2359304 | tf_op jit(solution)/shard_map/ppermute | solution.py:478
  327.4 22.5 %collective-permute-start.36 = (bf16[2,2,256,512]{3,2,1,0:T(8,128)(2,1)S(1)}, bf16[2,2,256,512]{3,2,1,0:T(8,128)(2,1)S(1)}, u32[]{:S(2)}, u32[]{:S(2)}) collective-permute-start(bf16[2,2,256,512]{3,2,1,0:T(8,128)(2,1)S(1)} %pad_maximum_fusion.17.line_ref), channel_id=1, source_target_pairs={{0,8},{1,9},{2,10},{3,11},{4,20},{5,21},{6,22},{7,23},{8,0},{9,1},... | collective-permute-start | bytes 3145736 | tf_op jit(solution)/shard_map/ppermute | solution.py:478
  328.0 22.0 %collective-permute-start.37 = (bf16[2,256,512]{2,1,0:T(8,128)(2,1)S(1)}, bf16[2,256,512]{2,1,0:T(8,128)(2,1)S(1)}, u32[]{:S(2)}, u32[]{:S(2)}) collective-permute-start(bf16[2,256,512]{2,1,0:T(8,128)(2,1)S(1)} %copy-done.23), channel_id=1, source_target_pairs={{0,8},{1,9},{2,10},{3,11},{4,20},{5,21},{6,22},{7,23},{8,0},{9,1},... | collective-permute-start | bytes 1572872 | tf_op jit(solution)/shard_map/ppermute | solution.py:478
  338.6 24.4 %collective-permute-start.34 = (bf16[4,256,256]{2,1,0:T(8,128)(2,1)S(1)}, bf16[4,256,256]{2,1,0:T(8,128)(2,1)S(1)}, u32[]{:S(2)}, u32[]{:S(2)}) collective-permute-start(bf16[4,256,256]{2,1,0:T(8,128)(2,1)S(1)} %fusion.75), channel_id=1, source_target_pairs={{0,2},{1,3},{2,0},{3,1},{4,6},{5,7},{6,4},{7,5},{8,10},{9,11},{10,... | collective-permute-start | bytes 1572872 | tf_op jit(solution)/shard_map/ppermute | solution.py:478
  338.7 36.4 %collective-permute-start.35 = (bf16[384,1024]{1,0:T(8,128)(2,1)S(1)}, bf16[384,1024]{1,0:T(8,128)(2,1)S(1)}, u32[]{:S(2)}, u32[]{:S(2)}) collective-permute-start(bf16[384,1024]{1,0:T(8,128)(2,1)S(1)} %add_convert_fusion.5), channel_id=1, source_target_pairs={{0,1},{1,0},{2,3},{3,2},{4,5},{5,4},{6,7},{7,6},{8,9},{9,8},{10,11... | collective-permute-start | bytes 2359304 | tf_op jit(solution)/shard_map/ppermute | solution.py:478
  350.3 38.1 %collective-permute-start.40 = (bf16[2,2,2,256,512]{4,3,2,1,0:T(8,128)(2,1)S(1)}, bf16[2,2,2,256,512]{4,3,2,1,0:T(8,128)(2,1)S(1)}, u32[]{:S(2)}, u32[]{:S(2)}) collective-permute-start(bf16[2,2,2,256,512]{4,3,2,1,0:T(8,128)(2,1)S(1)} %pad_maximum_fusion.3), channel_id=1, source_target_pairs={{0,16},{1,17},{2,18},{3,19},{4,12},{5,13},{6,14},{7,15},{8,24},{9,... | collective-permute-start | bytes 6291464 | tf_op jit(solution)/shard_map/ppermute | solution.py:478
  351.2 36.5 %collective-permute-start.41 = (bf16[2,2,256,512]{3,2,1,0:T(8,128)(2,1)S(1)}, bf16[2,2,256,512]{3,2,1,0:T(8,128)(2,1)S(1)}, u32[]{:S(2)}, u32[]{:S(2)}) collective-permute-start(bf16[2,2,256,512]{3,2,1,0:T(8,128)(2,1)S(1)} %pad_maximum_fusion.18), channel_id=1, source_target_pairs={{0,16},{1,17},{2,18},{3,19},{4,12},{5,13},{6,14},{7,15},{8,24},{9,... | collective-permute-start | bytes 3145736 | tf_op jit(solution)/shard_map/ppermute | solution.py:478
  388.7 55.2 %collective-permute-start.44 = (bf16[4,2,256,512]{3,2,1,0:T(8,128)(2,1)S(1)}, bf16[4,2,256,512]{3,2,1,0:T(8,128)(2,1)}, u32[]{:S(2)}, u32[]{:S(2)}) collective-permute-start(bf16[4,2,256,512]{3,2,1,0:T(8,128)(2,1)S(1)} %pad_maximum_fusion.4), channel_id=1, source_target_pairs={{0,1},{1,0},{2,3},{3,2},{4,5},{5,4},{6,7},{7,6},{8,9},{9,8},{10,11... | collective-permute-start | bytes 6291464 | tf_op jit(solution)/shard_map/ppermute | solution.py:478
  390.7 25.3 %collective-permute-start.42 = (bf16[2,4,256,256]{3,2,1,0:T(8,128)(2,1)S(1)}, bf16[2,4,256,256]{3,2,1,0:T(8,128)(2,1)S(1)}, u32[]{:S(2)}, u32[]{:S(2)}) collective-permute-start(bf16[2,4,256,256]{3,2,1,0:T(8,128)(2,1)S(1)} %pad_maximum_fusion.19.line_ref), channel_id=1, source_target_pairs={{0,8},{1,9},{2,10},{3,11},{4,20},{5,21},{6,22},{7,23},{8,0},{9,1},... | collective-permute-start | bytes 3145736 | tf_op jit(solution)/shard_map/ppermute | solution.py:478
  394.3 23.0 %collective-permute-start.47 = (bf16[1,1024,512]{2,1,0:T(8,128)(2,1)}, bf16[1,1024,512]{2,1,0:T(8,128)(2,1)}, u32[]{:S(2)}, u32[]{:S(2)}) collective-permute-start(bf16[1,1024,512]{2,1,0:T(8,128)(2,1)} %get-tuple-element.380), channel_id=1, source_target_pairs={{0,4},{1,5},{2,6},{3,7},{4,0},{5,1},{6,2},{7,3},{8,12},{9,13},{10,... | collective-permute-start | bytes 3145736 | tf_op jit(solution)/shard_map/ppermute | solution.py:478
  408.4 63.9 %collective-permute-start.51 = (bf16[384,1024]{1,0:T(8,128)(2,1)}, bf16[384,1024]{1,0:T(8,128)(2,1)}, u32[]{:S(2)}, u32[]{:S(2)}) collective-permute-start(bf16[384,1024]{1,0:T(8,128)(2,1)} %pad_maximum_fusion.25), channel_id=1, source_target_pairs={{0,0},{1,1},{2,4},{3,5},{4,2},{5,3},{6,6},{7,7},{8,8},{9,9},{10,12... | collective-permute-start | bytes 2359304 | tf_op jit(solution)/shard_map/ppermute | solution.py:478
  448.4 26.2 %collective-permute-start.45 = (bf16[2,2,4,256,256]{4,3,2,1,0:T(8,128)(2,1)}, bf16[2,2,4,256,256]{4,3,2,1,0:T(8,128)(2,1)S(1)}, u32[]{:S(2)}, u32[]{:S(2)}) collective-permute-start(bf16[2,2,4,256,256]{4,3,2,1,0:T(8,128)(2,1)} %pad_maximum_fusion.5), channel_id=1, source_target_pairs={{0,16},{1,17},{2,18},{3,19},{4,12},{5,13},{6,14},{7,15},{8,24},{9,... | collective-permute-start | bytes 6291464 | tf_op jit(solution)/shard_map/ppermute | solution.py:478
  476.0 20.7 %collective-permute-start.53 = (f32[5,1024]{1,0:T(8,128)S(1)}, f32[5,1024]{1,0:T(8,128)S(1)}, u32[]{:S(2)}, u32[]{:S(2)}) collective-permute-start(f32[5,1024]{1,0:T(8,128)S(1)} %add.376), channel_id=1, source_target_pairs={{0,8},{1,9},{2,10},{3,11},{4,12},{5,13},{6,14},{7,15},{8,0},{9,1},... | collective-permute-start | bytes 61448 | tf_op jit(solution)/shard_map/ppermute | solution.py:478
  479.6 34.1 %collective-permute-start.57 = (bf16[4,1024,128]{2,1,0:T(8,128)(2,1)S(1)}, bf16[4,1024,128]{2,1,0:T(8,128)(2,1)S(1)}, u32[]{:S(2)}, u32[]{:S(2)}) collective-permute-start(bf16[4,1024,128]{2,1,0:T(8,128)(2,1)S(1)} %pad_maximum_fusion.23), channel_id=1, source_target_pairs={{0,4},{1,5},{2,6},{3,7},{4,0},{5,1},{6,2},{7,3},{8,12},{9,13},{10,... | collective-permute-start | bytes 3145736 | tf_op jit(solution)/shard_map/ppermute | solution.py:478
  496.6 15.8 %collective-permute-start.59 = (bf16[4,128,512]{2,1,0:T(8,128)(2,1)S(1)}, bf16[4,128,512]{2,1,0:T(8,128)(2,1)S(1)}, u32[]{:S(2)}, u32[]{:S(2)}) collective-permute-start(bf16[4,128,512]{2,1,0:T(8,128)(2,1)S(1)} %get-tuple-element.326), channel_id=1, source_target_pairs={{0,4},{1,5},{2,6},{3,7},{4,0},{5,1},{6,2},{7,3},{8,12},{9,13},{10,... | collective-permute-start | bytes 1572872 | tf_op jit(solution)/shard_map/ppermute | solution.py:478
  (91 other events, 875.1 us)
